TPU v7x, 256 devices: a whole 4x4x8 slice. The times are simulated.
256 devices in a mesh: dp: 8 (over z_lo, x), tok: 32 (over z_hi, y, core).
Axes of the slice: x: 4, y: 4, z: 8 (z_hi: 4, z_lo: 2; z = z_hi * 2 + z_lo), core: 2. Of those that a mesh axis runs over, the one named last changes fastest.
Arguments:
- qkv_local: bfloat16 [8, 64, 96, 3840], P('dp', 'tok'), may hold values from -4.5 to 4.5
- qkv_global: bfloat16 [8, 64, 96, 3840], P('dp', 'tok'), may hold values from -4.5 to 4.5
- positions: int32 [8, 64, 96], P('dp', 'tok'), may hold values from 0 to 191, as said below
- slopes: float32 [8], replicated, may hold values from 0.02 to 0.5
- cotangent: bfloat16 [8, 64, 96, 1280], P('dp', 'tok'), may hold values from -6 to 6
- w_out_local: bfloat16 [1280, 1280], replicated, may hold values from -0.15625 to 0.15625
- w_out_global: bfloat16 [1280, 1280], replicated, may hold values from -0.15625 to 0.15625
Outputs:
- d_qkv_local: bfloat16 [8, 64, 96, 3840], P('dp', 'tok')
- d_qkv_global: bfloat16 [8, 64, 96, 3840], P('dp', 'tok')
- grad_w_local: float32 [1280, 1280], P('tok')
- grad_w_global: float32 [1280, 1280], P('tok')
Inputs may be any that keep to these rules, and one draw needn't show every extreme that they name: In every window the 96 entries are distinct and increasing positions of a window of 12 rows and 16 columns, numbered row by row.
All inputs are finite; a program needn't handle non-finite values.
Results may differ from a plain program's by a relative error of at most 0.0063.
Values may be sent and summed in bfloat16 or wider, within the bound.
No kernel may reach another device: no remote copies, remote signals or barrier semaphores. Data moves between devices by JAX's collectives and lax.ppermute only.
A program may use at most 128 MiB of HBM per device.

v0:
```python
import jax
import jax.numpy as jnp
from jax import lax
from jax.sharding import PartitionSpec as P

WC = 16


def attention_back(queries, key_block, values, grad_out, distance_bias):
    scaling = queries.shape[-1] ** (-0.5)
    scores = (
        jnp.einsum("bhid,bhjd->bhij", queries, key_block, preferred_element_type=jnp.float32)
        * scaling
        + distance_bias
    )
    row_top = jnp.max(scores, axis=-1, keepdims=True)
    weights = jnp.exp(scores - row_top)
    probs_full = weights / jnp.sum(weights, axis=-1, keepdims=True)
    probs_low = probs_full.astype(jnp.bfloat16)
    mixture = jnp.einsum(
        "bhij,bhjd->bhid", probs_low, values, preferred_element_type=jnp.float32
    ).astype(jnp.bfloat16)
    grad_probs = jnp.einsum("bhid,bhjd->bhij", grad_out, values, preferred_element_type=jnp.float32)
    inner_sum = jnp.sum(probs_full * grad_probs, axis=-1, keepdims=True)
    grad_scores = (probs_full * (grad_probs - inner_sum)).astype(jnp.bfloat16)
    grad_queries = (
        jnp.einsum("bhij,bhjd->bhid", grad_scores, key_block, preferred_element_type=jnp.float32)
        * scaling
    ).astype(jnp.bfloat16)
    grad_keys = (
        jnp.einsum("bhij,bhid->bhjd", grad_scores, queries, preferred_element_type=jnp.float32)
        * scaling
    ).astype(jnp.bfloat16)
    grad_values = jnp.einsum(
        "bhij,bhid->bhjd", probs_low, grad_out, preferred_element_type=jnp.float32
    ).astype(jnp.bfloat16)
    return (mixture, grad_queries, grad_keys, grad_values)


def unpack(packed, head_count, head_width):
    shaped = packed.reshape(packed.shape[:-1] + (3, head_count, head_width))
    return (shaped[..., 0, :, :], shaped[..., 1, :, :], shaped[..., 2, :, :])


def project_back(flat_grad, weight):
    return lax.dot_general(
        flat_grad, weight, (((1,), (1,)), ((), ())), preferred_element_type=jnp.float32
    ).astype(jnp.bfloat16)


def contract(activation, flat_grad):
    return lax.dot_general(
        activation, flat_grad, (((0,), (0,)), ((), ())), preferred_element_type=jnp.float32
    )


def per_device(qkv_local, qkv_global, positions, slopes, cotangent, w_out_local, w_out_global):
    samples, windows, keep_count, packed_width = qkv_local.shape
    head_count = slopes.shape[0]
    inner_width = packed_width // 3
    head_width = inner_width // head_count
    dmodel = cotangent.shape[-1]
    tok_parts = lax.axis_size("tok")
    grad_scale = (samples * lax.axis_size("dp") * windows * tok_parts * keep_count) ** (-0.5)
    groups_qkv, groups_grad = (
        lax.all_to_all(qkv_global, "tok", split_axis=2, concat_axis=1, tiled=True),
        lax.all_to_all(cotangent, "tok", split_axis=2, concat_axis=1, tiled=True),
    )
    window_count = groups_qkv.shape[1]
    slot_count = groups_qkv.shape[2]
    grad_groups_flat = groups_grad.reshape(-1, dmodel)
    grad_act_global = project_back(grad_groups_flat, w_out_global).reshape(
        samples, window_count, slot_count, head_count, head_width
    )
    queries, key_block, values = unpack(groups_qkv, head_count, head_width)

    def to_batch(tensor):
        return jnp.transpose(tensor, (0, 2, 3, 1, 4)).reshape(
            samples * slot_count, head_count, window_count, head_width
        )

    def from_batch(tensor):
        return jnp.transpose(
            tensor.reshape(samples, slot_count, head_count, window_count, head_width),
            (0, 3, 1, 2, 4),
        )

    mixture, grad_queries, grad_keys, grad_values = attention_back(
        to_batch(queries), to_batch(key_block), to_batch(values), to_batch(grad_act_global), 0.0
    )
    act_global = from_batch(mixture).reshape(-1, inner_width)
    grads_groups = jnp.stack(
        [from_batch(grad_queries), from_batch(grad_keys), from_batch(grad_values)], axis=3
    ).reshape(samples, window_count, slot_count, packed_width)
    d_qkv_global = lax.all_to_all(grads_groups, "tok", split_axis=1, concat_axis=2, tiled=True)
    flat_grad = cotangent.reshape(-1, dmodel)
    grad_act_local = project_back(flat_grad, w_out_local).reshape(
        samples * windows, keep_count, head_count, head_width
    )
    queries, key_block, values = unpack(
        qkv_local.reshape(samples * windows, keep_count, packed_width), head_count, head_width
    )
    flat_pos = positions.reshape(samples * windows, keep_count)
    pos_rows = flat_pos // WC
    pos_cols = flat_pos % WC
    distance = (
        jnp.abs(pos_rows[:, :, None] - pos_rows[:, None, :])
        + jnp.abs(pos_cols[:, :, None] - pos_cols[:, None, :])
    ).astype(jnp.float32)
    distance_bias = -(slopes[None, :, None, None] * distance[:, None, :, :])

    def to_heads(tensor):
        return jnp.transpose(tensor, (0, 2, 1, 3))

    mixture, grad_queries, grad_keys, grad_values = attention_back(
        to_heads(queries),
        to_heads(key_block),
        to_heads(values),
        to_heads(grad_act_local),
        distance_bias,
    )
    act_local = to_heads(mixture).reshape(-1, inner_width)
    d_qkv_local = jnp.stack(
        [to_heads(grad_queries), to_heads(grad_keys), to_heads(grad_values)], axis=2
    ).reshape(samples, windows, keep_count, packed_width)
    joined = lax.psum_scatter(
        jnp.concatenate(
            [contract(act_local, flat_grad), contract(act_global, grad_groups_flat)], axis=1
        )
        * grad_scale,
        "tok",
        scatter_dimension=0,
        tiled=True,
    )
    rows_local = joined[:, :dmodel]
    rows_global = joined[:, dmodel:]
    rows_local, rows_global = lax.psum((rows_local, rows_global), "dp")
    return (d_qkv_local, d_qkv_global, rows_local, rows_global)


def solution(mesh):
    placed = (
        P("dp", "tok", None, None),
        P("dp", "tok", None, None),
        P("dp", "tok", None),
        P(),
        P("dp", "tok", None, None),
        P(),
        P(),
    )
    return jax.shard_map(
        per_device,
        mesh=mesh,
        in_specs=placed,
        out_specs=(
            P("dp", "tok", None, None),
            P("dp", "tok", None, None),
            P("tok", None),
            P("tok", None),
        ),
        check_vma=False,
    )
```

profile of v0, /device:TPU:1, one launch (start us, length us, event | category | flops | bytes accessed | tf_op | source)
XLA Modules:
  0.0 382.3 jit_solution(14607548578613637460)
XLA Ops:
  9.6 12.8 %all-to-all-start.1 = ((bf16[1,2,96,1280]{3,1,0,2:T(2,128)(2,1)}), bf16[1,2,96,1280]{3,1,0,2:T(2,128)(2,1)}, u32[]{:S(2)}, u32[]{:S(2)}) async-start(bf16[1,2,96,1280]{3,1,0,2:T(2,128)(2,1)} %copy.64), calls=%async_computation.1 | async-start | bytes 983040 | tf_op jit(solution)/shard_map/all_to_all | solution.py:67
  22.5 4.0 %copy.60 = bf16[1,2,96,3840]{3,1,0,2:T(2,128)(2,1)} copy(bf16[1,2,96,3840]{3,2,1,0:T(8,128)(2,1)} %param.8) | data formatting | bytes 2949120 | tf_op args[1]
  26.5 13.8 %all-to-all-done.1 = bf16[1,2,96,1280]{3,1,0,2:T(2,128)(2,1)} async-done(((bf16[1,2,96,1280]{3,1,0,2:T(2,128)(2,1)}), bf16[1,2,96,1280]{3,1,0,2:T(2,128)(2,1)}, u32[]{:S(2)}, u32[]{:S(2)}) %all-to-all-start.1) | async-done | bytes 491552 | tf_op jit(solution)/shard_map/all_to_all | solution.py:67
  40.3 4.5 %all-to-all-start = ((bf16[1,2,96,3840]{3,1,0,2:T(2,128)(2,1)}), bf16[1,2,96,3840]{3,1,0,2:T(2,128)(2,1)}, u32[]{:S(2)}, u32[]{:S(2)}) async-start(bf16[1,2,96,3840]{3,1,0,2:T(2,128)(2,1)} %copy.60), calls=%async_computation | async-start | bytes 2949120 | tf_op jit(solution)/shard_map/all_to_all | solution.py:66
  45.0 3.7 copy.50
  52.7 2.8 fusion.14
  55.4 2.5 copy.74
  58.0 2.6 reshape.190
  60.6 5.0 %fusion.31 = f32[1280,1280]{0,1:T(8,128)} fusion(bf16[192,1280]{1,0:T(8,128)(2,1)} %reshape.190, bf16[192,1280]{1,0:T(8,128)(2,1)} %bitcast.169), kind=kOutput, calls=%fused_computation.68 | convolution fusion | flops 629145600 | bytes 7536640 | tf_op jit(solution)/shard_map/dot_general | solution.py:52
  69.9 12.5 %all-to-all-done = bf16[1,2,96,3840]{3,1,0,2:T(2,128)(2,1)} async-done(((bf16[1,2,96,3840]{3,1,0,2:T(2,128)(2,1)}), bf16[1,2,96,3840]{3,1,0,2:T(2,128)(2,1)}, u32[]{:S(2)}, u32[]{:S(2)}) %all-to-all-start) | async-done | bytes 1474592 | tf_op jit(solution)/shard_map/all_to_all | solution.py:66
  82.4 3.5 copy.61
  85.9 6.1 %reshape.179 = bf16[1,64,3,3,8,160]{5,4,3,1,2,0:T(8,128)(2,1)} reshape(bf16[1,32,2,3,3840]{4,2,1,3,0:T(2,128)(2,1)} %copy.61) | data formatting | bytes 2949120 | tf_op jit(solution)/shard_map/reshape | solution.py:41
  92.0 2.7 fusion.27
  96.3 3.0 fusion.7
  99.3 2.5 copy.76
  101.8 2.6 reshape.192
  106.7 8.4 %maximum_multiply_fusion = f32[1280,2560]{0,1:T(8,128)} fusion(f32[1280,1280]{0,1:T(8,128)S(1)} %fusion.32, f32[1280,1280]{0,1:T(8,128)} %fusion.31), kind=kLoop, calls=%fused_computation.2 | loop fusion | flops 6553600 | bytes 26214400 | tf_op jit(solution)/shard_map/mul | solution.py:127
  115.1 14.0 %copy.89 = f32[1280,2560]{1,0:T(8,128)} copy(f32[1280,2560]{0,1:T(8,128)} %maximum_multiply_fusion) | data formatting | bytes 26214400
  129.1 3.1 convolution_convert_fusion
  132.2 2.7 reshape.183
  134.9 3.1 fusion.6
  143.1 2.7 copy.87
  145.9 6.8 %reshape.193 = bf16[1,64,3,3840]{3,2,0,1:T(4,128)(2,1)} reshape(bf16[1,64,3,3,8,160]{5,4,3,2,1,0:T(8,128)(2,1)} %copy.87) | data formatting | bytes 2949120 | tf_op jit(solution)/shard_map/reshape | solution.py:94
  152.6 6.0 %all-to-all-start.2 = ((bf16[1,64,3,3840]{3,2,0,1:T(4,128)(2,1)}), bf16[1,64,3,3840]{3,2,0,1:T(4,128)(2,1)}, u32[]{:S(2)}, u32[]{:S(2)}) async-start(bf16[1,64,3,3840]{3,2,0,1:T(4,128)(2,1)} %reshape.193), calls=%async_computation.2 | async-start | bytes 3932160 | tf_op jit(solution)/shard_map/all_to_all | solution.py:95
  158.7 4.4 %convolution_convert_fusion.1 = bf16[192,1280]{1,0:T(8,128)(2,1)} fusion(bf16[192,1280]{1,0:T(8,128)(2,1)} %bitcast.170, bf16[1280,1280]{1,0:T(8,128)(2,1)} %param.12), kind=kOutput, calls=%fused_computation.4 | convolution fusion | flops 629391360 | bytes 4259840 | tf_op jit(solution)/shard_map/dot_general | solution.py:46
  163.1 2.7 reshape.177
  165.8 2.6 copy.54
  173.9 114.2 %reduce-scatter.4.cloned.1.call-done = f32[40,2560]{1,0:T(8,128)} async-done(((f32[1280,2560]{1,0:T(8,128)}), f32[40,2560]{1,0:T(8,128)}) %reduce-scatter.4.cloned.1.call-update) | async-done | bytes 409616
  293.0 2.8 fusion.13
  299.3 3.8 copy.77
  303.1 2.9 copy.122
  308.3 63.2 %all-reduce.3.cloned.1.call-done = (f32[40,1280]{0,1:T(8,128)}, f32[40,1280]{0,1:T(8,128)}) async-done(((f32[40,1280]{0,1:T(8,128)}, f32[40,1280]{0,1:T(8,128)}), (f32[40,1280]{0,1:T(8,128)}, f32[40,1280]{0,1:T(8,128)})) %all-reduce.3.cloned.1.call-update) | async-done | bytes 409616 | tf_op jit(solution)/shard_map/psum | solution.py:137
  (63 shorter events, 39.9 us)
Async XLA Ops:
  7.2 121.9 %copy-start = (bf16[1280,1280]{1,0:T(8,128)(2,1)S(1)}, bf16[1280,1280]{1,0:T(8,128)(2,1)}, u32[]{:S(2)}) copy-start(bf16[1280,1280]{1,0:T(8,128)(2,1)} %param.13) | copy-start | bytes 9830404
  9.6 30.6 %all-to-all-start.1 = ((bf16[1,2,96,1280]{3,1,0,2:T(2,128)(2,1)}), bf16[1,2,96,1280]{3,1,0,2:T(2,128)(2,1)}, u32[]{:S(2)}, u32[]{:S(2)}) async-start(bf16[1,2,96,1280]{3,1,0,2:T(2,128)(2,1)} %copy.64), calls=%async_computation.1 | async-start | bytes 983040 | tf_op jit(solution)/shard_map/all_to_all | solution.py:67
  40.3 42.1 %all-to-all-start = ((bf16[1,2,96,3840]{3,1,0,2:T(2,128)(2,1)}), bf16[1,2,96,3840]{3,1,0,2:T(2,128)(2,1)}, u32[]{:S(2)}, u32[]{:S(2)}) async-start(bf16[1,2,96,3840]{3,1,0,2:T(2,128)(2,1)} %copy.60), calls=%async_computation | async-start | bytes 2949120 | tf_op jit(solution)/shard_map/all_to_all | solution.py:66
  44.8 4.0 %copy-start.13 = (s32[1,2,96]{2,1,0:T(2,128)S(1)}, s32[1,2,96]{2,1,0:T(2,128)}, u32[]{:S(2)}) copy-start(s32[1,2,96]{2,1,0:T(2,128)} %param.9) | copy-start | bytes 2308
  44.8 4.1 %copy-start.14 = (f32[8]{0:T(128)S(1)}, f32[8]{0:T(128)}, u32[]{:S(2)}) copy-start(f32[8]{0:T(128)} %param.10) | copy-start | bytes 100
  44.8 243.3 %reduce-scatter.4.cloned.1.call-start = ((), (), s32[]{:S(2)}) async-start(), calls=%async_computation.4 | async-start | bytes 13516800
  50.7 0.9 copy-start.10
  94.7 1.6 copy-start.2
  94.7 1.6 copy-start.4
  95.1 1.2 copy-start.11
  138.0 2.2 copy-start.7
  140.1 1.2 copy-start.5
  140.2 1.6 copy-start.3
  141.4 1.2 copy-start.9
  152.6 150.5 %all-to-all-start.2 = ((bf16[1,64,3,3840]{3,2,0,1:T(4,128)(2,1)}), bf16[1,64,3,3840]{3,2,0,1:T(4,128)(2,1)}, u32[]{:S(2)}, u32[]{:S(2)}) async-start(bf16[1,64,3,3840]{3,2,0,1:T(4,128)(2,1)} %reshape.193), calls=%async_computation.2 | async-start | bytes 3932160 | tf_op jit(solution)/shard_map/all_to_all | solution.py:95
  158.6 212.9 %all-reduce.3.cloned.1.call-start = ((), (), s32[]{:S(2)}) async-start(), calls=%async_computation.5 | async-start | bytes 2621440 | tf_op jit(solution)/shard_map/psum | solution.py:137
  168.4 2.2 copy-start.6
  170.8 0.8 copy-start.1
  295.7 1.6 copy-start.8
  295.7 1.6 copy-start.12
Sparse Core Ops, SparseCore 0:
  129.2 158.8 reduce-scatter.3
  293.1 78.4 all-reduce.2
where the time goes:
time: 388 us; the launch traced here: 382 us
  waiting for transfers between devices  204 us (53%)
  local copies, waits for them, and re-layouts  90.8 us (23%)
  matrix products  37.6 us (10%)
  starting transfers between devices  23.6 us (6%)
  between operations  14.3 us (4%)
  other arithmetic  12.2 us (3%)
    unnamed x3, waiting for transfers between devices  114 us
    psum x1, waiting for transfers between devices, per_device(): rows_local, rows_global = lax.psum((rows_local, rows_global), 'dp')  63.2 us
    unnamed x40, local copies, waits for them, and re-layouts  39.3 us
    all_to_all x1, waiting for transfers between devices, per_device(): lax.all_to_all(cotangent, 'tok', split_axis=2, concat_axis=1, tiled=True)  13.8 us
    all_to_all x1, starting transfers between devices, per_device(): lax.all_to_all(cotangent, 'tok', split_axis=2, concat_axis=1, tiled=True)  12.8 us
    all_to_all x1, waiting for transfers between devices, per_device(): lax.all_to_all(qkv_global, 'tok', split_axis=2, concat_axis=1, tiled=True)  12.5 us
    reshape x2, local copies, waits for them, and re-layouts, per_device(): grads_groups = jnp.stack([from_batch(grad_queries), from_batch(grad_keys)...  9.48 us
    mul x1, other arithmetic, per_device(): jnp.concatenate([contract(act_local, flat_grad), contract(act_global, gra...  8.39 us
  transfers between devices with their start and end apart: 5, of which 4 were waited for; matrix products, arithmetic and copies ran while one was open for 22% of the time, Pallas kernels for 0%

commit v1 on v0

v1 whole, which is shorter than its diff:
```python
import functools

import jax
import jax.numpy as jnp
import numpy as np
from jax import lax
from jax.experimental import pallas as pl
from jax.experimental.pallas import tpu as pltpu
from jax.sharding import PartitionSpec as P

WC = 16
HW = 160
VMEM_LIMIT = 56 * 1024 * 1024
BF16 = jnp.bfloat16
F32 = jnp.float32


def dot_nn(a, b):
    return lax.dot_general(a, b, (((1,), (0,)), ((), ())), preferred_element_type=F32)


def dot_nt(a, b):
    return lax.dot_general(a, b, (((1,), (1,)), ((), ())), preferred_element_type=F32)


def dot_tn(a, b):
    return lax.dot_general(a, b, (((0,), (0,)), ((), ())), preferred_element_type=F32)


def order_matrix(old, new):
    sizes = dict(old)
    count = int(np.prod(list(sizes.values())))
    index = np.arange(count).reshape([s for _, s in old])
    names = [n for n, _ in old]
    moved = np.transpose(index, [names.index(n) for n in new]).reshape(-1)
    hot = np.zeros((count, count), np.float32)
    hot[np.arange(count), moved] = 1.0
    return hot


HOME = order_matrix([("s", 4), ("w", 2), ("p", 16), ("t", 3)], ["p", "s", "w", "t"])
GROUP = order_matrix([("p", 16), ("s", 4), ("w", 2), ("t", 3)], ["s", "t", "p", "w"])


def call(kernel, outs, *args, smem=(), scratch=(), flops=0, name=None):
    specs = [
        pl.BlockSpec(memory_space=pltpu.SMEM if i in smem else pltpu.VMEM)
        for i in range(len(args))
    ]
    size = sum(int(np.prod(a.shape)) * a.dtype.itemsize for a in args)
    size += sum(int(np.prod(o.shape)) * o.dtype.itemsize for o in outs)
    return pl.pallas_call(
        kernel,
        out_shape=outs,
        in_specs=specs,
        out_specs=[pl.BlockSpec(memory_space=pltpu.VMEM) for _ in outs],
        scratch_shapes=scratch,
        compiler_params=pltpu.CompilerParams(vmem_limit_bytes=VMEM_LIMIT),
        cost_estimate=pl.CostEstimate(flops=flops, bytes_accessed=size, transcendentals=0),
        name=name,
    )(*args)


def sds(shape, dtype):
    return jax.ShapeDtypeStruct(shape, dtype)


def head_masks():
    lane = lax.broadcasted_iota(jnp.int32, (1, 256), 1)
    return [
        ((lane >= 32 * h) & (lane < 32 * h + HW)).astype(F32).astype(BF16) for h in range(4)
    ]


def side_by_side(parts):
    lane = lax.broadcasted_iota(jnp.int32, (1, 128), 1)
    tiles = [parts[0][:, :128]]
    for h in range(3):
        tiles.append(jnp.where(lane < 32 * (h + 1), parts[h][:, 128:], parts[h + 1][:, :128]))
    tiles.append(parts[3][:, 128:])
    return jnp.concatenate(tiles, axis=1)


def four_heads(q, k, v, g, masks, bias=None):
    scaling = HW ** (-0.5)
    act, dq, dk, dv = [], [], [], []
    for h in range(4):
        win = slice(128 * h, 128 * h + 256)
        qh, kh, vh, gh = q[:, win], k[:, win], v[:, win], g[:, win]
        scores = dot_nt(qh * masks[h], kh) * scaling
        if bias is not None:
            scores = scores + bias(h)
        weights = jnp.exp(scores - jnp.max(scores, axis=-1, keepdims=True))
        probs = weights / jnp.sum(weights, axis=-1, keepdims=True)
        low = probs.astype(BF16)
        grad_probs = dot_nt(gh * masks[h], vh)
        inner = jnp.sum(probs * grad_probs, axis=-1, keepdims=True)
        grad_scores = (probs * (grad_probs - inner)).astype(BF16)
        act.append(dot_nn(low, vh))
        dq.append(dot_nn(grad_scores, kh) * scaling)
        dk.append(dot_tn(grad_scores, qh) * scaling)
        dv.append(dot_tn(low, gh))
    return [side_by_side(x).astype(BF16) for x in (act, dq, dk, dv)]


def row_order(place):
    x, zh, y, c = place[0], place[1], place[2], place[3]
    col = lax.broadcasted_iota(jnp.int32, (8, 1280), 1)
    half = jnp.where(col >= 640, 1, 0)
    rem = col - 640 * half

    def digit(value, size):
        total = jnp.zeros_like(value)
        for k in range(1, 4):
            total = total + jnp.where(value >= k * size, 1, 0)
        return total, value - total * size

    dx, rem = digit(rem, 160)
    dy, rem = digit(rem, 40)
    dz, rem = digit(rem, 10)
    core = (c + half) & 1
    lane = ((((zh + dz) & 3) * 4 + ((y + dy) & 3)) * 2 + core) * 40 + ((x + dx) & 3) * 10 + rem
    return lane


def in_row_order(act, place):
    lane = row_order(place)[:1]
    pieces = []
    for part in range(5):
        rows = lax.broadcasted_iota(jnp.int32, (1280, 256), 0)
        hot = (rows == lane[:, 256 * part : 256 * part + 256]).astype(F32).astype(BF16)
        pieces.append(dot_nn(act, hot).astype(BF16))
    return jnp.concatenate(pieces, axis=1)


def pack_kernel(qkv, cot, order, out):
    hot = order[...]
    for c in range(2):
        rows = slice(48 * c, 48 * c + 48)
        pieces = [qkv[w, rows, 1280 * s : 1280 * s + 1280] for s in range(3) for w in range(2)]
        pieces += [cot[w, rows, :] for w in range(2)]
        whole = jnp.concatenate(pieces, axis=0)
        out[384 * c : 384 * c + 384, :] = dot_nn(hot, whole).astype(BF16)


def unpack_kernel(got, order, out):
    hot = order[...]
    for c in range(2):
        rows = dot_tn(hot, got[384 * c : 384 * c + 384, :]).astype(BF16)
        for s in range(4):
            width = 1024 if s < 3 else 768
            for w in range(2):
                start = 96 * s + 48 * w
                out[w, 48 * c : 48 * c + 48, 1024 * s : 1024 * s + width] = rows[
                    start : start + 48, :width
                ]


def local_kernel(place, slopes, qkv, cot, weight, positions, d_out, act_own, act_other, act_all):
    masks = head_masks()
    flat = jnp.concatenate([cot[0], cot[1]], axis=0)
    g = dot_nt(flat, weight[...]).astype(BF16)
    for w in range(2):
        spread = jnp.broadcast_to(positions[w : w + 1, :], (96, 96))
        spread_t = spread.astype(F32).T.astype(jnp.int32)
        distance = (
            jnp.abs((spread >> 4) - (spread_t >> 4)) + jnp.abs((spread & 15) - (spread_t & 15))
        ).astype(F32)
        for half in range(2):
            lanes = slice(640 * half, 640 * half + 640)
            q, k, v = [
                qkv[w, :, 1280 * s + 640 * half : 1280 * s + 640 * half + 640] for s in range(3)
            ]
            act, dq, dk, dv = four_heads(
                q,
                k,
                v,
                g[96 * w : 96 * w + 96, lanes],
                masks,
                lambda h: -(slopes[4 * half + h] * distance),
            )
            act_all[96 * w : 96 * w + 96, lanes] = act
            for s, part in enumerate((dq, dk, dv)):
                d_out[w, :, 1280 * s + 640 * half : 1280 * s + 640 * half + 640] = part
    ordered = in_row_order(act_all[...], place)
    act_own[...] = ordered[:, :640]
    act_other[...] = ordered[:, 640:]


def global_kernel(place, got, weight, order, back, act_own, act_other, cot, data, grads, act_all):
    masks = head_masks()
    hot = order[...]
    for c in range(2):
        rows = dot_nn(hot, got[384 * c : 384 * c + 384, :]).astype(BF16)
        for s in range(4):
            for t in range(3):
                start = 96 * s + 32 * t
                piece = rows[start : start + 32, :]
                if s < 3:
                    data[s, 64 * t + 32 * c : 64 * t + 32 * c + 32, :] = piece
                else:
                    cot[64 * t + 32 * c : 64 * t + 32 * c + 32, :] = piece
    g = dot_nt(cot[...], weight[...]).astype(BF16)
    grads[:, 3840:] = jnp.zeros((192, 256), BF16)
    for t in range(3):
        rows = slice(64 * t, 64 * t + 64)
        for half in range(2):
            lanes = slice(640 * half, 640 * half + 640)
            q, k, v = [data[s, rows, lanes] for s in range(3)]
            act, dq, dk, dv = four_heads(q, k, v, g[rows, lanes], masks)
            act_all[rows, lanes] = act
            for s, part in enumerate((dq, dk, dv)):
                grads[rows, 1280 * s + 640 * half : 1280 * s + 640 * half + 640] = part
    for c in range(2):
        pieces = [
            grads[64 * t + 32 * c : 64 * t + 32 * c + 32, 1024 * s : 1024 * s + 1024]
            for s in range(4)
            for t in range(3)
        ]
        whole = jnp.concatenate(pieces, axis=0)
        back[384 * c : 384 * c + 384, :] = dot_tn(hot, whole).astype(BF16)
    ordered = in_row_order(act_all[...], place)
    act_own[...] = ordered[:, :640]
    act_other[...] = ordered[:, 640:]


def weight_kernel(act, act_far, cot, cot_far, own, one, two, three):
    a, b = act[...], act_far[...]
    for part in range(5):
        cols = slice(256 * part, 256 * part + 256)
        total = dot_tn(a, cot[:, cols]) + dot_tn(b, cot_far[:, cols])
        own[:, cols] = total[:160]
        for d, ref in ((1, one), (2, two), (3, three)):
            ref[:, cols] = total[160 * d : 160 * d + 160].astype(BF16)


def sum_x_kernel(own, a, b, c, kept, one, two, three):
    total = own[...] + a[...].astype(F32) + b[...].astype(F32) + c[...].astype(F32)
    kept[...] = total[:40]
    for d, ref in ((1, one), (2, two), (3, three)):
        ref[...] = total[40 * d : 40 * d + 40].astype(BF16)


def sum_y_kernel(own, a, b, c, total):
    total[...] = own[...] + a[...].astype(F32) + b[...].astype(F32) + c[...].astype(F32)


def join_kernel(local, own, a, b, c, kept, one, two, three):
    first = local[...]
    second = own[...] + a[...].astype(F32) + b[...].astype(F32) + c[...].astype(F32)
    for d, ref in ((0, kept), (1, one), (2, two), (3, three)):
        rows = slice(10 * d, 10 * d + 10)
        both = jnp.concatenate([first[rows], second[rows], jnp.zeros((4, 1280), F32)], axis=0)
        ref[...] = both.astype(ref.dtype)


def sum_z_kernel(own, a, b, c, total):
    total[...] = own[...] + a[...].astype(F32) + b[...].astype(F32) + c[...].astype(F32)


def final_kernel(scale, place, *refs):
    pieces, (local, glob) = refs[:8], refs[8:]
    x = place[0]
    sums = [(pieces[2 * d][...] + pieces[2 * d + 1][...]) * scale for d in range(4)]
    for p in range(4):
        d = (x - p) & 3
        chosen = jnp.where(
            d == 0, sums[0], jnp.where(d == 1, sums[1], jnp.where(d == 2, sums[2], sums[3]))
        )
        local[10 * p : 10 * p + 10, :] = chosen[:10]
        glob[10 * p : 10 * p + 10, :] = chosen[10:20]


def chip(z, y, c):
    return z * 8 + y * 2 + c


def swap_cores(a):
    return lax.ppermute(a, "tok", [(i, i ^ 1) for i in range(32)])


def along_x(a, d, flip=0):
    pairs = [
        (z * 4 + x, (z ^ flip) * 4 + (x + d) % 4) for z in range(2) for x in range(4)
    ]
    return lax.ppermute(a, "dp", pairs)


def along_tok(a, dz, dy):
    pairs = [
        (chip(z, y, c), chip((z + dz) % 4, (y + dy) % 4, c))
        for z in range(4)
        for y in range(4)
        for c in range(2)
    ]
    return lax.ppermute(a, "tok", pairs)


TOK_ORDER = [[chip(0, 0, c) + 2 * p for c in range(2) for p in range(16)]]


def exchange(a):
    return lax.all_to_all(
        a, "tok", split_axis=0, concat_axis=0, axis_index_groups=TOK_ORDER, tiled=True
    )


def weight_sums(act_own, act_other, cot, name):
    act_far = swap_cores(act_other)
    cot_far = swap_cores(cot)
    own, one, two, three = call(
        weight_kernel,
        [sds((160, 1280), F32)] + [sds((160, 1280), BF16)] * 3,
        act_own,
        act_far,
        cot,
        cot_far,
        flops=2 * 640 * 384 * 1280,
        name=name + "_weight",
    )
    a, b, c = along_x(one, 1), along_x(two, 2), along_x(three, 3)
    own, one, two, three = call(
        sum_x_kernel,
        [sds((40, 1280), F32)] + [sds((40, 1280), BF16)] * 3,
        own,
        a,
        b,
        c,
        name=name + "_sum_x",
    )
    return own, along_tok(one, 0, 1), along_tok(two, 0, 2), along_tok(three, 0, 3)


def per_device(qkv_local, qkv_global, positions, slopes, cotangent, w_out_local, w_out_global):
    tokens = 192 * 256
    scale = float(tokens) ** (-0.5)
    dp, tok = lax.axis_index("dp"), lax.axis_index("tok")
    place = jnp.stack([dp % 4, tok // 8, (tok // 2) % 4, tok % 2]).astype(jnp.int32)
    qkv_local = qkv_local.reshape(2, 96, 3840)
    qkv_global = qkv_global.reshape(2, 96, 3840)
    cotangent = cotangent.reshape(2, 96, 1280)
    positions = positions.reshape(2, 96)
    home = jnp.asarray(HOME, BF16)
    group = jnp.asarray(GROUP, BF16)

    (packed,) = call(
        pack_kernel, [sds((768, 1280), BF16)], qkv_global, cotangent, home, name="pack"
    )
    got = exchange(packed)

    d_local, act_own, act_other = call(
        local_kernel,
        [sds((2, 96, 3840), BF16), sds((192, 640), BF16), sds((192, 640), BF16)],
        place,
        slopes,
        qkv_local,
        cotangent,
        w_out_local,
        positions,
        smem=(0, 1),
        scratch=[pltpu.VMEM((192, 1280), BF16)],
        flops=2 * 10**9,
        name="local",
    )
    own, a, b, c = weight_sums(act_own, act_other, cotangent.reshape(192, 1280), "local")
    (sum_local,) = call(sum_y_kernel, [sds((40, 1280), F32)], own, a, b, c, name="local_sum_y")

    back, act_own, act_other, cot = call(
        global_kernel,
        [
            sds((768, 1024), BF16),
            sds((192, 640), BF16),
            sds((192, 640), BF16),
            sds((192, 1280), BF16),
        ],
        place,
        got,
        w_out_global,
        group,
        smem=(0,),
        scratch=[
            pltpu.VMEM((3, 192, 1280), BF16),
            pltpu.VMEM((192, 4096), BF16),
            pltpu.VMEM((192, 1280), BF16),
        ],
        flops=2 * 10**9,
        name="global",
    )
    returned = exchange(back)
    own, a, b, c = weight_sums(act_own, act_other, cot, "global")
    own, one, two, three = call(
        join_kernel,
        [sds((24, 1280), F32)] + [sds((24, 1280), BF16)] * 3,
        sum_local,
        own,
        a,
        b,
        c,
        name="join",
    )
    a, b, c = along_tok(one, 1, 0), along_tok(two, 2, 0), along_tok(three, 3, 0)
    (mine,) = call(sum_z_kernel, [sds((24, 1280), F32)], own, a, b, c, name="sum_z")
    pieces = [
        mine if d == 0 and flip == 0 else along_x(mine, d, flip)
        for d in range(4)
        for flip in range(2)
    ]
    grad_local, grad_global = call(
        functools.partial(final_kernel, scale),
        [sds((40, 1280), F32), sds((40, 1280), F32)],
        place,
        *pieces,
        smem=(0,),
        name="final",
    )
    (d_global,) = call(
        unpack_kernel, [sds((2, 96, 3840), BF16)], returned, home, name="unpack"
    )
    return (
        d_local.reshape(1, 2, 96, 3840),
        d_global.reshape(1, 2, 96, 3840),
        grad_local,
        grad_global,
    )


def solution(mesh):
    placed = (
        P("dp", "tok", None, None),
        P("dp", "tok", None, None),
        P("dp", "tok", None),
        P(),
        P("dp", "tok", None, None),
        P(),
        P(),
    )
    return jax.shard_map(
        per_device,
        mesh=mesh,
        in_specs=placed,
        out_specs=(
            P("dp", "tok", None, None),
            P("dp", "tok", None, None),
            P("tok", None),
            P("tok", None),
        ),
        check_vma=False,
    )
```

time: 388 us -> 206 us (0.53); the launches traced: 382 us -> 206 us
  waiting for transfers between devices: 204 us -> 79.1 us
  local copies, waits for them, and re-layouts: 90.8 us -> 8.94 us
  Pallas kernels: 0 us -> 57.3 us
  matrix products: 37.6 us -> 0 us
  starting transfers between devices: 23.6 us -> 59.1 us
  between operations: 14.3 us -> 0.84 us
  other arithmetic: 12.2 us -> 0.64 us
    unnamed x3 -> x0, waiting for transfers between devices: 114 us -> none
    psum x1 -> x0, waiting for transfers between devices: 63.2 us -> none  [per_device(): rows_local, rows_global = lax.psum((rows_local, rows_global), 'dp')]
    pallas_call x0 -> x12, Pallas kernels: none -> 57.3 us  [call(): pl.pallas_call(kernel, out_shape=outs, in_specs=specs, out_specs=[pl.Bloc...]
    ppermute x0 -> x26, starting transfers between devices: none -> 38.8 us  [the longest x9 20.4 us: along_tok(): return lax.ppermute(a, 'tok', pairs)]
    dot_general x16 -> x0, matrix products: 37.6 us -> none  [the longest x2 7.48 us: project_back(): lax.dot_general(flat_grad, weight, (((1,), (1,)), ((), ())), preferred_el...]
    ppermute x0 -> x26, waiting for transfers between devices: none -> 33 us  [the longest x13 27.7 us: along_x(): return lax.ppermute(a, 'dp', pairs)]
    unnamed x40 -> x62, local copies, waits for them, and re-layouts: 39.3 us -> 8.94 us
    reshape x8 -> x0, local copies, waits for them, and re-layouts: 28.4 us -> none  [the longest x2 9.48 us: per_device(): grads_groups = jnp.stack([from_batch(grad_queries), from_batch(grad_keys)...]
  transfers between devices with their start and end apart: 5 -> 28, of which waited for: 4 -> 15; matrix products, arithmetic and copies ran while one was open for 22% -> 0% of each run, Pallas kernels for 0% -> 16%
where the time goes in v1:
time: 206 us
  waiting for transfers between devices  79.1 us (38%)
  starting transfers between devices  59.1 us (29%)
  Pallas kernels  57.3 us (28%)
  local copies, waits for them, and re-layouts  8.94 us (4%)
    pallas_call x12, Pallas kernels, call(): pl.pallas_call(kernel, out_shape=outs, in_specs=specs, out_specs=[pl.Bloc...  57.3 us
    all_to_all x2, waiting for transfers between devices, exchange(): lax.all_to_all(a, 'tok', split_axis=0, concat_axis=0, axis_index_groups=T...  46.1 us
    ppermute x13, waiting for transfers between devices, along_x(): return lax.ppermute(a, 'dp', pairs)  27.7 us
    ppermute x9, starting transfers between devices, along_tok(): return lax.ppermute(a, 'tok', pairs)  20.4 us
    all_to_all x2, starting transfers between devices, exchange(): lax.all_to_all(a, 'tok', split_axis=0, concat_axis=0, axis_index_groups=T...  20.3 us
    ppermute x13, starting transfers between devices, along_x(): return lax.ppermute(a, 'dp', pairs)  16.8 us
    unnamed x62, local copies, waits for them, and re-layouts  8.94 us
  transfers between devices with their start and end apart: 28, of which 15 were waited for; matrix products, arithmetic and copies ran while one was open for 0% of the time, Pallas kernels for 16%

profile of v1, /device:TPU:1, one launch (start us, length us, event | category | flops | bytes accessed | tf_op | source)
XLA Modules:
  0.0 205.9 jit_solution(6582323004068952177)
XLA Ops:
  0.6 4.0 %pack.1 = bf16[768,1280]{1,0:T(8,128)(2,1)} custom-call(bf16[2,96,3840]{2,1,0:T(8,128)(2,1)} %bitcast.19, bf16[2,96,1280]{2,1,0:T(8,128)(2,1)} %bitcast.21, bf16[384,384]{1,0:T(8,128)(2,1)} %constant.61.clone.order), custom_call_target="tpu_custom_call" | custom-call | bytes 4227072 | tf_op jit(solution)/shard_map/pack/pallas_call | solution.py:52
  4.7 12.8 %all-to-all-start = ((bf16[32,24,1280]{2,1,0:T(8,128)(2,1)}), bf16[32,24,1280]{2,1,0:T(8,128)(2,1)S(1)}, u32[]{:S(2)}, u32[]{:S(2)}) async-start(bf16[32,24,1280]{2,1,0:T(8,128)(2,1)} %bitcast.15), calls=%async_computation | async-start | bytes 3932160 | tf_op jit(solution)/shard_map/all_to_all | solution.py:303
  18.1 46.1 %all-to-all-done = bf16[32,24,1280]{2,1,0:T(8,128)(2,1)S(1)} async-done(((bf16[32,24,1280]{2,1,0:T(8,128)(2,1)}), bf16[32,24,1280]{2,1,0:T(8,128)(2,1)S(1)}, u32[]{:S(2)}, u32[]{:S(2)}) %all-to-all-start) | async-done | bytes 1966112 | tf_op jit(solution)/shard_map/all_to_all | solution.py:303
  65.5 17.6 %global.1 = (bf16[768,1024]{1,0:T(8,128)(2,1)}, bf16[192,640]{1,0:T(8,128)(2,1)}, bf16[192,640]{1,0:T(8,128)(2,1)}, bf16[192,1280]{1,0:T(8,128)(2,1)}) custom-call(s32[4]{0:T(128)} %pad_add_fusion.place, bf16[768,1280]{1,0:T(8,128)(2,1)} %bitcast.17, bf16[1280,1280]{1,0:T(8,128)(2,1)} %weight.3, bf16[384,384]{1,0:T(8,128)(2,1)} %constant.62.clone.order), custom_call_target="tpu_custom_call" | custom-call | flops 2000000000 | bytes 8093712 | tf_op jit(solution)/shard_map/global/pallas_call | solution.py:52
  83.1 7.5 %all-to-all-start.1 = ((bf16[32,24,1024]{2,1,0:T(8,128)(2,1)}), bf16[32,24,1024]{2,1,0:T(8,128)(2,1)S(1)}, u32[]{:S(2)}, u32[]{:S(2)}) async-start(bf16[32,24,1024]{2,1,0:T(8,128)(2,1)} %bitcast.18), calls=%async_computation.1 | async-start | bytes 3145728 | tf_op jit(solution)/shard_map/all_to_all | solution.py:303
  91.2 12.5 %local.1 = (bf16[2,96,3840]{2,1,0:T(8,128)(2,1)}, bf16[192,640]{1,0:T(8,128)(2,1)}, bf16[192,640]{1,0:T(8,128)(2,1)}) custom-call(s32[4]{0:T(128)} %pad_add_fusion.place, f32[8]{0:T(128)} %slopes.1, bf16[2,96,3840]{2,1,0:T(8,128)(2,1)} %bitcast.25, bf16[2,96,1280]{2,1,0:T(8,128)(2,1)} %bitcast.22, bf16[1280,1280]{1,0:T(8,128)(2,1)} %weight.2, s32[2,96]{1,0:T(2,128)} %bitcast.26), custom_call_target="tpu_custom_call" | custom-call | flops 2000000000 | bytes 7209776 | tf_op jit(solution)/shard_map/local/pallas_call | solution.py:52
  106.3 3.7 %local_weight.1 = (f32[160,1280]{1,0:T(8,128)}, bf16[160,1280]{1,0:T(8,128)(2,1)}, bf16[160,1280]{1,0:T(8,128)(2,1)}, bf16[160,1280]{1,0:T(8,128)(2,1)}) custom-call(bf16[192,640]{1,0:T(8,128)(2,1)} %get-tuple-element.35.act, bf16[192,640]{1,0:T(8,128)(2,1)} %copy-done.30, bf16[192,1280]{1,0:T(8,128)(2,1)} %bitcast.23, bf16[192,1280]{1,0:T(8,128)(2,1)} %copy-done.27), custom_call_target="tpu_custom_call" | custom-call | flops 629145600 | bytes 3522560 | tf_op jit(solution)/shard_map/local_weight/pallas_call | solution.py:52
  111.4 2.5 %collective-permute-start.3 = (bf16[160,1280]{1,0:T(8,128)(2,1)}, bf16[160,1280]{1,0:T(8,128)(2,1)S(1)}, u32[]{:S(2)}, u32[]{:S(2)}) collective-permute-start(bf16[160,1280]{1,0:T(8,128)(2,1)} %get-tuple-element.39), channel_id=1, source_target_pairs={{0,64},{32,96},{64,0},{96,32},{128,192},{160,224},{192,128},{224,1... | collective-permute-start | bytes 1228808 | tf_op jit(solution)/shard_map/ppermute | solution.py:286
  116.3 3.7 %global_weight.1 = (f32[160,1280]{1,0:T(8,128)}, bf16[160,1280]{1,0:T(8,128)(2,1)}, bf16[160,1280]{1,0:T(8,128)(2,1)}, bf16[160,1280]{1,0:T(8,128)(2,1)}) custom-call(bf16[192,640]{1,0:T(8,128)(2,1)} %get-tuple-element.45.act, bf16[192,640]{1,0:T(8,128)(2,1)} %copy-done.29, bf16[192,1280]{1,0:T(8,128)(2,1)} %get-tuple-element.47.cot, ...), custom_call_target="tpu_custom_call" | custom-call | flops 629145600 | bytes 3522560 | tf_op jit(solution)/shard_map/global_weight/pallas_call | solution.py:52
  123.2 8.5 %collective-permute-done.3.b = bf16[160,1280]{1,0:T(8,128)(2,1)S(1)} collective-permute-done((bf16[160,1280]{1,0:T(8,128)(2,1)}, bf16[160,1280]{1,0:T(8,128)(2,1)S(1)}, u32[]{:S(2)}, u32[]{:S(2)}) %collective-permute-start.3) | collective-permute-done | bytes 409632 | tf_op jit(solution)/shard_map/ppermute | solution.py:286
  133.2 2.3 %local_sum_x.1 = (f32[40,1280]{1,0:T(8,128)}, bf16[40,1280]{1,0:T(8,128)(2,1)}, bf16[40,1280]{1,0:T(8,128)(2,1)}, bf16[40,1280]{1,0:T(8,128)(2,1)}) custom-call(f32[160,1280]{1,0:T(8,128)} %get-tuple-element.37.own, bf16[160,1280]{1,0:T(8,128)(2,1)} %copy-done.4, bf16[160,1280]{1,0:T(8,128)(2,1)} %copy-done.6, bf16[160,1280]{1,0:T(8,128)(2,1)} %copy-done.8), custom_call_target="tpu_custom_call" | custom-call | bytes 2560000 | tf_op jit(solution)/shard_map/local_sum_x/pallas_call | solution.py:52
  136.8 2.4 %collective-permute-start.6 = (bf16[40,1280]{1,0:T(8,128)(2,1)}, bf16[40,1280]{1,0:T(8,128)(2,1)S(1)}, u32[]{:S(2)}, u32[]{:S(2)}) collective-permute-start(bf16[40,1280]{1,0:T(8,128)(2,1)} %get-tuple-element.43), channel_id=1, source_target_pairs={{0,4},{1,5},{2,6},{3,7},{4,0},{5,1},{6,2},{7,3},{8,12},{9,13},{10,... | collective-permute-start | bytes 307208 | tf_op jit(solution)/shard_map/ppermute | solution.py:296
  139.2 1.9 collective-permute-done.10.a
  141.1 2.6 %collective-permute-start.7 = (bf16[40,1280]{1,0:T(8,128)(2,1)}, bf16[40,1280]{1,0:T(8,128)(2,1)S(1)}, u32[]{:S(2)}, u32[]{:S(2)}) collective-permute-start(bf16[40,1280]{1,0:T(8,128)(2,1)} %get-tuple-element.44), channel_id=1, source_target_pairs={{0,6},{1,7},{2,0},{3,1},{4,2},{5,3},{6,4},{7,5},{8,14},{9,15},{10,... | collective-permute-start | bytes 307208 | tf_op jit(solution)/shard_map/ppermute | solution.py:296
  143.8 5.5 %collective-permute-done.11.b = bf16[160,1280]{1,0:T(8,128)(2,1)S(1)} collective-permute-done((bf16[160,1280]{1,0:T(8,128)(2,1)}, bf16[160,1280]{1,0:T(8,128)(2,1)S(1)}, u32[]{:S(2)}, u32[]{:S(2)}) %collective-permute-start.11) | collective-permute-done | bytes 409632 | tf_op jit(solution)/shard_map/ppermute | solution.py:286
  150.8 2.4 %global_sum_x.1 = (f32[40,1280]{1,0:T(8,128)}, bf16[40,1280]{1,0:T(8,128)(2,1)}, bf16[40,1280]{1,0:T(8,128)(2,1)}, bf16[40,1280]{1,0:T(8,128)(2,1)}) custom-call(f32[160,1280]{1,0:T(8,128)} %get-tuple-element.48.own, bf16[160,1280]{1,0:T(8,128)(2,1)} %copy-done.3, bf16[160,1280]{1,0:T(8,128)(2,1)} %copy-done.5, bf16[160,1280]{1,0:T(8,128)(2,1)} %copy-done.7), custom_call_target="tpu_custom_call" | custom-call | bytes 2560000 | tf_op jit(solution)/shard_map/global_sum_x/pallas_call | solution.py:52
  154.5 2.4 %collective-permute-start.14 = (bf16[40,1280]{1,0:T(8,128)(2,1)}, bf16[40,1280]{1,0:T(8,128)(2,1)S(1)}, u32[]{:S(2)}, u32[]{:S(2)}) collective-permute-start(bf16[40,1280]{1,0:T(8,128)(2,1)} %get-tuple-element.54), channel_id=1, source_target_pairs={{0,4},{1,5},{2,6},{3,7},{4,0},{5,1},{6,2},{7,3},{8,12},{9,13},{10,... | collective-permute-start | bytes 307208 | tf_op jit(solution)/shard_map/ppermute | solution.py:296
  158.7 1.8 local_sum_y.1.local
  161.9 1.9 join.1
  163.8 2.6 %collective-permute-start.16 = (bf16[24,1280]{1,0:T(8,128)(2,1)}, bf16[24,1280]{1,0:T(8,128)(2,1)S(1)}, u32[]{:S(2)}, u32[]{:S(2)}) collective-permute-start(bf16[24,1280]{1,0:T(8,128)(2,1)} %get-tuple-element.57), channel_id=1, source_target_pairs={{0,8},{1,9},{2,10},{3,11},{4,12},{5,13},{6,14},{7,15},{8,16},{9,17... | collective-permute-start | bytes 184328 | tf_op jit(solution)/shard_map/ppermute | solution.py:296
  166.5 3.3 %collective-permute-start.17 = (bf16[24,1280]{1,0:T(8,128)(2,1)}, bf16[24,1280]{1,0:T(8,128)(2,1)S(1)}, u32[]{:S(2)}, u32[]{:S(2)}) collective-permute-start(bf16[24,1280]{1,0:T(8,128)(2,1)} %get-tuple-element.58), channel_id=1, source_target_pairs={{0,16},{1,17},{2,18},{3,19},{4,20},{5,21},{6,22},{7,23},{8,24},{9,... | collective-permute-start | bytes 184328 | tf_op jit(solution)/shard_map/ppermute | solution.py:296
  169.8 3.3 %collective-permute-start.18 = (bf16[24,1280]{1,0:T(8,128)(2,1)}, bf16[24,1280]{1,0:T(8,128)(2,1)S(1)}, u32[]{:S(2)}, u32[]{:S(2)}) collective-permute-start(bf16[24,1280]{1,0:T(8,128)(2,1)} %get-tuple-element.59), channel_id=1, source_target_pairs={{0,24},{1,25},{2,26},{3,27},{4,28},{5,29},{6,30},{7,31},{8,0},{9,1... | collective-permute-start | bytes 184328 | tf_op jit(solution)/shard_map/ppermute | solution.py:296
  174.4 2.0 collective-permute-done.18.c
  177.0 1.6 sum_z.1.refs_0_
  178.6 3.3 %collective-permute-start.25 = (f32[24,1280]{1,0:T(8,128)}, f32[24,1280]{1,0:T(8,128)S(1)}, u32[]{:S(2)}, u32[]{:S(2)}) collective-permute-start(f32[24,1280]{1,0:T(8,128)} %sum_z.1.refs_0_), channel_id=1, source_target_pairs={{0,224},{32,128},{64,160},{96,192},{128,96},{160,0},{192,32},{224,... | collective-permute-start | bytes 368648 | tf_op jit(solution)/shard_map/ppermute | solution.py:286
  182.8 2.7 %collective-permute-start.22 = (f32[24,1280]{1,0:T(8,128)}, f32[24,1280]{1,0:T(8,128)S(1)}, u32[]{:S(2)}, u32[]{:S(2)}) collective-permute-start(f32[24,1280]{1,0:T(8,128)} %sum_z.1.refs_0_), channel_id=1, source_target_pairs={{0,64},{32,96},{64,0},{96,32},{128,192},{160,224},{192,128},{224,1... | collective-permute-start | bytes 368648 | tf_op jit(solution)/shard_map/ppermute | solution.py:286
  185.5 1.7 collective-permute-start.21
  187.2 3.4 %collective-permute-done.24.refs_6_ = f32[24,1280]{1,0:T(8,128)S(1)} collective-permute-done((f32[24,1280]{1,0:T(8,128)}, f32[24,1280]{1,0:T(8,128)S(1)}, u32[]{:S(2)}, u32[]{:S(2)}) %collective-permute-start.24) | collective-permute-done | bytes 122912 | tf_op jit(solution)/shard_map/ppermute | solution.py:286
  191.7 1.7 collective-permute-done.22.refs_4_
  193.4 4.3 %collective-permute-done.20.refs_2_ = f32[24,1280]{1,0:T(8,128)S(1)} collective-permute-done((f32[24,1280]{1,0:T(8,128)}, f32[24,1280]{1,0:T(8,128)S(1)}, u32[]{:S(2)}, u32[]{:S(2)}) %collective-permute-start.20) | collective-permute-done | bytes 122912 | tf_op jit(solution)/shard_map/ppermute | solution.py:286
  198.9 2.2 %final.1 = (f32[40,1280]{1,0:T(8,128)}, f32[40,1280]{1,0:T(8,128)}) custom-call(s32[4]{0:T(128)} %pad_add_fusion.place, f32[24,1280]{1,0:T(8,128)} %sum_z.1.refs_0_, f32[24,1280]{1,0:T(8,128)} %copy-done.15, f32[24,1280]{1,0:T(8,128)} %copy-done.14, f32[24,1280]{1,0:T(8,128)} %copy-done.13, f32[24,1280]{1,0:T(8,128)} %copy-done.12, f32[24,1280]{1,0:T(8,128)} %copy-done.11, ...), custom_call_target="tpu_custom_call" | custom-call | bytes 1392656 | tf_op jit(solution)/shard_map/final/pallas_call | solution.py:52
  202.3 3.5 %unpack.1 = bf16[2,96,3840]{2,1,0:T(8,128)(2,1)} custom-call(bf16[768,1024]{1,0:T(8,128)(2,1)} %bitcast.16, bf16[384,384]{1,0:T(8,128)(2,1)} %constant.61.clone.order), custom_call_target="tpu_custom_call" | custom-call | bytes 3342336 | tf_op jit(solution)/shard_map/unpack/pallas_call | solution.py:52
  (99 shorter events, 27.2 us)
Async XLA Ops:
  4.7 59.5 %all-to-all-start = ((bf16[32,24,1280]{2,1,0:T(8,128)(2,1)}), bf16[32,24,1280]{2,1,0:T(8,128)(2,1)S(1)}, u32[]{:S(2)}, u32[]{:S(2)}) async-start(bf16[32,24,1280]{2,1,0:T(8,128)(2,1)} %bitcast.15), calls=%async_computation | async-start | bytes 3932160 | tf_op jit(solution)/shard_map/all_to_all | solution.py:303
  83.1 118.1 %all-to-all-start.1 = ((bf16[32,24,1024]{2,1,0:T(8,128)(2,1)}), bf16[32,24,1024]{2,1,0:T(8,128)(2,1)S(1)}, u32[]{:S(2)}, u32[]{:S(2)}) async-start(bf16[32,24,1024]{2,1,0:T(8,128)(2,1)} %bitcast.18), calls=%async_computation.1 | async-start | bytes 3145728 | tf_op jit(solution)/shard_map/all_to_all | solution.py:303
  90.7 14.7 %collective-permute-start.1 = (bf16[192,1280]{1,0:T(8,128)(2,1)S(1)}, bf16[192,1280]{1,0:T(8,128)(2,1)S(1)}, u32[]{:S(2)}, u32[]{:S(2)}) collective-permute-start(bf16[192,1280]{1,0:T(8,128)(2,1)S(1)} %bitcast.24), channel_id=1, source_target_pairs={{0,1},{1,0},{2,3},{3,2},{4,5},{5,4},{6,7},{7,6},{8,9},{9,8},{10,11... | collective-permute-start | bytes 1474568 | tf_op jit(solution)/shard_map/ppermute | solution.py:279
  91.2 12.8 %copy-start.25 = (bf16[192,1280]{1,0:T(8,128)(2,1)S(1)}, bf16[192,1280]{1,0:T(8,128)(2,1)}, u32[]{:S(2)}) copy-start(bf16[192,1280]{1,0:T(8,128)(2,1)} %get-tuple-element.47.cot) | copy-start | bytes 1474564
  103.7 1.7 collective-permute-start
  103.9 11.5 %collective-permute-start.9 = (bf16[192,1280]{1,0:T(8,128)(2,1)S(1)}, bf16[192,1280]{1,0:T(8,128)(2,1)S(1)}, u32[]{:S(2)}, u32[]{:S(2)}) collective-permute-start(bf16[192,1280]{1,0:T(8,128)(2,1)S(1)} %copy-done.25), channel_id=1, source_target_pairs={{0,1},{1,0},{2,3},{3,2},{4,5},{5,4},{6,7},{7,6},{8,9},{9,8},{10,11... | collective-permute-start | bytes 1474568 | tf_op jit(solution)/shard_map/ppermute | solution.py:279
  109.9 12.2 %collective-permute-start.2 = (bf16[160,1280]{1,0:T(8,128)(2,1)}, bf16[160,1280]{1,0:T(8,128)(2,1)S(1)}, u32[]{:S(2)}, u32[]{:S(2)}) collective-permute-start(bf16[160,1280]{1,0:T(8,128)(2,1)} %get-tuple-element.38), channel_id=1, source_target_pairs={{0,32},{32,64},{64,96},{96,0},{128,160},{160,192},{192,224},{224,1... | collective-permute-start | bytes 1228808 | tf_op jit(solution)/shard_map/ppermute | solution.py:286
  110.9 4.5 %collective-permute-start.8 = (bf16[192,640]{1,0:T(8,128)(2,1)S(1)}, bf16[192,640]{1,0:T(8,128)(2,1)S(1)}, u32[]{:S(2)}, u32[]{:S(2)}) collective-permute-start(bf16[192,640]{1,0:T(8,128)(2,1)S(1)} %copy-done.28), channel_id=1, source_target_pairs={{0,1},{1,0},{2,3},{3,2},{4,5},{5,4},{6,7},{7,6},{8,9},{9,8},{10,11... | collective-permute-start | bytes 737288 | tf_op jit(solution)/shard_map/ppermute | solution.py:279
  111.4 20.3 %collective-permute-start.3 = (bf16[160,1280]{1,0:T(8,128)(2,1)}, bf16[160,1280]{1,0:T(8,128)(2,1)S(1)}, u32[]{:S(2)}, u32[]{:S(2)}) collective-permute-start(bf16[160,1280]{1,0:T(8,128)(2,1)} %get-tuple-element.39), channel_id=1, source_target_pairs={{0,64},{32,96},{64,0},{96,32},{128,192},{160,224},{192,128},{224,1... | collective-permute-start | bytes 1228808 | tf_op jit(solution)/shard_map/ppermute | solution.py:286
  114.0 18.5 %collective-permute-start.4 = (bf16[160,1280]{1,0:T(8,128)(2,1)}, bf16[160,1280]{1,0:T(8,128)(2,1)S(1)}, u32[]{:S(2)}, u32[]{:S(2)}) collective-permute-start(bf16[160,1280]{1,0:T(8,128)(2,1)} %get-tuple-element.40), channel_id=1, source_target_pairs={{0,96},{32,0},{64,32},{96,64},{128,224},{160,128},{192,160},{224,1... | collective-permute-start | bytes 1228808 | tf_op jit(solution)/shard_map/ppermute | solution.py:286
  120.0 21.2 %collective-permute-start.10 = (bf16[160,1280]{1,0:T(8,128)(2,1)}, bf16[160,1280]{1,0:T(8,128)(2,1)S(1)}, u32[]{:S(2)}, u32[]{:S(2)}) collective-permute-start(bf16[160,1280]{1,0:T(8,128)(2,1)} %get-tuple-element.49), channel_id=1, source_target_pairs={{0,32},{32,64},{64,96},{96,0},{128,160},{160,192},{192,224},{224,1... | collective-permute-start | bytes 1228808 | tf_op jit(solution)/shard_map/ppermute | solution.py:286
  120.0 29.3 %collective-permute-start.11 = (bf16[160,1280]{1,0:T(8,128)(2,1)}, bf16[160,1280]{1,0:T(8,128)(2,1)S(1)}, u32[]{:S(2)}, u32[]{:S(2)}) collective-permute-start(bf16[160,1280]{1,0:T(8,128)(2,1)} %get-tuple-element.50), channel_id=1, source_target_pairs={{0,64},{32,96},{64,0},{96,32},{128,192},{160,224},{192,128},{224,1... | collective-permute-start | bytes 1228808 | tf_op jit(solution)/shard_map/ppermute | solution.py:286
  122.1 10.3 %copy-start.4 = (bf16[160,1280]{1,0:T(8,128)(2,1)}, bf16[160,1280]{1,0:T(8,128)(2,1)S(1)}, u32[]{:S(2)}) copy-start(bf16[160,1280]{1,0:T(8,128)(2,1)S(1)} %collective-permute-done.2.a) | copy-start | bytes 1228804
  122.1 27.9 %collective-permute-start.12 = (bf16[160,1280]{1,0:T(8,128)(2,1)}, bf16[160,1280]{1,0:T(8,128)(2,1)S(1)}, u32[]{:S(2)}, u32[]{:S(2)}) collective-permute-start(bf16[160,1280]{1,0:T(8,128)(2,1)} %get-tuple-element.51), channel_id=1, source_target_pairs={{0,96},{32,0},{64,32},{96,64},{128,224},{160,128},{192,160},{224,1... | collective-permute-start | bytes 1228808 | tf_op jit(solution)/shard_map/ppermute | solution.py:286
  135.5 21.4 %collective-permute-start.5 = (bf16[40,1280]{1,0:T(8,128)(2,1)}, bf16[40,1280]{1,0:T(8,128)(2,1)S(1)}, u32[]{:S(2)}, u32[]{:S(2)}) collective-permute-start(bf16[40,1280]{1,0:T(8,128)(2,1)} %get-tuple-element.42), channel_id=1, source_target_pairs={{0,2},{1,3},{2,4},{3,5},{4,6},{5,7},{6,0},{7,1},{8,10},{9,11},{10,... | collective-permute-start | bytes 307208 | tf_op jit(solution)/shard_map/ppermute | solution.py:296
  136.8 21.2 %collective-permute-start.6 = (bf16[40,1280]{1,0:T(8,128)(2,1)}, bf16[40,1280]{1,0:T(8,128)(2,1)S(1)}, u32[]{:S(2)}, u32[]{:S(2)}) collective-permute-start(bf16[40,1280]{1,0:T(8,128)(2,1)} %get-tuple-element.43), channel_id=1, source_target_pairs={{0,4},{1,5},{2,6},{3,7},{4,0},{5,1},{6,2},{7,3},{8,12},{9,13},{10,... | collective-permute-start | bytes 307208 | tf_op jit(solution)/shard_map/ppermute | solution.py:296
  141.1 8.9 %copy-start.3 = (bf16[160,1280]{1,0:T(8,128)(2,1)}, bf16[160,1280]{1,0:T(8,128)(2,1)S(1)}, u32[]{:S(2)}) copy-start(bf16[160,1280]{1,0:T(8,128)(2,1)S(1)} %collective-permute-done.10.a) | copy-start | bytes 1228804
  141.1 16.9 %collective-permute-start.7 = (bf16[40,1280]{1,0:T(8,128)(2,1)}, bf16[40,1280]{1,0:T(8,128)(2,1)S(1)}, u32[]{:S(2)}, u32[]{:S(2)}) collective-permute-start(bf16[40,1280]{1,0:T(8,128)(2,1)} %get-tuple-element.44), channel_id=1, source_target_pairs={{0,6},{1,7},{2,0},{3,1},{4,2},{5,3},{6,4},{7,5},{8,14},{9,15},{10,... | collective-permute-start | bytes 307208 | tf_op jit(solution)/shard_map/ppermute | solution.py:296
  153.1 7.4 %collective-permute-start.13 = (bf16[40,1280]{1,0:T(8,128)(2,1)}, bf16[40,1280]{1,0:T(8,128)(2,1)S(1)}, u32[]{:S(2)}, u32[]{:S(2)}) collective-permute-start(bf16[40,1280]{1,0:T(8,128)(2,1)} %get-tuple-element.53), channel_id=1, source_target_pairs={{0,2},{1,3},{2,4},{3,5},{4,6},{5,7},{6,0},{7,1},{8,10},{9,11},{10,... | collective-permute-start | bytes 307208 | tf_op jit(solution)/shard_map/ppermute | solution.py:296
  154.5 6.6 %collective-permute-start.14 = (bf16[40,1280]{1,0:T(8,128)(2,1)}, bf16[40,1280]{1,0:T(8,128)(2,1)S(1)}, u32[]{:S(2)}, u32[]{:S(2)}) collective-permute-start(bf16[40,1280]{1,0:T(8,128)(2,1)} %get-tuple-element.54), channel_id=1, source_target_pairs={{0,4},{1,5},{2,6},{3,7},{4,0},{5,1},{6,2},{7,3},{8,12},{9,13},{10,... | collective-permute-start | bytes 307208 | tf_op jit(solution)/shard_map/ppermute | solution.py:296
  156.9 4.4 %collective-permute-start.15 = (bf16[40,1280]{1,0:T(8,128)(2,1)}, bf16[40,1280]{1,0:T(8,128)(2,1)S(1)}, u32[]{:S(2)}, u32[]{:S(2)}) collective-permute-start(bf16[40,1280]{1,0:T(8,128)(2,1)} %get-tuple-element.55), channel_id=1, source_target_pairs={{0,6},{1,7},{2,0},{3,1},{4,2},{5,3},{6,4},{7,5},{8,14},{9,15},{10,... | collective-permute-start | bytes 307208 | tf_op jit(solution)/shard_map/ppermute | solution.py:296
  163.8 9.2 %collective-permute-start.16 = (bf16[24,1280]{1,0:T(8,128)(2,1)}, bf16[24,1280]{1,0:T(8,128)(2,1)S(1)}, u32[]{:S(2)}, u32[]{:S(2)}) collective-permute-start(bf16[24,1280]{1,0:T(8,128)(2,1)} %get-tuple-element.57), channel_id=1, source_target_pairs={{0,8},{1,9},{2,10},{3,11},{4,12},{5,13},{6,14},{7,15},{8,16},{9,17... | collective-permute-start | bytes 184328 | tf_op jit(solution)/shard_map/ppermute | solution.py:296
  166.5 7.9 %collective-permute-start.17 = (bf16[24,1280]{1,0:T(8,128)(2,1)}, bf16[24,1280]{1,0:T(8,128)(2,1)S(1)}, u32[]{:S(2)}, u32[]{:S(2)}) collective-permute-start(bf16[24,1280]{1,0:T(8,128)(2,1)} %get-tuple-element.58), channel_id=1, source_target_pairs={{0,16},{1,17},{2,18},{3,19},{4,20},{5,21},{6,22},{7,23},{8,24},{9,... | collective-permute-start | bytes 184328 | tf_op jit(solution)/shard_map/ppermute | solution.py:296
  169.8 6.6 %collective-permute-start.18 = (bf16[24,1280]{1,0:T(8,128)(2,1)}, bf16[24,1280]{1,0:T(8,128)(2,1)S(1)}, u32[]{:S(2)}, u32[]{:S(2)}) collective-permute-start(bf16[24,1280]{1,0:T(8,128)(2,1)} %get-tuple-element.59), channel_id=1, source_target_pairs={{0,24},{1,25},{2,26},{3,27},{4,28},{5,29},{6,30},{7,31},{8,0},{9,1... | collective-permute-start | bytes 184328 | tf_op jit(solution)/shard_map/ppermute | solution.py:296
  178.6 8.6 %collective-permute-start.25 = (f32[24,1280]{1,0:T(8,128)}, f32[24,1280]{1,0:T(8,128)S(1)}, u32[]{:S(2)}, u32[]{:S(2)}) collective-permute-start(f32[24,1280]{1,0:T(8,128)} %sum_z.1.refs_0_), channel_id=1, source_target_pairs={{0,224},{32,128},{64,160},{96,192},{128,96},{160,0},{192,32},{224,... | collective-permute-start | bytes 368648 | tf_op jit(solution)/shard_map/ppermute | solution.py:286
  181.9 8.7 %collective-permute-start.24 = (f32[24,1280]{1,0:T(8,128)}, f32[24,1280]{1,0:T(8,128)S(1)}, u32[]{:S(2)}, u32[]{:S(2)}) collective-permute-start(f32[24,1280]{1,0:T(8,128)} %sum_z.1.refs_0_), channel_id=1, source_target_pairs={{0,96},{32,0},{64,32},{96,64},{128,224},{160,128},{192,160},{224,1... | collective-permute-start | bytes 368648 | tf_op jit(solution)/shard_map/ppermute | solution.py:286
  182.1 9.6 %collective-permute-start.23 = (f32[24,1280]{1,0:T(8,128)}, f32[24,1280]{1,0:T(8,128)S(1)}, u32[]{:S(2)}, u32[]{:S(2)}) collective-permute-start(f32[24,1280]{1,0:T(8,128)} %sum_z.1.refs_0_), channel_id=1, source_target_pairs={{0,192},{32,224},{64,128},{96,160},{128,64},{160,96},{192,0},{224,... | collective-permute-start | bytes 368648 | tf_op jit(solution)/shard_map/ppermute | solution.py:286
  182.8 10.6 %collective-permute-start.22 = (f32[24,1280]{1,0:T(8,128)}, f32[24,1280]{1,0:T(8,128)S(1)}, u32[]{:S(2)}, u32[]{:S(2)}) collective-permute-start(f32[24,1280]{1,0:T(8,128)} %sum_z.1.refs_0_), channel_id=1, source_target_pairs={{0,64},{32,96},{64,0},{96,32},{128,192},{160,224},{192,128},{224,1... | collective-permute-start | bytes 368648 | tf_op jit(solution)/shard_map/ppermute | solution.py:286
  185.5 7.8 %collective-permute-start.21 = (f32[24,1280]{1,0:T(8,128)}, f32[24,1280]{1,0:T(8,128)S(1)}, u32[]{:S(2)}, u32[]{:S(2)}) collective-permute-start(f32[24,1280]{1,0:T(8,128)} %sum_z.1.refs_0_), channel_id=1, source_target_pairs={{0,160},{32,192},{64,224},{96,128},{128,32},{160,64},{192,96},{224... | collective-permute-start | bytes 368648 | tf_op jit(solution)/shard_map/ppermute | solution.py:286
  187.2 10.4 %copy-start.9 = (f32[24,1280]{1,0:T(8,128)}, f32[24,1280]{1,0:T(8,128)S(1)}, u32[]{:S(2)}) copy-start(f32[24,1280]{1,0:T(8,128)S(1)} %collective-permute-done.25.refs_7_) | copy-start | bytes 368644
  187.2 10.4 %collective-permute-start.20 = (f32[24,1280]{1,0:T(8,128)}, f32[24,1280]{1,0:T(8,128)S(1)}, u32[]{:S(2)}, u32[]{:S(2)}) collective-permute-start(f32[24,1280]{1,0:T(8,128)} %sum_z.1.refs_0_), channel_id=1, source_target_pairs={{0,32},{32,64},{64,96},{96,0},{128,160},{160,192},{192,224},{224,1... | collective-permute-start | bytes 368648 | tf_op jit(solution)/shard_map/ppermute | solution.py:286
  190.6 7.0 %collective-permute-start.19 = (f32[24,1280]{1,0:T(8,128)}, f32[24,1280]{1,0:T(8,128)S(1)}, u32[]{:S(2)}, u32[]{:S(2)}) collective-permute-start(f32[24,1280]{1,0:T(8,128)} %sum_z.1.refs_0_), channel_id=1, source_target_pairs={{0,128},{32,160},{64,192},{96,224},{128,0},{160,32},{192,64},{224,... | collective-permute-start | bytes 368648 | tf_op jit(solution)/shard_map/ppermute | solution.py:286
  (27 other events, 57.0 us)

commit v2 on v1

--- a/solution.py
+++ b/solution.py
@@ -42,9 +42,11 @@
 GROUP = order_matrix([("p", 16), ("s", 4), ("w", 2), ("t", 3)], ["s", "t", "p", "w"])
 
 
-def call(kernel, outs, *args, smem=(), scratch=(), flops=0, name=None):
+def call(kernel, outs, *args, smem=(), unread=(), scratch=(), flops=0, name=None):
     specs = [
-        pl.BlockSpec(memory_space=pltpu.SMEM if i in smem else pltpu.VMEM)
+        pl.BlockSpec(
+            memory_space=pltpu.SMEM if i in smem else pl.ANY if i in unread else pltpu.VMEM
+        )
         for i in range(len(args))
     ]
     size = sum(int(np.prod(a.shape)) * a.dtype.itemsize for a in args)
@@ -187,7 +189,7 @@
     act_other[...] = ordered[:, 640:]
 
 
-def global_kernel(place, got, weight, order, back, act_own, act_other, cot, data, grads, act_all):
+def global_kernel(place, after, got, weight, order, back, act_own, act_other, cot, data, grads, act_all):
     masks = head_masks()
     hot = order[...]
     for c in range(2):
@@ -255,20 +257,17 @@
 
 
 def sum_z_kernel(own, a, b, c, total):
-    total[...] = own[...] + a[...].astype(F32) + b[...].astype(F32) + c[...].astype(F32)
-
-
-def final_kernel(scale, place, *refs):
-    pieces, (local, glob) = refs[:8], refs[8:]
-    x = place[0]
-    sums = [(pieces[2 * d][...] + pieces[2 * d + 1][...]) * scale for d in range(4)]
-    for p in range(4):
-        d = (x - p) & 3
-        chosen = jnp.where(
-            d == 0, sums[0], jnp.where(d == 1, sums[1], jnp.where(d == 2, sums[2], sums[3]))
-        )
-        local[10 * p : 10 * p + 10, :] = chosen[:10]
-        glob[10 * p : 10 * p + 10, :] = chosen[10:20]
+    one = own[...] + a[...].astype(F32) + b[...].astype(F32) + c[...].astype(F32)
+    one = one.astype(BF16)
+    for i in range(8):
+        total[i] = one
+
+
+def final_kernel(scale, pieces, local, glob):
+    for x in range(4):
+        both = (pieces[x].astype(F32) + pieces[4 + x].astype(F32)) * scale
+        local[10 * x : 10 * x + 10, :] = both[:10]
+        glob[10 * x : 10 * x + 10, :] = both[10:20]
 
 
 def chip(z, y, c):
@@ -279,10 +278,8 @@
     return lax.ppermute(a, "tok", [(i, i ^ 1) for i in range(32)])
 
 
-def along_x(a, d, flip=0):
-    pairs = [
-        (z * 4 + x, (z ^ flip) * 4 + (x + d) % 4) for z in range(2) for x in range(4)
-    ]
+def along_x(a, d):
+    pairs = [(z * 4 + x, z * 4 + (x + d) % 4) for z in range(2) for x in range(4)]
     return lax.ppermute(a, "dp", pairs)
 
 
@@ -328,7 +325,11 @@
         c,
         name=name + "_sum_x",
     )
-    return own, along_tok(one, 0, 1), along_tok(two, 0, 2), along_tok(three, 0, 3)
+    return own, one, two, three
+
+
+def along_y(one, two, three):
+    return along_tok(one, 0, 1), along_tok(two, 0, 2), along_tok(three, 0, 3)
 
 
 def per_device(qkv_local, qkv_global, positions, slopes, cotangent, w_out_local, w_out_global):
@@ -362,8 +363,11 @@
         flops=2 * 10**9,
         name="local",
     )
-    own, a, b, c = weight_sums(act_own, act_other, cotangent.reshape(192, 1280), "local")
-    (sum_local,) = call(sum_y_kernel, [sds((40, 1280), F32)], own, a, b, c, name="local_sum_y")
+    first_own, *others = weight_sums(act_own, act_other, cotangent.reshape(192, 1280), "local")
+    a, b, c = along_y(*others)
+    (sum_local,) = call(
+        sum_y_kernel, [sds((40, 1280), F32)], first_own, a, b, c, name="local_sum_y"
+    )
 
     back, act_own, act_other, cot = call(
         global_kernel,
@@ -374,10 +378,12 @@
             sds((192, 1280), BF16),
         ],
         place,
+        first_own,
         got,
         w_out_global,
         group,
         smem=(0,),
+        unread=(1,),
         scratch=[
             pltpu.VMEM((3, 192, 1280), BF16),
             pltpu.VMEM((192, 4096), BF16),
@@ -387,7 +393,8 @@
         name="global",
     )
     returned = exchange(back)
-    own, a, b, c = weight_sums(act_own, act_other, cot, "global")
+    own, *others = weight_sums(act_own, act_other, cot, "global")
+    a, b, c = along_y(*others)
     own, one, two, three = call(
         join_kernel,
         [sds((24, 1280), F32)] + [sds((24, 1280), BF16)] * 3,
@@ -399,18 +406,12 @@
         name="join",
     )
     a, b, c = along_tok(one, 1, 0), along_tok(two, 2, 0), along_tok(three, 3, 0)
-    (mine,) = call(sum_z_kernel, [sds((24, 1280), F32)], own, a, b, c, name="sum_z")
-    pieces = [
-        mine if d == 0 and flip == 0 else along_x(mine, d, flip)
-        for d in range(4)
-        for flip in range(2)
-    ]
+    (mine,) = call(sum_z_kernel, [sds((8, 24, 1280), BF16)], own, a, b, c, name="sum_z")
+    pieces = lax.all_to_all(mine, "dp", split_axis=0, concat_axis=0, tiled=True)
     grad_local, grad_global = call(
         functools.partial(final_kernel, scale),
         [sds((40, 1280), F32), sds((40, 1280), F32)],
-        place,
-        *pieces,
-        smem=(0,),
+        pieces,
         name="final",
     )
     (d_global,) = call(

time: 206 us -> 211 us (1.024)
  blocking collectives: 0 us -> 14.3 us
  starting transfers between devices: 59.1 us -> 46.1 us
  waiting for transfers between devices: 79.1 us -> 83 us
    all_to_all x0 -> x1, blocking collectives: none -> 14.3 us  [per_device(): pieces = lax.all_to_all(mine, 'dp', split_axis=0, concat_axis=0, tiled=True)]
    ppermute x9, starting transfers between devices: 20.4 us -> 7.68 us  [along_tok(): return lax.ppermute(a, 'tok', pairs)]
    ppermute x13 -> x6, starting transfers between devices: 16.8 us -> 9.59 us  [along_x(): return lax.ppermute(a, 'dp', pairs)]
    ppermute x13 -> x6, waiting for transfers between devices: 27.7 us -> 33.7 us  [along_x(): return lax.ppermute(a, 'dp', pairs)]
    all_to_all x2, waiting for transfers between devices: 46.1 us -> 40.9 us  [exchange(): lax.all_to_all(a, 'tok', split_axis=0, concat_axis=0, axis_index_groups=T...]
    all_to_all x2, starting transfers between devices: 20.3 us -> 24.7 us  [exchange(): lax.all_to_all(a, 'tok', split_axis=0, concat_axis=0, axis_index_groups=T...]
    ppermute x4, starting transfers between devices: 1.57 us -> 4.06 us  [swap_cores(): return lax.ppermute(a, 'tok', [(i, i ^ 1) for i in range(32)])]
    ppermute x4, waiting for transfers between devices: 1.22 us -> 3.39 us  [swap_cores(): return lax.ppermute(a, 'tok', [(i, i ^ 1) for i in range(32)])]
  transfers between devices with their start and end apart: 28 -> 21, of which waited for: 15 -> 12; matrix products, arithmetic and copies ran while one was open for 0% -> 0% of each run, Pallas kernels for 16% -> 12%
where the time goes in v2:
time: 211 us; the launch traced here: 210 us
  waiting for transfers between devices  83 us (39%)
  Pallas kernels  57 us (27%)
  starting transfers between devices  46.1 us (22%)
  blocking collectives  14.3 us (7%)
  local copies, waits for them, and re-layouts  8.67 us (4%)
    pallas_call x12, Pallas kernels, call(): pl.pallas_call(kernel, out_shape=outs, in_specs=specs, out_specs=[pl.Bloc...  57 us
    all_to_all x2, waiting for transfers between devices, exchange(): lax.all_to_all(a, 'tok', split_axis=0, concat_axis=0, axis_index_groups=T...  40.9 us
    ppermute x6, waiting for transfers between devices, along_x(): return lax.ppermute(a, 'dp', pairs)  33.7 us
    all_to_all x2, starting transfers between devices, exchange(): lax.all_to_all(a, 'tok', split_axis=0, concat_axis=0, axis_index_groups=T...  24.7 us
    all_to_all x1, blocking collectives, per_device(): pieces = lax.all_to_all(mine, 'dp', split_axis=0, concat_axis=0, tiled=True)  14.3 us
    ppermute x6, starting transfers between devices, along_x(): return lax.ppermute(a, 'dp', pairs)  9.59 us
    unnamed x50, local copies, waits for them, and re-layouts  8.67 us
    ppermute x9, starting transfers between devices, along_tok(): return lax.ppermute(a, 'tok', pairs)  7.68 us
  transfers between devices with their start and end apart: 21, of which 12 were waited for; matrix products, arithmetic and copies ran while one was open for 0% of the time, Pallas kernels for 12%

profile of v2, /device:TPU:1, one launch (start us, length us, event | category | flops | bytes accessed | tf_op | source)
XLA Modules:
  0.0 210.5 jit_solution(2344597247024697502)
XLA Ops:
  0.6 4.0 %pack.1 = bf16[768,1280]{1,0:T(8,128)(2,1)} custom-call(bf16[2,96,3840]{2,1,0:T(8,128)(2,1)} %bitcast.18, bf16[2,96,1280]{2,1,0:T(8,128)(2,1)} %bitcast.20, bf16[384,384]{1,0:T(8,128)(2,1)} %constant.61.clone.order), custom_call_target="tpu_custom_call" | custom-call | bytes 4227072 | tf_op jit(solution)/shard_map/pack/pallas_call | solution.py:54
  4.7 12.9 %all-to-all-start = ((bf16[32,24,1280]{2,1,0:T(8,128)(2,1)}), bf16[32,24,1280]{2,1,0:T(8,128)(2,1)S(1)}, u32[]{:S(2)}, u32[]{:S(2)}) async-start(bf16[32,24,1280]{2,1,0:T(8,128)(2,1)} %bitcast.15), calls=%async_computation | async-start | bytes 3932160 | tf_op jit(solution)/shard_map/all_to_all | solution.py:300
  18.6 12.4 %local.1 = (bf16[2,96,3840]{2,1,0:T(8,128)(2,1)}, bf16[192,640]{1,0:T(8,128)(2,1)}, bf16[192,640]{1,0:T(8,128)(2,1)}) custom-call(s32[4]{0:T(128)} %pad_add_fusion.place, f32[8]{0:T(128)} %slopes.1, bf16[2,96,3840]{2,1,0:T(8,128)(2,1)} %bitcast.24, bf16[2,96,1280]{2,1,0:T(8,128)(2,1)} %bitcast.21, bf16[1280,1280]{1,0:T(8,128)(2,1)} %weight.2, s32[2,96]{1,0:T(2,128)} %bitcast.25), custom_call_target="tpu_custom_call" | custom-call | flops 2000000000 | bytes 7209776 | tf_op jit(solution)/shard_map/local/pallas_call | solution.py:54
  31.3 1.4 collective-permute-done.act_far
  33.6 3.7 %local_weight.1 = (f32[160,1280]{1,0:T(8,128)}, bf16[160,1280]{1,0:T(8,128)(2,1)}, bf16[160,1280]{1,0:T(8,128)(2,1)}, bf16[160,1280]{1,0:T(8,128)(2,1)}) custom-call(bf16[192,640]{1,0:T(8,128)(2,1)} %get-tuple-element.34.act, bf16[192,640]{1,0:T(8,128)(2,1)} %copy-done.21, bf16[192,1280]{1,0:T(8,128)(2,1)} %bitcast.22, bf16[192,1280]{1,0:T(8,128)(2,1)} %copy-done.18), custom_call_target="tpu_custom_call" | custom-call | flops 629145600 | bytes 3522560 | tf_op jit(solution)/shard_map/local_weight/pallas_call | solution.py:54
  38.5 2.4 %collective-permute-start.3 = (bf16[160,1280]{1,0:T(8,128)(2,1)}, bf16[160,1280]{1,0:T(8,128)(2,1)S(1)}, u32[]{:S(2)}, u32[]{:S(2)}) collective-permute-start(bf16[160,1280]{1,0:T(8,128)(2,1)} %get-tuple-element.38), channel_id=1, source_target_pairs={{0,64},{32,96},{64,0},{96,32},{128,192},{160,224},{192,128},{224,1... | collective-permute-start | bytes 1228808 | tf_op jit(solution)/shard_map/ppermute | solution.py:283
  42.1 7.4 %collective-permute-done.2.a = bf16[160,1280]{1,0:T(8,128)(2,1)S(1)} collective-permute-done((bf16[160,1280]{1,0:T(8,128)(2,1)}, bf16[160,1280]{1,0:T(8,128)(2,1)S(1)}, u32[]{:S(2)}, u32[]{:S(2)}) %collective-permute-start.2) | collective-permute-done | bytes 409632 | tf_op jit(solution)/shard_map/ppermute | solution.py:283
  49.5 9.8 %collective-permute-done.3.b = bf16[160,1280]{1,0:T(8,128)(2,1)S(1)} collective-permute-done((bf16[160,1280]{1,0:T(8,128)(2,1)}, bf16[160,1280]{1,0:T(8,128)(2,1)S(1)}, u32[]{:S(2)}, u32[]{:S(2)}) %collective-permute-start.3) | collective-permute-done | bytes 409632 | tf_op jit(solution)/shard_map/ppermute | solution.py:283
  60.1 2.3 %local_sum_x.1 = (f32[40,1280]{1,0:T(8,128)}, bf16[40,1280]{1,0:T(8,128)(2,1)}, bf16[40,1280]{1,0:T(8,128)(2,1)}, bf16[40,1280]{1,0:T(8,128)(2,1)}) custom-call(f32[160,1280]{1,0:T(8,128)} %get-tuple-element.36.own, bf16[160,1280]{1,0:T(8,128)(2,1)} %copy-done.6, bf16[160,1280]{1,0:T(8,128)(2,1)} %copy-done.7, bf16[160,1280]{1,0:T(8,128)(2,1)} %copy-done.8), custom_call_target="tpu_custom_call" | custom-call | bytes 2560000 | tf_op jit(solution)/shard_map/local_sum_x/pallas_call | solution.py:54
  62.4 1.9 all-to-all-done
  65.6 17.6 %global.1 = (bf16[768,1024]{1,0:T(8,128)(2,1)}, bf16[192,640]{1,0:T(8,128)(2,1)}, bf16[192,640]{1,0:T(8,128)(2,1)}, bf16[192,1280]{1,0:T(8,128)(2,1)}) custom-call(s32[4]{0:T(128)} %pad_add_fusion.place, f32[40,1280]{1,0:T(8,128)} %get-tuple-element.40.after.own, bf16[768,1280]{1,0:T(8,128)(2,1)} %bitcast.17, bf16[1280,1280]{1,0:T(8,128)(2,1)} %weight.3, ...), custom_call_target="tpu_custom_call" | custom-call | flops 2000000000 | bytes 8298512 | tf_op jit(solution)/shard_map/global/pallas_call | solution.py:54
  83.2 3.4 %collective-permute-start.9 = (bf16[192,1280]{1,0:T(8,128)(2,1)}, bf16[192,1280]{1,0:T(8,128)(2,1)S(1)}, u32[]{:S(2)}, u32[]{:S(2)}) collective-permute-start(bf16[192,1280]{1,0:T(8,128)(2,1)} %get-tuple-element.47.cot), channel_id=1, source_target_pairs={{0,1},{1,0},{2,3},{3,2},{4,5},{5,4},{6,7},{7,6},{8,9},{9,8},{10,11... | collective-permute-start | bytes 1474568 | tf_op jit(solution)/shard_map/ppermute | solution.py:278
  86.7 2.0 collective-permute-done.8.act_far
  89.5 3.7 %global_weight.1 = (f32[160,1280]{1,0:T(8,128)}, bf16[160,1280]{1,0:T(8,128)(2,1)}, bf16[160,1280]{1,0:T(8,128)(2,1)}, bf16[160,1280]{1,0:T(8,128)(2,1)}) custom-call(bf16[192,640]{1,0:T(8,128)(2,1)} %get-tuple-element.45.act, bf16[192,640]{1,0:T(8,128)(2,1)} %copy-done.20, bf16[192,1280]{1,0:T(8,128)(2,1)} %get-tuple-element.47.cot, ...), custom_call_target="tpu_custom_call" | custom-call | flops 629145600 | bytes 3522560 | tf_op jit(solution)/shard_map/global_weight/pallas_call | solution.py:54
  94.3 2.1 %collective-permute-start.11 = (bf16[160,1280]{1,0:T(8,128)(2,1)}, bf16[160,1280]{1,0:T(8,128)(2,1)S(1)}, u32[]{:S(2)}, u32[]{:S(2)}) collective-permute-start(bf16[160,1280]{1,0:T(8,128)(2,1)} %get-tuple-element.50), channel_id=1, source_target_pairs={{0,64},{32,96},{64,0},{96,32},{128,192},{160,224},{192,128},{224,1... | collective-permute-start | bytes 1228808 | tf_op jit(solution)/shard_map/ppermute | solution.py:283
  96.5 1.5 collective-permute-start.12
  98.1 7.2 %collective-permute-done.10.a = bf16[160,1280]{1,0:T(8,128)(2,1)S(1)} collective-permute-done((bf16[160,1280]{1,0:T(8,128)(2,1)}, bf16[160,1280]{1,0:T(8,128)(2,1)S(1)}, u32[]{:S(2)}, u32[]{:S(2)}) %collective-permute-start.10) | collective-permute-done | bytes 409632 | tf_op jit(solution)/shard_map/ppermute | solution.py:283
  105.3 9.4 %collective-permute-done.11.b = bf16[160,1280]{1,0:T(8,128)(2,1)S(1)} collective-permute-done((bf16[160,1280]{1,0:T(8,128)(2,1)}, bf16[160,1280]{1,0:T(8,128)(2,1)S(1)}, u32[]{:S(2)}, u32[]{:S(2)}) %collective-permute-start.11) | collective-permute-done | bytes 409632 | tf_op jit(solution)/shard_map/ppermute | solution.py:283
  115.6 2.4 %global_sum_x.1 = (f32[40,1280]{1,0:T(8,128)}, bf16[40,1280]{1,0:T(8,128)(2,1)}, bf16[40,1280]{1,0:T(8,128)(2,1)}, bf16[40,1280]{1,0:T(8,128)(2,1)}) custom-call(f32[160,1280]{1,0:T(8,128)} %get-tuple-element.48.own, bf16[160,1280]{1,0:T(8,128)(2,1)} %copy-done.3, bf16[160,1280]{1,0:T(8,128)(2,1)} %copy-done.4, bf16[160,1280]{1,0:T(8,128)(2,1)} %copy-done.5), custom_call_target="tpu_custom_call" | custom-call | bytes 2560000 | tf_op jit(solution)/shard_map/global_sum_x/pallas_call | solution.py:54
  118.0 2.7 %collective-permute-start.15 = (bf16[40,1280]{1,0:T(8,128)(2,1)}, bf16[40,1280]{1,0:T(8,128)(2,1)S(1)}, u32[]{:S(2)}, u32[]{:S(2)}) collective-permute-start(bf16[40,1280]{1,0:T(8,128)(2,1)} %get-tuple-element.55), channel_id=1, source_target_pairs={{0,6},{1,7},{2,0},{3,1},{4,2},{5,3},{6,4},{7,5},{8,14},{9,15},{10,... | collective-permute-start | bytes 307208 | tf_op jit(solution)/shard_map/ppermute | solution.py:293
  122.0 1.8 local_sum_y.1.local
  123.9 2.0 collective-permute-done.13.a
  126.6 1.9 join.1
  128.5 2.1 %collective-permute-start.17 = (bf16[24,1280]{1,0:T(8,128)(2,1)}, bf16[24,1280]{1,0:T(8,128)(2,1)S(1)}, u32[]{:S(2)}, u32[]{:S(2)}) collective-permute-start(bf16[24,1280]{1,0:T(8,128)(2,1)} %get-tuple-element.58), channel_id=1, source_target_pairs={{0,16},{1,17},{2,18},{3,19},{4,20},{5,21},{6,22},{7,23},{8,24},{9,... | collective-permute-start | bytes 184328 | tf_op jit(solution)/shard_map/ppermute | solution.py:293
  130.6 2.7 %collective-permute-start.18 = (bf16[24,1280]{1,0:T(8,128)(2,1)}, bf16[24,1280]{1,0:T(8,128)(2,1)S(1)}, u32[]{:S(2)}, u32[]{:S(2)}) collective-permute-start(bf16[24,1280]{1,0:T(8,128)(2,1)} %get-tuple-element.59), channel_id=1, source_target_pairs={{0,24},{1,25},{2,26},{3,27},{4,28},{5,29},{6,30},{7,31},{8,0},{9,1... | collective-permute-start | bytes 184328 | tf_op jit(solution)/shard_map/ppermute | solution.py:293
  134.0 2.0 collective-permute-done.17.b
  136.9 1.8 sum_z.1
  138.7 14.3 %all_to_all.27.pieces = bf16[8,24,1280]{2,1,0:T(8,128)(2,1)} all-to-all(bf16[8,24,1280]{2,1,0:T(8,128)(2,1)} %sum_z.1), channel_id=1, replica_groups=mesh['dp'=8,'tok'=32] {'dp'}, dimensions={0} | all-to-all | bytes 983040 | tf_op jit(solution)/shard_map/all_to_all | solution.py:410
  153.0 11.9 %all-to-all-start.1 = ((bf16[32,24,1024]{2,1,0:T(8,128)(2,1)}), bf16[32,24,1024]{2,1,0:T(8,128)(2,1)S(1)}, u32[]{:S(2)}, u32[]{:S(2)}) async-start(bf16[32,24,1024]{2,1,0:T(8,128)(2,1)} %bitcast.12), calls=%async_computation.1 | async-start | bytes 3145728 | tf_op jit(solution)/shard_map/all_to_all | solution.py:300
  164.8 1.9 final.1
  166.7 39.1 %all-to-all-done.1 = bf16[32,24,1024]{2,1,0:T(8,128)(2,1)S(1)} async-done(((bf16[32,24,1024]{2,1,0:T(8,128)(2,1)}), bf16[32,24,1024]{2,1,0:T(8,128)(2,1)S(1)}, u32[]{:S(2)}, u32[]{:S(2)}) %all-to-all-start.1) | async-done | bytes 1572896 | tf_op jit(solution)/shard_map/all_to_all | solution.py:300
  206.9 3.5 %unpack.1 = bf16[2,96,3840]{2,1,0:T(8,128)(2,1)} custom-call(bf16[768,1024]{1,0:T(8,128)(2,1)} %bitcast.16, bf16[384,384]{1,0:T(8,128)(2,1)} %constant.61.clone.order), custom_call_target="tpu_custom_call" | custom-call | bytes 3342336 | tf_op jit(solution)/shard_map/unpack/pallas_call | solution.py:54
  (74 shorter events, 14.6 us)
Async XLA Ops:
  4.7 12.9 %copy-start.2 = (bf16[1,2,96,1280]{3,2,1,0:T(8,128)(2,1)S(1)}, bf16[1,2,96,1280]{3,2,1,0:T(8,128)(2,1)}, u32[]{:S(2)}) copy-start(bf16[1,2,96,1280]{3,2,1,0:T(8,128)(2,1)} %param.13) | copy-start | bytes 1474564
  4.7 59.7 %all-to-all-start = ((bf16[32,24,1280]{2,1,0:T(8,128)(2,1)}), bf16[32,24,1280]{2,1,0:T(8,128)(2,1)S(1)}, u32[]{:S(2)}, u32[]{:S(2)}) async-start(bf16[32,24,1280]{2,1,0:T(8,128)(2,1)} %bitcast.15), calls=%async_computation | async-start | bytes 3932160 | tf_op jit(solution)/shard_map/all_to_all | solution.py:300
  17.6 15.1 %collective-permute-start.1 = (bf16[192,1280]{1,0:T(8,128)(2,1)S(1)}, bf16[192,1280]{1,0:T(8,128)(2,1)S(1)}, u32[]{:S(2)}, u32[]{:S(2)}) collective-permute-start(bf16[192,1280]{1,0:T(8,128)(2,1)S(1)} %bitcast.23), channel_id=1, source_target_pairs={{0,1},{1,0},{2,3},{3,2},{4,5},{5,4},{6,7},{7,6},{8,9},{9,8},{10,11... | collective-permute-start | bytes 1474568 | tf_op jit(solution)/shard_map/ppermute | solution.py:278
  31.0 1.7 collective-permute-start
  37.3 12.2 %collective-permute-start.2 = (bf16[160,1280]{1,0:T(8,128)(2,1)}, bf16[160,1280]{1,0:T(8,128)(2,1)S(1)}, u32[]{:S(2)}, u32[]{:S(2)}) collective-permute-start(bf16[160,1280]{1,0:T(8,128)(2,1)} %get-tuple-element.37), channel_id=1, source_target_pairs={{0,32},{32,64},{64,96},{96,0},{128,160},{160,192},{192,224},{224,1... | collective-permute-start | bytes 1228808 | tf_op jit(solution)/shard_map/ppermute | solution.py:283
  38.5 20.7 %collective-permute-start.3 = (bf16[160,1280]{1,0:T(8,128)(2,1)}, bf16[160,1280]{1,0:T(8,128)(2,1)S(1)}, u32[]{:S(2)}, u32[]{:S(2)}) collective-permute-start(bf16[160,1280]{1,0:T(8,128)(2,1)} %get-tuple-element.38), channel_id=1, source_target_pairs={{0,64},{32,96},{64,0},{96,32},{128,192},{160,224},{192,128},{224,1... | collective-permute-start | bytes 1228808 | tf_op jit(solution)/shard_map/ppermute | solution.py:283
  40.9 18.3 %collective-permute-start.4 = (bf16[160,1280]{1,0:T(8,128)(2,1)}, bf16[160,1280]{1,0:T(8,128)(2,1)S(1)}, u32[]{:S(2)}, u32[]{:S(2)}) collective-permute-start(bf16[160,1280]{1,0:T(8,128)(2,1)} %get-tuple-element.39), channel_id=1, source_target_pairs={{0,96},{32,0},{64,32},{96,64},{128,224},{160,128},{192,160},{224,1... | collective-permute-start | bytes 1228808 | tf_op jit(solution)/shard_map/ppermute | solution.py:283
  49.5 9.8 %copy-start.6 = (bf16[160,1280]{1,0:T(8,128)(2,1)}, bf16[160,1280]{1,0:T(8,128)(2,1)S(1)}, u32[]{:S(2)}) copy-start(bf16[160,1280]{1,0:T(8,128)(2,1)S(1)} %collective-permute-done.2.a) | copy-start | bytes 1228804
  64.3 1.3 copy-start.1
  83.2 14.8 %copy-start.24 = (bf16[40,1280]{1,0:T(8,128)(2,1)S(1)}, bf16[40,1280]{1,0:T(8,128)(2,1)}, u32[]{:S(2)}) copy-start(bf16[40,1280]{1,0:T(8,128)(2,1)} %get-tuple-element.42) | copy-start | bytes 307204
  83.2 14.8 %copy-start.23 = (bf16[40,1280]{1,0:T(8,128)(2,1)S(1)}, bf16[40,1280]{1,0:T(8,128)(2,1)}, u32[]{:S(2)}) copy-start(bf16[40,1280]{1,0:T(8,128)(2,1)} %get-tuple-element.43) | copy-start | bytes 307204
  83.2 22.1 %copy-start.22 = (bf16[40,1280]{1,0:T(8,128)(2,1)S(1)}, bf16[40,1280]{1,0:T(8,128)(2,1)}, u32[]{:S(2)}) copy-start(bf16[40,1280]{1,0:T(8,128)(2,1)} %get-tuple-element.44) | copy-start | bytes 307204
  83.2 5.4 %collective-permute-start.9 = (bf16[192,1280]{1,0:T(8,128)(2,1)}, bf16[192,1280]{1,0:T(8,128)(2,1)S(1)}, u32[]{:S(2)}, u32[]{:S(2)}) collective-permute-start(bf16[192,1280]{1,0:T(8,128)(2,1)} %get-tuple-element.47.cot), channel_id=1, source_target_pairs={{0,1},{1,0},{2,3},{3,2},{4,5},{5,4},{6,7},{7,6},{8,9},{9,8},{10,11... | collective-permute-start | bytes 1474568 | tf_op jit(solution)/shard_map/ppermute | solution.py:278
  86.6 2.1 collective-permute-start.8
  93.2 12.1 %collective-permute-start.10 = (bf16[160,1280]{1,0:T(8,128)(2,1)}, bf16[160,1280]{1,0:T(8,128)(2,1)S(1)}, u32[]{:S(2)}, u32[]{:S(2)}) collective-permute-start(bf16[160,1280]{1,0:T(8,128)(2,1)} %get-tuple-element.49), channel_id=1, source_target_pairs={{0,32},{32,64},{64,96},{96,0},{128,160},{160,192},{192,224},{224,1... | collective-permute-start | bytes 1228808 | tf_op jit(solution)/shard_map/ppermute | solution.py:283
  94.3 20.3 %collective-permute-start.11 = (bf16[160,1280]{1,0:T(8,128)(2,1)}, bf16[160,1280]{1,0:T(8,128)(2,1)S(1)}, u32[]{:S(2)}, u32[]{:S(2)}) collective-permute-start(bf16[160,1280]{1,0:T(8,128)(2,1)} %get-tuple-element.50), channel_id=1, source_target_pairs={{0,64},{32,96},{64,0},{96,32},{128,192},{160,224},{192,128},{224,1... | collective-permute-start | bytes 1228808 | tf_op jit(solution)/shard_map/ppermute | solution.py:283
  96.5 18.2 %collective-permute-start.12 = (bf16[160,1280]{1,0:T(8,128)(2,1)}, bf16[160,1280]{1,0:T(8,128)(2,1)S(1)}, u32[]{:S(2)}, u32[]{:S(2)}) collective-permute-start(bf16[160,1280]{1,0:T(8,128)(2,1)} %get-tuple-element.51), channel_id=1, source_target_pairs={{0,96},{32,0},{64,32},{96,64},{128,224},{160,128},{192,160},{224,1... | collective-permute-start | bytes 1228808 | tf_op jit(solution)/shard_map/ppermute | solution.py:283
  98.0 20.1 %collective-permute-start.5 = (bf16[40,1280]{1,0:T(8,128)(2,1)S(1)}, bf16[40,1280]{1,0:T(8,128)(2,1)S(1)}, u32[]{:S(2)}, u32[]{:S(2)}) collective-permute-start(bf16[40,1280]{1,0:T(8,128)(2,1)S(1)} %copy-done.24), channel_id=1, source_target_pairs={{0,2},{1,3},{2,4},{3,5},{4,6},{5,7},{6,0},{7,1},{8,10},{9,11},{10,... | collective-permute-start | bytes 307208 | tf_op jit(solution)/shard_map/ppermute | solution.py:293
  98.0 22.8 %collective-permute-start.6 = (bf16[40,1280]{1,0:T(8,128)(2,1)S(1)}, bf16[40,1280]{1,0:T(8,128)(2,1)S(1)}, u32[]{:S(2)}, u32[]{:S(2)}) collective-permute-start(bf16[40,1280]{1,0:T(8,128)(2,1)S(1)} %copy-done.23), channel_id=1, source_target_pairs={{0,4},{1,5},{2,6},{3,7},{4,0},{5,1},{6,2},{7,3},{8,12},{9,13},{10,... | collective-permute-start | bytes 307208 | tf_op jit(solution)/shard_map/ppermute | solution.py:293
  105.3 9.4 %copy-start.3 = (bf16[160,1280]{1,0:T(8,128)(2,1)}, bf16[160,1280]{1,0:T(8,128)(2,1)S(1)}, u32[]{:S(2)}) copy-start(bf16[160,1280]{1,0:T(8,128)(2,1)S(1)} %collective-permute-done.10.a) | copy-start | bytes 1228804
  105.3 15.5 %collective-permute-start.7 = (bf16[40,1280]{1,0:T(8,128)(2,1)S(1)}, bf16[40,1280]{1,0:T(8,128)(2,1)S(1)}, u32[]{:S(2)}, u32[]{:S(2)}) collective-permute-start(bf16[40,1280]{1,0:T(8,128)(2,1)S(1)} %copy-done.22), channel_id=1, source_target_pairs={{0,6},{1,7},{2,0},{3,1},{4,2},{5,3},{6,4},{7,5},{8,14},{9,15},{10,... | collective-permute-start | bytes 307208 | tf_op jit(solution)/shard_map/ppermute | solution.py:293
  114.7 0.9 copy-start.5
  118.0 7.9 %collective-permute-start.13 = (bf16[40,1280]{1,0:T(8,128)(2,1)}, bf16[40,1280]{1,0:T(8,128)(2,1)S(1)}, u32[]{:S(2)}, u32[]{:S(2)}) collective-permute-start(bf16[40,1280]{1,0:T(8,128)(2,1)} %get-tuple-element.53), channel_id=1, source_target_pairs={{0,2},{1,3},{2,4},{3,5},{4,6},{5,7},{6,0},{7,1},{8,10},{9,11},{10,... | collective-permute-start | bytes 307208 | tf_op jit(solution)/shard_map/ppermute | solution.py:293
  118.0 7.9 %collective-permute-start.14 = (bf16[40,1280]{1,0:T(8,128)(2,1)}, bf16[40,1280]{1,0:T(8,128)(2,1)S(1)}, u32[]{:S(2)}, u32[]{:S(2)}) collective-permute-start(bf16[40,1280]{1,0:T(8,128)(2,1)} %get-tuple-element.54), channel_id=1, source_target_pairs={{0,4},{1,5},{2,6},{3,7},{4,0},{5,1},{6,2},{7,3},{8,12},{9,13},{10,... | collective-permute-start | bytes 307208 | tf_op jit(solution)/shard_map/ppermute | solution.py:293
  118.0 2.7 %copy-start.9 = (bf16[40,1280]{1,0:T(8,128)(2,1)}, bf16[40,1280]{1,0:T(8,128)(2,1)S(1)}, u32[]{:S(2)}) copy-start(bf16[40,1280]{1,0:T(8,128)(2,1)S(1)} %collective-permute-done.5.a) | copy-start | bytes 307204
  118.0 7.8 %collective-permute-start.15 = (bf16[40,1280]{1,0:T(8,128)(2,1)}, bf16[40,1280]{1,0:T(8,128)(2,1)S(1)}, u32[]{:S(2)}, u32[]{:S(2)}) collective-permute-start(bf16[40,1280]{1,0:T(8,128)(2,1)} %get-tuple-element.55), channel_id=1, source_target_pairs={{0,6},{1,7},{2,0},{3,1},{4,2},{5,3},{6,4},{7,5},{8,14},{9,15},{10,... | collective-permute-start | bytes 307208 | tf_op jit(solution)/shard_map/ppermute | solution.py:293
  128.5 5.5 %collective-permute-start.16 = (bf16[24,1280]{1,0:T(8,128)(2,1)}, bf16[24,1280]{1,0:T(8,128)(2,1)S(1)}, u32[]{:S(2)}, u32[]{:S(2)}) collective-permute-start(bf16[24,1280]{1,0:T(8,128)(2,1)} %get-tuple-element.57), channel_id=1, source_target_pairs={{0,8},{1,9},{2,10},{3,11},{4,12},{5,13},{6,14},{7,15},{8,16},{9,17... | collective-permute-start | bytes 184328 | tf_op jit(solution)/shard_map/ppermute | solution.py:293
  128.5 7.4 %collective-permute-start.17 = (bf16[24,1280]{1,0:T(8,128)(2,1)}, bf16[24,1280]{1,0:T(8,128)(2,1)S(1)}, u32[]{:S(2)}, u32[]{:S(2)}) collective-permute-start(bf16[24,1280]{1,0:T(8,128)(2,1)} %get-tuple-element.58), channel_id=1, source_target_pairs={{0,16},{1,17},{2,18},{3,19},{4,20},{5,21},{6,22},{7,23},{8,24},{9,... | collective-permute-start | bytes 184328 | tf_op jit(solution)/shard_map/ppermute | solution.py:293
  130.6 5.6 %collective-permute-start.18 = (bf16[24,1280]{1,0:T(8,128)(2,1)}, bf16[24,1280]{1,0:T(8,128)(2,1)S(1)}, u32[]{:S(2)}, u32[]{:S(2)}) collective-permute-start(bf16[24,1280]{1,0:T(8,128)(2,1)} %get-tuple-element.59), channel_id=1, source_target_pairs={{0,24},{1,25},{2,26},{3,27},{4,28},{5,29},{6,30},{7,31},{8,0},{9,1... | collective-permute-start | bytes 184328 | tf_op jit(solution)/shard_map/ppermute | solution.py:293
  134.0 2.3 %copy-start.15 = (bf16[24,1280]{1,0:T(8,128)(2,1)}, bf16[24,1280]{1,0:T(8,128)(2,1)S(1)}, u32[]{:S(2)}) copy-start(bf16[24,1280]{1,0:T(8,128)(2,1)S(1)} %collective-permute-done.16.a) | copy-start | bytes 184324
  153.0 52.8 %all-to-all-start.1 = ((bf16[32,24,1024]{2,1,0:T(8,128)(2,1)}), bf16[32,24,1024]{2,1,0:T(8,128)(2,1)S(1)}, u32[]{:S(2)}, u32[]{:S(2)}) async-start(bf16[32,24,1024]{2,1,0:T(8,128)(2,1)} %bitcast.12), calls=%async_computation.1 | async-start | bytes 3145728 | tf_op jit(solution)/shard_map/all_to_all | solution.py:300
  205.7 1.2 copy-start
  (14 other events, 10.1 us)

commit v3 on v2

--- a/solution.py
+++ b/solution.py
@@ -256,14 +256,14 @@
         ref[...] = both.astype(ref.dtype)
 
 
-def sum_z_kernel(own, a, b, c, total):
+def sum_z_kernel(after, own, a, b, c, total):
     one = own[...] + a[...].astype(F32) + b[...].astype(F32) + c[...].astype(F32)
     one = one.astype(BF16)
     for i in range(8):
         total[i] = one
 
 
-def final_kernel(scale, pieces, local, glob):
+def final_kernel(scale, after, pieces, local, glob):
     for x in range(4):
         both = (pieces[x].astype(F32) + pieces[4 + x].astype(F32)) * scale
         local[10 * x : 10 * x + 10, :] = both[:10]
@@ -406,16 +406,28 @@
         name="join",
     )
     a, b, c = along_tok(one, 1, 0), along_tok(two, 2, 0), along_tok(three, 3, 0)
-    (mine,) = call(sum_z_kernel, [sds((8, 24, 1280), BF16)], own, a, b, c, name="sum_z")
+    (mine,) = call(
+        sum_z_kernel,
+        [sds((8, 24, 1280), BF16)],
+        returned,
+        own,
+        a,
+        b,
+        c,
+        unread=(0,),
+        name="sum_z",
+    )
     pieces = lax.all_to_all(mine, "dp", split_axis=0, concat_axis=0, tiled=True)
+    (d_global,) = call(
+        unpack_kernel, [sds((2, 96, 3840), BF16)], returned, home, name="unpack"
+    )
     grad_local, grad_global = call(
         functools.partial(final_kernel, scale),
         [sds((40, 1280), F32), sds((40, 1280), F32)],
+        d_global,
         pieces,
+        unread=(0,),
         name="final",
-    )
-    (d_global,) = call(
-        unpack_kernel, [sds((2, 96, 3840), BF16)], returned, home, name="unpack"
     )
     return (
         d_local.reshape(1, 2, 96, 3840),

time: 211 us -> 168 us (0.80)
  the two profiles are of different devices: /device:TPU:1 before, /device:TPU:64 now
where the time goes in v3:
time: 168 us; the launch traced here: 167 us
  Pallas kernels  56.9 us (34%)
  starting transfers between devices  54.9 us (33%)
  waiting for transfers between devices  45.3 us (27%)
  local copies, waits for them, and re-layouts  8.68 us (5%)
    pallas_call x12, Pallas kernels, call(): pl.pallas_call(kernel, out_shape=outs, in_specs=specs, out_specs=[pl.Bloc...  56.9 us
    ppermute x6, waiting for transfers between devices, along_x(): return lax.ppermute(a, 'dp', pairs)  27.6 us
    all_to_all x2, starting transfers between devices, exchange(): lax.all_to_all(a, 'tok', split_axis=0, concat_axis=0, axis_index_groups=T...  19.5 us
    ppermute x9, starting transfers between devices, along_tok(): return lax.ppermute(a, 'tok', pairs)  18.6 us
    ppermute x6, starting transfers between devices, along_x(): return lax.ppermute(a, 'dp', pairs)  10.8 us
    unnamed x56, local copies, waits for them, and re-layouts  8.68 us
    ppermute x9, waiting for transfers between devices, along_tok(): return lax.ppermute(a, 'tok', pairs)  7.42 us
    all_to_all x1, waiting for transfers between devices, per_device(): pieces = lax.all_to_all(mine, 'dp', split_axis=0, concat_axis=0, tiled=True)  5.78 us
  transfers between devices with their start and end apart: 22, of which 12 were waited for; matrix products, arithmetic and copies ran while one was open for 0% of the time, Pallas kernels for 19%

profile of v3, /device:TPU:64, one launch (start us, length us, event | category | flops | bytes accessed | tf_op | source)
XLA Modules:
  0.0 167.2 jit_solution(1069889486651773566)
XLA Ops:
  0.6 4.0 %pack.1 = bf16[768,1280]{1,0:T(8,128)(2,1)} custom-call(bf16[2,96,3840]{2,1,0:T(8,128)(2,1)} %bitcast.21, bf16[2,96,1280]{2,1,0:T(8,128)(2,1)} %bitcast.22, bf16[384,384]{1,0:T(8,128)(2,1)} %constant.61.clone.order), custom_call_target="tpu_custom_call" | custom-call | bytes 4227072 | tf_op jit(solution)/shard_map/pack/pallas_call | solution.py:54
  4.7 11.0 %all-to-all-start = ((bf16[32,24,1280]{2,1,0:T(8,128)(2,1)}), bf16[32,24,1280]{2,1,0:T(8,128)(2,1)S(1)}, u32[]{:S(2)}, u32[]{:S(2)}) async-start(bf16[32,24,1280]{2,1,0:T(8,128)(2,1)} %bitcast.17), calls=%async_computation | async-start | bytes 3932160 | tf_op jit(solution)/shard_map/all_to_all | solution.py:300
  16.5 12.4 %local.1 = (bf16[2,96,3840]{2,1,0:T(8,128)(2,1)}, bf16[192,640]{1,0:T(8,128)(2,1)}, bf16[192,640]{1,0:T(8,128)(2,1)}) custom-call(s32[4]{0:T(128)} %pad_add_fusion.place, f32[8]{0:T(128)} %slopes.1, bf16[2,96,3840]{2,1,0:T(8,128)(2,1)} %bitcast.26, bf16[2,96,1280]{2,1,0:T(8,128)(2,1)} %bitcast.23, bf16[1280,1280]{1,0:T(8,128)(2,1)} %weight.2, s32[2,96]{1,0:T(2,128)} %bitcast.27), custom_call_target="tpu_custom_call" | custom-call | flops 2000000000 | bytes 7209776 | tf_op jit(solution)/shard_map/local/pallas_call | solution.py:54
  31.6 3.7 %local_weight.1 = (f32[160,1280]{1,0:T(8,128)}, bf16[160,1280]{1,0:T(8,128)(2,1)}, bf16[160,1280]{1,0:T(8,128)(2,1)}, bf16[160,1280]{1,0:T(8,128)(2,1)}) custom-call(bf16[192,640]{1,0:T(8,128)(2,1)} %get-tuple-element.34.act, bf16[192,640]{1,0:T(8,128)(2,1)} %copy-done.24, bf16[192,1280]{1,0:T(8,128)(2,1)} %bitcast.24, bf16[192,1280]{1,0:T(8,128)(2,1)} %copy-done.19), custom_call_target="tpu_custom_call" | custom-call | flops 629145600 | bytes 3522560 | tf_op jit(solution)/shard_map/local_weight/pallas_call | solution.py:54
  35.2 1.5 collective-permute-start.2
  36.7 2.7 %collective-permute-start.3 = (bf16[160,1280]{1,0:T(8,128)(2,1)}, bf16[160,1280]{1,0:T(8,128)(2,1)S(1)}, u32[]{:S(2)}, u32[]{:S(2)}) collective-permute-start(bf16[160,1280]{1,0:T(8,128)(2,1)} %get-tuple-element.38), channel_id=1, source_target_pairs={{0,64},{32,96},{64,0},{96,32},{128,192},{160,224},{192,128},{224,1... | collective-permute-start | bytes 1228808 | tf_op jit(solution)/shard_map/ppermute | solution.py:283
  40.9 7.5 %collective-permute-done.2.a = bf16[160,1280]{1,0:T(8,128)(2,1)S(1)} collective-permute-done((bf16[160,1280]{1,0:T(8,128)(2,1)}, bf16[160,1280]{1,0:T(8,128)(2,1)S(1)}, u32[]{:S(2)}, u32[]{:S(2)}) %collective-permute-start.2) | collective-permute-done | bytes 409632 | tf_op jit(solution)/shard_map/ppermute | solution.py:283
  48.4 9.8 %collective-permute-done.3.b = bf16[160,1280]{1,0:T(8,128)(2,1)S(1)} collective-permute-done((bf16[160,1280]{1,0:T(8,128)(2,1)}, bf16[160,1280]{1,0:T(8,128)(2,1)S(1)}, u32[]{:S(2)}, u32[]{:S(2)}) %collective-permute-start.3) | collective-permute-done | bytes 409632 | tf_op jit(solution)/shard_map/ppermute | solution.py:283
  59.1 2.3 %local_sum_x.1 = (f32[40,1280]{1,0:T(8,128)}, bf16[40,1280]{1,0:T(8,128)(2,1)}, bf16[40,1280]{1,0:T(8,128)(2,1)}, bf16[40,1280]{1,0:T(8,128)(2,1)}) custom-call(f32[160,1280]{1,0:T(8,128)} %get-tuple-element.36.own, bf16[160,1280]{1,0:T(8,128)(2,1)} %copy-done.7, bf16[160,1280]{1,0:T(8,128)(2,1)} %copy-done.8, bf16[160,1280]{1,0:T(8,128)(2,1)} %copy-done.9), custom_call_target="tpu_custom_call" | custom-call | bytes 2560000 | tf_op jit(solution)/shard_map/local_sum_x/pallas_call | solution.py:54
  64.1 17.6 %global.1 = (bf16[768,1024]{1,0:T(8,128)(2,1)}, bf16[192,640]{1,0:T(8,128)(2,1)}, bf16[192,640]{1,0:T(8,128)(2,1)}, bf16[192,1280]{1,0:T(8,128)(2,1)}) custom-call(s32[4]{0:T(128)} %pad_add_fusion.place, f32[40,1280]{1,0:T(8,128)} %get-tuple-element.40.after.own, bf16[768,1280]{1,0:T(8,128)(2,1)} %bitcast.19, bf16[1280,1280]{1,0:T(8,128)(2,1)} %weight.3, ...), custom_call_target="tpu_custom_call" | custom-call | flops 2000000000 | bytes 8298512 | tf_op jit(solution)/shard_map/global/pallas_call | solution.py:54
  81.7 8.5 %all-to-all-start.1 = ((bf16[32,24,1024]{2,1,0:T(8,128)(2,1)}), bf16[32,24,1024]{2,1,0:T(8,128)(2,1)S(1)}, u32[]{:S(2)}, u32[]{:S(2)}) async-start(bf16[32,24,1024]{2,1,0:T(8,128)(2,1)} %bitcast.20), calls=%async_computation.1 | async-start | bytes 3145728 | tf_op jit(solution)/shard_map/all_to_all | solution.py:300
  90.8 1.7 %collective-permute-done.8.act_far = bf16[192,640]{1,0:T(8,128)(2,1)S(1)} collective-permute-done((bf16[192,640]{1,0:T(8,128)(2,1)S(1)}, bf16[192,640]{1,0:T(8,128)(2,1)S(1)}, u32[]{:S(2)}, u32[]{:S(2)}) %collective-permute-start.8) | collective-permute-done | bytes 245792 | tf_op jit(solution)/shard_map/ppermute | solution.py:278
  93.4 3.7 %global_weight.1 = (f32[160,1280]{1,0:T(8,128)}, bf16[160,1280]{1,0:T(8,128)(2,1)}, bf16[160,1280]{1,0:T(8,128)(2,1)}, bf16[160,1280]{1,0:T(8,128)(2,1)}) custom-call(bf16[192,640]{1,0:T(8,128)(2,1)} %get-tuple-element.45.act, bf16[192,640]{1,0:T(8,128)(2,1)} %copy-done.23, bf16[192,1280]{1,0:T(8,128)(2,1)} %get-tuple-element.47.cot, ...), custom_call_target="tpu_custom_call" | custom-call | flops 629145600 | bytes 3522560 | tf_op jit(solution)/shard_map/global_weight/pallas_call | solution.py:54
  98.3 2.4 %collective-permute-start.11 = (bf16[160,1280]{1,0:T(8,128)(2,1)}, bf16[160,1280]{1,0:T(8,128)(2,1)S(1)}, u32[]{:S(2)}, u32[]{:S(2)}) collective-permute-start(bf16[160,1280]{1,0:T(8,128)(2,1)} %get-tuple-element.50), channel_id=1, source_target_pairs={{0,64},{32,96},{64,0},{96,32},{128,192},{160,224},{192,128},{224,1... | collective-permute-start | bytes 1228808 | tf_op jit(solution)/shard_map/ppermute | solution.py:283
  100.6 1.6 collective-permute-start.12
  103.7 2.7 %collective-permute-start.6 = (bf16[40,1280]{1,0:T(8,128)(2,1)S(1)}, bf16[40,1280]{1,0:T(8,128)(2,1)S(1)}, u32[]{:S(2)}, u32[]{:S(2)}) collective-permute-start(bf16[40,1280]{1,0:T(8,128)(2,1)S(1)} %copy-done.26), channel_id=1, source_target_pairs={{0,4},{1,5},{2,6},{3,7},{4,0},{5,1},{6,2},{7,3},{8,12},{9,13},{10,... | collective-permute-start | bytes 307208 | tf_op jit(solution)/shard_map/ppermute | solution.py:293
  106.3 4.1 %collective-permute-done.10.a = bf16[160,1280]{1,0:T(8,128)(2,1)S(1)} collective-permute-done((bf16[160,1280]{1,0:T(8,128)(2,1)}, bf16[160,1280]{1,0:T(8,128)(2,1)S(1)}, u32[]{:S(2)}, u32[]{:S(2)}) %collective-permute-start.10) | collective-permute-done | bytes 409632 | tf_op jit(solution)/shard_map/ppermute | solution.py:283
  110.4 2.7 %collective-permute-start.7 = (bf16[40,1280]{1,0:T(8,128)(2,1)S(1)}, bf16[40,1280]{1,0:T(8,128)(2,1)S(1)}, u32[]{:S(2)}, u32[]{:S(2)}) collective-permute-start(bf16[40,1280]{1,0:T(8,128)(2,1)S(1)} %copy-done.25), channel_id=1, source_target_pairs={{0,6},{1,7},{2,0},{3,1},{4,2},{5,3},{6,4},{7,5},{8,14},{9,15},{10,... | collective-permute-start | bytes 307208 | tf_op jit(solution)/shard_map/ppermute | solution.py:293
  113.1 6.0 %collective-permute-done.11.b = bf16[160,1280]{1,0:T(8,128)(2,1)S(1)} collective-permute-done((bf16[160,1280]{1,0:T(8,128)(2,1)}, bf16[160,1280]{1,0:T(8,128)(2,1)S(1)}, u32[]{:S(2)}, u32[]{:S(2)}) %collective-permute-start.11) | collective-permute-done | bytes 409632 | tf_op jit(solution)/shard_map/ppermute | solution.py:283
  120.2 2.3 %global_sum_x.1 = (f32[40,1280]{1,0:T(8,128)}, bf16[40,1280]{1,0:T(8,128)(2,1)}, bf16[40,1280]{1,0:T(8,128)(2,1)}, bf16[40,1280]{1,0:T(8,128)(2,1)}) custom-call(f32[160,1280]{1,0:T(8,128)} %get-tuple-element.48.own, bf16[160,1280]{1,0:T(8,128)(2,1)} %copy-done.4, bf16[160,1280]{1,0:T(8,128)(2,1)} %copy-done.5, bf16[160,1280]{1,0:T(8,128)(2,1)} %copy-done.6), custom_call_target="tpu_custom_call" | custom-call | bytes 2560000 | tf_op jit(solution)/shard_map/global_sum_x/pallas_call | solution.py:54
  124.0 2.7 %collective-permute-start.14 = (bf16[40,1280]{1,0:T(8,128)(2,1)}, bf16[40,1280]{1,0:T(8,128)(2,1)S(1)}, u32[]{:S(2)}, u32[]{:S(2)}) collective-permute-start(bf16[40,1280]{1,0:T(8,128)(2,1)} %get-tuple-element.54), channel_id=1, source_target_pairs={{0,4},{1,5},{2,6},{3,7},{4,0},{5,1},{6,2},{7,3},{8,12},{9,13},{10,... | collective-permute-start | bytes 307208 | tf_op jit(solution)/shard_map/ppermute | solution.py:293
  129.4 1.8 %local_sum_y.1.local = f32[40,1280]{1,0:T(8,128)} custom-call(f32[40,1280]{1,0:T(8,128)} %get-tuple-element.40.after.own, bf16[40,1280]{1,0:T(8,128)(2,1)} %copy-done.10, bf16[40,1280]{1,0:T(8,128)(2,1)} %copy-done.11, bf16[40,1280]{1,0:T(8,128)(2,1)} %copy-done.12), custom_call_target="tpu_custom_call" | custom-call | bytes 716800 | tf_op jit(solution)/shard_map/local_sum_y/pallas_call | solution.py:54
  133.4 1.9 %join.1 = (f32[24,1280]{1,0:T(8,128)}, bf16[24,1280]{1,0:T(8,128)(2,1)}, bf16[24,1280]{1,0:T(8,128)(2,1)}, bf16[24,1280]{1,0:T(8,128)(2,1)}) custom-call(f32[40,1280]{1,0:T(8,128)} %local_sum_y.1.local, f32[40,1280]{1,0:T(8,128)} %get-tuple-element.52.own, bf16[40,1280]{1,0:T(8,128)(2,1)} %copy-done.13, bf16[40,1280]{1,0:T(8,128)(2,1)} %copy-done.14, ...), custom_call_target="tpu_custom_call" | custom-call | bytes 1024000 | tf_op jit(solution)/shard_map/join/pallas_call | solution.py:54
  135.3 2.4 %collective-permute-start.16 = (bf16[24,1280]{1,0:T(8,128)(2,1)}, bf16[24,1280]{1,0:T(8,128)(2,1)S(1)}, u32[]{:S(2)}, u32[]{:S(2)}) collective-permute-start(bf16[24,1280]{1,0:T(8,128)(2,1)} %get-tuple-element.57), channel_id=1, source_target_pairs={{0,8},{1,9},{2,10},{3,11},{4,12},{5,13},{6,14},{7,15},{8,16},{9,17... | collective-permute-start | bytes 184328 | tf_op jit(solution)/shard_map/ppermute | solution.py:293
  137.7 1.8 %collective-permute-start.17 = (bf16[24,1280]{1,0:T(8,128)(2,1)}, bf16[24,1280]{1,0:T(8,128)(2,1)S(1)}, u32[]{:S(2)}, u32[]{:S(2)}) collective-permute-start(bf16[24,1280]{1,0:T(8,128)(2,1)} %get-tuple-element.58), channel_id=1, source_target_pairs={{0,16},{1,17},{2,18},{3,19},{4,20},{5,21},{6,22},{7,23},{8,24},{9,... | collective-permute-start | bytes 184328 | tf_op jit(solution)/shard_map/ppermute | solution.py:293
  139.5 1.9 %collective-permute-start.18 = (bf16[24,1280]{1,0:T(8,128)(2,1)}, bf16[24,1280]{1,0:T(8,128)(2,1)S(1)}, u32[]{:S(2)}, u32[]{:S(2)}) collective-permute-start(bf16[24,1280]{1,0:T(8,128)(2,1)} %get-tuple-element.59), channel_id=1, source_target_pairs={{0,24},{1,25},{2,26},{3,27},{4,28},{5,29},{6,30},{7,31},{8,0},{9,1... | collective-permute-start | bytes 184328 | tf_op jit(solution)/shard_map/ppermute | solution.py:293
  141.4 5.2 %collective-permute-done.17.b = bf16[24,1280]{1,0:T(8,128)(2,1)S(1)} collective-permute-done((bf16[24,1280]{1,0:T(8,128)(2,1)}, bf16[24,1280]{1,0:T(8,128)(2,1)S(1)}, u32[]{:S(2)}, u32[]{:S(2)}) %collective-permute-start.17) | collective-permute-done | bytes 61472 | tf_op jit(solution)/shard_map/ppermute | solution.py:293
  148.6 1.8 %sum_z.1 = bf16[8,24,1280]{2,1,0:T(8,128)(2,1)} custom-call(bf16[768,1024]{1,0:T(8,128)(2,1)} %bitcast.15, f32[24,1280]{1,0:T(8,128)} %get-tuple-element.56.own, bf16[24,1280]{1,0:T(8,128)(2,1)} %copy-done.16, bf16[24,1280]{1,0:T(8,128)(2,1)} %copy-done.17, bf16[24,1280]{1,0:T(8,128)(2,1)} %copy-done.18), custom_call_target="tpu_custom_call" | custom-call | bytes 2371584 | tf_op jit(solution)/shard_map/sum_z/pallas_call | solution.py:54
  150.4 4.8 %all-to-all-start.2 = ((bf16[8,24,1280]{2,1,0:T(8,128)(2,1)}), bf16[8,24,1280]{2,1,0:T(8,128)(2,1)S(1)}, u32[]{:S(2)}, u32[]{:S(2)}) async-start(bf16[8,24,1280]{2,1,0:T(8,128)(2,1)} %sum_z.1), calls=%async_computation.2 | async-start | bytes 983040 | tf_op jit(solution)/shard_map/all_to_all | solution.py:420
  155.2 3.5 %unpack.1.after = bf16[2,96,3840]{2,1,0:T(8,128)(2,1)} custom-call(bf16[768,1024]{1,0:T(8,128)(2,1)} %bitcast.16, bf16[384,384]{1,0:T(8,128)(2,1)} %constant.61.clone.order), custom_call_target="tpu_custom_call" | custom-call | bytes 3342336 | tf_op jit(solution)/shard_map/unpack/pallas_call | solution.py:54
  158.8 5.8 %all-to-all-done.2.pieces = bf16[8,24,1280]{2,1,0:T(8,128)(2,1)S(1)} async-done(((bf16[8,24,1280]{2,1,0:T(8,128)(2,1)}), bf16[8,24,1280]{2,1,0:T(8,128)(2,1)S(1)}, u32[]{:S(2)}, u32[]{:S(2)}) %all-to-all-start.2) | async-done | bytes 491552 | tf_op jit(solution)/shard_map/all_to_all | solution.py:420
  165.3 1.9 %final.1 = (f32[40,1280]{1,0:T(8,128)}, f32[40,1280]{1,0:T(8,128)}) custom-call(bf16[2,96,3840]{2,1,0:T(8,128)(2,1)} %unpack.1.after, bf16[8,24,1280]{2,1,0:T(8,128)(2,1)} %copy-done.2), custom_call_target="tpu_custom_call" | custom-call | bytes 2375680 | tf_op jit(solution)/shard_map/final/pallas_call | solution.py:54
  (81 shorter events, 22.7 us)
Async XLA Ops:
  4.7 11.0 %copy-start.3 = (bf16[1,2,96,1280]{3,2,1,0:T(8,128)(2,1)S(1)}, bf16[1,2,96,1280]{3,2,1,0:T(8,128)(2,1)}, u32[]{:S(2)}) copy-start(bf16[1,2,96,1280]{3,2,1,0:T(8,128)(2,1)} %param.13) | copy-start | bytes 1474564
  4.7 58.2 %all-to-all-start = ((bf16[32,24,1280]{2,1,0:T(8,128)(2,1)}), bf16[32,24,1280]{2,1,0:T(8,128)(2,1)S(1)}, u32[]{:S(2)}, u32[]{:S(2)}) async-start(bf16[32,24,1280]{2,1,0:T(8,128)(2,1)} %bitcast.17), calls=%async_computation | async-start | bytes 3932160 | tf_op jit(solution)/shard_map/all_to_all | solution.py:300
  15.7 14.9 %collective-permute-start.1 = (bf16[192,1280]{1,0:T(8,128)(2,1)S(1)}, bf16[192,1280]{1,0:T(8,128)(2,1)S(1)}, u32[]{:S(2)}, u32[]{:S(2)}) collective-permute-start(bf16[192,1280]{1,0:T(8,128)(2,1)S(1)} %bitcast.25), channel_id=1, source_target_pairs={{0,1},{1,0},{2,3},{3,2},{4,5},{5,4},{6,7},{7,6},{8,9},{9,8},{10,11... | collective-permute-start | bytes 1474568 | tf_op jit(solution)/shard_map/ppermute | solution.py:278
  28.9 1.7 %collective-permute-start = (bf16[192,640]{1,0:T(8,128)(2,1)}, bf16[192,640]{1,0:T(8,128)(2,1)S(1)}, u32[]{:S(2)}, u32[]{:S(2)}) collective-permute-start(bf16[192,640]{1,0:T(8,128)(2,1)} %get-tuple-element.35), channel_id=1, source_target_pairs={{0,1},{1,0},{2,3},{3,2},{4,5},{5,4},{6,7},{7,6},{8,9},{9,8},{10,11... | collective-permute-start | bytes 737288 | tf_op jit(solution)/shard_map/ppermute | solution.py:278
  35.2 13.2 %collective-permute-start.2 = (bf16[160,1280]{1,0:T(8,128)(2,1)}, bf16[160,1280]{1,0:T(8,128)(2,1)S(1)}, u32[]{:S(2)}, u32[]{:S(2)}) collective-permute-start(bf16[160,1280]{1,0:T(8,128)(2,1)} %get-tuple-element.37), channel_id=1, source_target_pairs={{0,32},{32,64},{64,96},{96,0},{128,160},{160,192},{192,224},{224,1... | collective-permute-start | bytes 1228808 | tf_op jit(solution)/shard_map/ppermute | solution.py:283
  36.7 21.4 %collective-permute-start.3 = (bf16[160,1280]{1,0:T(8,128)(2,1)}, bf16[160,1280]{1,0:T(8,128)(2,1)S(1)}, u32[]{:S(2)}, u32[]{:S(2)}) collective-permute-start(bf16[160,1280]{1,0:T(8,128)(2,1)} %get-tuple-element.38), channel_id=1, source_target_pairs={{0,64},{32,96},{64,0},{96,32},{128,192},{160,224},{192,128},{224,1... | collective-permute-start | bytes 1228808 | tf_op jit(solution)/shard_map/ppermute | solution.py:283
  39.5 18.7 %collective-permute-start.4 = (bf16[160,1280]{1,0:T(8,128)(2,1)}, bf16[160,1280]{1,0:T(8,128)(2,1)S(1)}, u32[]{:S(2)}, u32[]{:S(2)}) collective-permute-start(bf16[160,1280]{1,0:T(8,128)(2,1)} %get-tuple-element.39), channel_id=1, source_target_pairs={{0,96},{32,0},{64,32},{96,64},{128,224},{160,128},{192,160},{224,1... | collective-permute-start | bytes 1228808 | tf_op jit(solution)/shard_map/ppermute | solution.py:283
  48.4 9.8 %copy-start.7 = (bf16[160,1280]{1,0:T(8,128)(2,1)}, bf16[160,1280]{1,0:T(8,128)(2,1)S(1)}, u32[]{:S(2)}) copy-start(bf16[160,1280]{1,0:T(8,128)(2,1)S(1)} %collective-permute-done.2.a) | copy-start | bytes 1228804
  81.7 8.5 %copy-start.20 = (bf16[192,1280]{1,0:T(8,128)(2,1)S(1)}, bf16[192,1280]{1,0:T(8,128)(2,1)}, u32[]{:S(2)}) copy-start(bf16[192,1280]{1,0:T(8,128)(2,1)} %get-tuple-element.47.cot) | copy-start | bytes 1474564
  81.7 8.8 %copy-start.22 = (bf16[192,640]{1,0:T(8,128)(2,1)S(1)}, bf16[192,640]{1,0:T(8,128)(2,1)}, u32[]{:S(2)}) copy-start(bf16[192,640]{1,0:T(8,128)(2,1)} %get-tuple-element.46) | copy-start | bytes 737284
  81.7 65.7 %all-to-all-start.1 = ((bf16[32,24,1024]{2,1,0:T(8,128)(2,1)}), bf16[32,24,1024]{2,1,0:T(8,128)(2,1)S(1)}, u32[]{:S(2)}, u32[]{:S(2)}) async-start(bf16[32,24,1024]{2,1,0:T(8,128)(2,1)} %bitcast.20), calls=%async_computation.1 | async-start | bytes 3145728 | tf_op jit(solution)/shard_map/all_to_all | solution.py:300
  90.2 12.0 %copy-start.27 = (bf16[40,1280]{1,0:T(8,128)(2,1)S(1)}, bf16[40,1280]{1,0:T(8,128)(2,1)}, u32[]{:S(2)}) copy-start(bf16[40,1280]{1,0:T(8,128)(2,1)} %get-tuple-element.42) | copy-start | bytes 307204
  90.2 13.5 %copy-start.26 = (bf16[40,1280]{1,0:T(8,128)(2,1)S(1)}, bf16[40,1280]{1,0:T(8,128)(2,1)}, u32[]{:S(2)}) copy-start(bf16[40,1280]{1,0:T(8,128)(2,1)} %get-tuple-element.43) | copy-start | bytes 307204
  90.2 20.2 %copy-start.25 = (bf16[40,1280]{1,0:T(8,128)(2,1)S(1)}, bf16[40,1280]{1,0:T(8,128)(2,1)}, u32[]{:S(2)}) copy-start(bf16[40,1280]{1,0:T(8,128)(2,1)} %get-tuple-element.44) | copy-start | bytes 307204
  90.2 2.3 %collective-permute-start.9 = (bf16[192,1280]{1,0:T(8,128)(2,1)S(1)}, bf16[192,1280]{1,0:T(8,128)(2,1)S(1)}, u32[]{:S(2)}, u32[]{:S(2)}) collective-permute-start(bf16[192,1280]{1,0:T(8,128)(2,1)S(1)} %copy-done.20), channel_id=1, source_target_pairs={{0,1},{1,0},{2,3},{3,2},{4,5},{5,4},{6,7},{7,6},{8,9},{9,8},{10,11... | collective-permute-start | bytes 1474568 | tf_op jit(solution)/shard_map/ppermute | solution.py:278
  90.4 2.1 %collective-permute-start.8 = (bf16[192,640]{1,0:T(8,128)(2,1)S(1)}, bf16[192,640]{1,0:T(8,128)(2,1)S(1)}, u32[]{:S(2)}, u32[]{:S(2)}) collective-permute-start(bf16[192,640]{1,0:T(8,128)(2,1)S(1)} %copy-done.22), channel_id=1, source_target_pairs={{0,1},{1,0},{2,3},{3,2},{4,5},{5,4},{6,7},{7,6},{8,9},{9,8},{10,11... | collective-permute-start | bytes 737288 | tf_op jit(solution)/shard_map/ppermute | solution.py:278
  97.1 13.4 %collective-permute-start.10 = (bf16[160,1280]{1,0:T(8,128)(2,1)}, bf16[160,1280]{1,0:T(8,128)(2,1)S(1)}, u32[]{:S(2)}, u32[]{:S(2)}) collective-permute-start(bf16[160,1280]{1,0:T(8,128)(2,1)} %get-tuple-element.49), channel_id=1, source_target_pairs={{0,32},{32,64},{64,96},{96,0},{128,160},{160,192},{192,224},{224,1... | collective-permute-start | bytes 1228808 | tf_op jit(solution)/shard_map/ppermute | solution.py:283
  98.3 20.9 %collective-permute-start.11 = (bf16[160,1280]{1,0:T(8,128)(2,1)}, bf16[160,1280]{1,0:T(8,128)(2,1)S(1)}, u32[]{:S(2)}, u32[]{:S(2)}) collective-permute-start(bf16[160,1280]{1,0:T(8,128)(2,1)} %get-tuple-element.50), channel_id=1, source_target_pairs={{0,64},{32,96},{64,0},{96,32},{128,192},{160,224},{192,128},{224,1... | collective-permute-start | bytes 1228808 | tf_op jit(solution)/shard_map/ppermute | solution.py:283
  100.6 18.7 %collective-permute-start.12 = (bf16[160,1280]{1,0:T(8,128)(2,1)}, bf16[160,1280]{1,0:T(8,128)(2,1)S(1)}, u32[]{:S(2)}, u32[]{:S(2)}) collective-permute-start(bf16[160,1280]{1,0:T(8,128)(2,1)} %get-tuple-element.51), channel_id=1, source_target_pairs={{0,96},{32,0},{64,32},{96,64},{128,224},{160,128},{192,160},{224,1... | collective-permute-start | bytes 1228808 | tf_op jit(solution)/shard_map/ppermute | solution.py:283
  102.2 24.5 %collective-permute-start.5 = (bf16[40,1280]{1,0:T(8,128)(2,1)S(1)}, bf16[40,1280]{1,0:T(8,128)(2,1)S(1)}, u32[]{:S(2)}, u32[]{:S(2)}) collective-permute-start(bf16[40,1280]{1,0:T(8,128)(2,1)S(1)} %copy-done.27), channel_id=1, source_target_pairs={{0,2},{1,3},{2,4},{3,5},{4,6},{5,7},{6,0},{7,1},{8,10},{9,11},{10,... | collective-permute-start | bytes 307208 | tf_op jit(solution)/shard_map/ppermute | solution.py:293
  103.7 24.5 %collective-permute-start.6 = (bf16[40,1280]{1,0:T(8,128)(2,1)S(1)}, bf16[40,1280]{1,0:T(8,128)(2,1)S(1)}, u32[]{:S(2)}, u32[]{:S(2)}) collective-permute-start(bf16[40,1280]{1,0:T(8,128)(2,1)S(1)} %copy-done.26), channel_id=1, source_target_pairs={{0,4},{1,5},{2,6},{3,7},{4,0},{5,1},{6,2},{7,3},{8,12},{9,13},{10,... | collective-permute-start | bytes 307208 | tf_op jit(solution)/shard_map/ppermute | solution.py:293
  110.4 9.0 %copy-start.4 = (bf16[160,1280]{1,0:T(8,128)(2,1)}, bf16[160,1280]{1,0:T(8,128)(2,1)S(1)}, u32[]{:S(2)}) copy-start(bf16[160,1280]{1,0:T(8,128)(2,1)S(1)} %collective-permute-done.10.a) | copy-start | bytes 1228804
  110.4 17.7 %collective-permute-start.7 = (bf16[40,1280]{1,0:T(8,128)(2,1)S(1)}, bf16[40,1280]{1,0:T(8,128)(2,1)S(1)}, u32[]{:S(2)}, u32[]{:S(2)}) collective-permute-start(bf16[40,1280]{1,0:T(8,128)(2,1)S(1)} %copy-done.25), channel_id=1, source_target_pairs={{0,6},{1,7},{2,0},{3,1},{4,2},{5,3},{6,4},{7,5},{8,14},{9,15},{10,... | collective-permute-start | bytes 307208 | tf_op jit(solution)/shard_map/ppermute | solution.py:293
  122.5 8.7 %collective-permute-start.13 = (bf16[40,1280]{1,0:T(8,128)(2,1)}, bf16[40,1280]{1,0:T(8,128)(2,1)S(1)}, u32[]{:S(2)}, u32[]{:S(2)}) collective-permute-start(bf16[40,1280]{1,0:T(8,128)(2,1)} %get-tuple-element.53), channel_id=1, source_target_pairs={{0,2},{1,3},{2,4},{3,5},{4,6},{5,7},{6,0},{7,1},{8,10},{9,11},{10,... | collective-permute-start | bytes 307208 | tf_op jit(solution)/shard_map/ppermute | solution.py:293
  124.0 8.7 %collective-permute-start.14 = (bf16[40,1280]{1,0:T(8,128)(2,1)}, bf16[40,1280]{1,0:T(8,128)(2,1)S(1)}, u32[]{:S(2)}, u32[]{:S(2)}) collective-permute-start(bf16[40,1280]{1,0:T(8,128)(2,1)} %get-tuple-element.54), channel_id=1, source_target_pairs={{0,4},{1,5},{2,6},{3,7},{4,0},{5,1},{6,2},{7,3},{8,12},{9,13},{10,... | collective-permute-start | bytes 307208 | tf_op jit(solution)/shard_map/ppermute | solution.py:293
  126.7 1.5 copy-start.10
  126.7 6.0 %collective-permute-start.15 = (bf16[40,1280]{1,0:T(8,128)(2,1)}, bf16[40,1280]{1,0:T(8,128)(2,1)S(1)}, u32[]{:S(2)}, u32[]{:S(2)}) collective-permute-start(bf16[40,1280]{1,0:T(8,128)(2,1)} %get-tuple-element.55), channel_id=1, source_target_pairs={{0,6},{1,7},{2,0},{3,1},{4,2},{5,3},{6,4},{7,5},{8,14},{9,15},{10,... | collective-permute-start | bytes 307208 | tf_op jit(solution)/shard_map/ppermute | solution.py:293
  135.3 6.2 %collective-permute-start.16 = (bf16[24,1280]{1,0:T(8,128)(2,1)}, bf16[24,1280]{1,0:T(8,128)(2,1)S(1)}, u32[]{:S(2)}, u32[]{:S(2)}) collective-permute-start(bf16[24,1280]{1,0:T(8,128)(2,1)} %get-tuple-element.57), channel_id=1, source_target_pairs={{0,8},{1,9},{2,10},{3,11},{4,12},{5,13},{6,14},{7,15},{8,16},{9,17... | collective-permute-start | bytes 184328 | tf_op jit(solution)/shard_map/ppermute | solution.py:293
  137.7 9.0 %collective-permute-start.17 = (bf16[24,1280]{1,0:T(8,128)(2,1)}, bf16[24,1280]{1,0:T(8,128)(2,1)S(1)}, u32[]{:S(2)}, u32[]{:S(2)}) collective-permute-start(bf16[24,1280]{1,0:T(8,128)(2,1)} %get-tuple-element.58), channel_id=1, source_target_pairs={{0,16},{1,17},{2,18},{3,19},{4,20},{5,21},{6,22},{7,23},{8,24},{9,... | collective-permute-start | bytes 184328 | tf_op jit(solution)/shard_map/ppermute | solution.py:293
  139.5 7.9 %collective-permute-start.18 = (bf16[24,1280]{1,0:T(8,128)(2,1)}, bf16[24,1280]{1,0:T(8,128)(2,1)S(1)}, u32[]{:S(2)}, u32[]{:S(2)}) collective-permute-start(bf16[24,1280]{1,0:T(8,128)(2,1)} %get-tuple-element.59), channel_id=1, source_target_pairs={{0,24},{1,25},{2,26},{3,27},{4,28},{5,29},{6,30},{7,31},{8,0},{9,1... | collective-permute-start | bytes 184328 | tf_op jit(solution)/shard_map/ppermute | solution.py:293
  141.4 6.0 %copy-start.16 = (bf16[24,1280]{1,0:T(8,128)(2,1)}, bf16[24,1280]{1,0:T(8,128)(2,1)S(1)}, u32[]{:S(2)}) copy-start(bf16[24,1280]{1,0:T(8,128)(2,1)S(1)} %collective-permute-done.16.a) | copy-start | bytes 184324
  150.4 14.2 %all-to-all-start.2 = ((bf16[8,24,1280]{2,1,0:T(8,128)(2,1)}), bf16[8,24,1280]{2,1,0:T(8,128)(2,1)S(1)}, u32[]{:S(2)}, u32[]{:S(2)}) async-start(bf16[8,24,1280]{2,1,0:T(8,128)(2,1)} %sum_z.1), calls=%async_computation.2 | async-start | bytes 983040 | tf_op jit(solution)/shard_map/all_to_all | solution.py:420
  (18 other events, 15.1 us)

commit v4 on v3

v4 whole, which is shorter than its diff:
```python
import functools

import jax
import jax.numpy as jnp
import numpy as np
from jax import lax
from jax.experimental import pallas as pl
from jax.experimental.pallas import tpu as pltpu
from jax.sharding import PartitionSpec as P

WC = 16
HW = 160
VMEM_LIMIT = 56 * 1024 * 1024
BF16 = jnp.bfloat16
F32 = jnp.float32


def dot_nn(a, b):
    return lax.dot_general(a, b, (((1,), (0,)), ((), ())), preferred_element_type=F32)


def dot_nt(a, b):
    return lax.dot_general(a, b, (((1,), (1,)), ((), ())), preferred_element_type=F32)


def dot_tn(a, b):
    return lax.dot_general(a, b, (((0,), (0,)), ((), ())), preferred_element_type=F32)


def order_matrix(old, new):
    sizes = dict(old)
    count = int(np.prod(list(sizes.values())))
    index = np.arange(count).reshape([s for _, s in old])
    names = [n for n, _ in old]
    moved = np.transpose(index, [names.index(n) for n in new]).reshape(-1)
    hot = np.zeros((count, count), np.float32)
    hot[np.arange(count), moved] = 1.0
    return hot


HOME = order_matrix([("s", 2), ("o", 2), ("w", 2), ("p", 8), ("t", 6)], ["p", "s", "o", "w", "t"])
GROUP = order_matrix([("p", 8), ("s", 2), ("o", 2), ("w", 2), ("t", 6)], ["s", "o", "t", "p", "w"])
FAR_COT = order_matrix([("p", 16), ("o", 2), ("w", 2), ("t", 6)], ["o", "t", "p", "w"])
BACK = order_matrix([("s", 3), ("o", 2), ("t", 6), ("p", 8), ("w", 2)], ["p", "s", "o", "w", "t"])
UNPACK = order_matrix([("p", 8), ("s", 3), ("o", 2), ("w", 2), ("t", 6)], ["s", "o", "w", "p", "t"])


def call(kernel, outs, *args, smem=(), unread=(), scratch=(), flops=0, name=None):
    specs = [
        pl.BlockSpec(
            memory_space=pltpu.SMEM if i in smem else pl.ANY if i in unread else pltpu.VMEM
        )
        for i in range(len(args))
    ]
    size = sum(int(np.prod(a.shape)) * a.dtype.itemsize for a in args)
    size += sum(int(np.prod(o.shape)) * o.dtype.itemsize for o in outs)
    return pl.pallas_call(
        kernel,
        out_shape=outs,
        in_specs=specs,
        out_specs=[pl.BlockSpec(memory_space=pltpu.VMEM) for _ in outs],
        scratch_shapes=scratch,
        compiler_params=pltpu.CompilerParams(vmem_limit_bytes=VMEM_LIMIT),
        cost_estimate=pl.CostEstimate(flops=flops, bytes_accessed=size, transcendentals=0),
        name=name,
    )(*args)


def sds(shape, dtype):
    return jax.ShapeDtypeStruct(shape, dtype)


def head_masks():
    lane = lax.broadcasted_iota(jnp.int32, (1, 256), 1)
    return [
        ((lane >= 32 * h) & (lane < 32 * h + HW)).astype(F32).astype(BF16) for h in range(4)
    ]


def side_by_side(parts):
    lane = lax.broadcasted_iota(jnp.int32, (1, 128), 1)
    tiles = [parts[0][:, :128]]
    for h in range(3):
        tiles.append(jnp.where(lane < 32 * (h + 1), parts[h][:, 128:], parts[h + 1][:, :128]))
    tiles.append(parts[3][:, 128:])
    return jnp.concatenate(tiles, axis=1)


def probabilities(q, k, masks, bias=None):
    scaling = HW ** (-0.5)
    probs = []
    for h in range(4):
        win = slice(128 * h, 128 * h + 256)
        scores = dot_nt(q[:, win] * masks[h], k[:, win]) * scaling
        if bias is not None:
            scores = scores + bias(h)
        weights = jnp.exp(scores - jnp.max(scores, axis=-1, keepdims=True))
        probs.append(weights / jnp.sum(weights, axis=-1, keepdims=True))
    return probs


def mixture(probs, v):
    parts = [
        dot_nn(probs[h].astype(BF16), v[:, 128 * h : 128 * h + 256]) for h in range(4)
    ]
    return side_by_side(parts).astype(BF16)


def gradients(probs, q, k, v, g, masks):
    scaling = HW ** (-0.5)
    dq, dk, dv = [], [], []
    for h in range(4):
        win = slice(128 * h, 128 * h + 256)
        grad_probs = dot_nt(g[:, win] * masks[h], v[:, win])
        inner = jnp.sum(probs[h] * grad_probs, axis=-1, keepdims=True)
        grad_scores = (probs[h] * (grad_probs - inner)).astype(BF16)
        dq.append(dot_nn(grad_scores, k[:, win]) * scaling)
        dk.append(dot_tn(grad_scores, q[:, win]) * scaling)
        dv.append(dot_tn(probs[h].astype(BF16), g[:, win]))
    return [side_by_side(x).astype(BF16) for x in (dq, dk, dv)]


def row_order(place):
    x, zh, y = place[0], place[1], place[2]
    rem = lax.broadcasted_iota(jnp.int32, (8, 640), 1)

    def digit(value, size):
        total = jnp.zeros_like(value)
        for k in range(1, 4):
            total = total + jnp.where(value >= k * size, 1, 0)
        return total, value - total * size

    dx, rem = digit(rem, 160)
    dy, rem = digit(rem, 40)
    df, rem = digit(rem, 10)
    to = (zh + df) & 3
    return (((to >> 1) * 4 + ((y + dy) & 3)) * 2 + (to & 1)) * 40 + ((x + dx) & 3) * 10 + rem


def row_hot(place):
    lane = row_order(place)[:1]
    rows = lax.broadcasted_iota(jnp.int32, (640, 640), 0)
    return (rows == lane).astype(F32).astype(BF16)


def lanes_of(section, core):
    return pl.ds(pl.multiple_of(1280 * section + 640 * core, 128), 640)


def far_kernel(place, qkv, out):
    for s in range(3):
        for w in range(2):
            out[w, :, 640 * s : 640 * s + 640] = qkv[w, :, lanes_of(s, 1 - place[3])]


def pack_kernel(place, qkv, far, cot, order, out):
    hot = order[...]
    for group in range(2):
        rows = slice(48 * group, 48 * group + 48)

        def section(s):
            own = [qkv[w, rows, lanes_of(s, place[3])] for w in range(2)]
            return own + [far[w, rows, 640 * s : 640 * s + 640] for w in range(2)]

        cots = [cot[w, rows, 640 * half : 640 * half + 640] for half in range(2) for w in range(2)]
        for part, pieces in enumerate((section(0) + section(1), section(2) + cots)):
            sent = dot_nn(hot, jnp.concatenate(pieces, axis=0)).astype(BF16)
            for p in range(8):
                start = 96 * (8 * group + p) + 48 * part
                out[start : start + 48, :] = sent[48 * p : 48 * p + 48, :]


def unpack_kernel(got, order, mine, other):
    hot = order[...]
    for group in range(2):
        rows = dot_nn(hot, got[576 * group : 576 * group + 576, :]).astype(BF16)
        for s in range(3):
            for o, ref in enumerate((mine, other)):
                for w in range(2):
                    start = 48 * ((s * 2 + o) * 2 + w)
                    ref[w, 48 * group : 48 * group + 48, 640 * s : 640 * s + 640] = rows[
                        start : start + 48, :
                    ]


def merge_kernel(place, mine, far, out):
    for s in range(3):
        for w in range(2):
            out[w, :, lanes_of(s, place[3])] = mine[w, :, 640 * s : 640 * s + 640]
            out[w, :, lanes_of(s, 1 - place[3])] = far[w, :, 640 * s : 640 * s + 640]


def local_kernel(place, slopes, qkv, cot, weight, positions, d_out, act_own, act_other, act_all):
    masks = head_masks()
    flat = jnp.concatenate([cot[0], cot[1]], axis=0)
    g = dot_nt(flat, weight[...]).astype(BF16)
    for w in range(2):
        spread = jnp.broadcast_to(positions[w : w + 1, :], (96, 96))
        spread_t = spread.astype(F32).T.astype(jnp.int32)
        distance = (
            jnp.abs((spread >> 4) - (spread_t >> 4)) + jnp.abs((spread & 15) - (spread_t & 15))
        ).astype(F32)
        for half in range(2):
            lanes = slice(640 * half, 640 * half + 640)
            q, k, v = [
                qkv[w, :, 1280 * s + 640 * half : 1280 * s + 640 * half + 640] for s in range(3)
            ]
            probs = probabilities(q, k, masks, lambda h: -(slopes[4 * half + h] * distance))
            act_all[96 * w : 96 * w + 96, lanes] = mixture(probs, v)
            grads = gradients(probs, q, k, v, g[96 * w : 96 * w + 96, lanes], masks)
            for s, part in enumerate(grads):
                d_out[w, :, 1280 * s + 640 * half : 1280 * s + 640 * half + 640] = part
    hot = row_hot(place)
    act_own[...] = dot_nn(act_all[:, lanes_of(0, place[3])], hot).astype(BF16)
    act_other[...] = dot_nn(act_all[:, lanes_of(0, 1 - place[3])], hot).astype(BF16)


def group_kernel(place, after, got, order, data, cot, probs_out, act, act_all):
    masks = head_masks()
    hot = order[...]
    for group in range(2):
        for part in range(2):
            pieces = [
                got[96 * (8 * group + p) + 48 * part : 96 * (8 * group + p) + 48 * part + 48, :]
                for p in range(8)
            ]
            rows = dot_nn(hot, jnp.concatenate(pieces, axis=0)).astype(BF16)
            for s in range(2):
                for o in range(2):
                    for t in range(6):
                        start = 16 * ((s * 2 + o) * 6 + t)
                        piece = rows[start : start + 16, :]
                        to = slice(32 * t + 16 * group, 32 * t + 16 * group + 16)
                        if part == 1 and s == 1:
                            cot[to, 640 * o : 640 * o + 640] = piece
                        else:
                            data[2 * part + s, o, to, :] = piece
    for t in range(6):
        rows = slice(32 * t, 32 * t + 32)
        q, k, v = [
            jnp.concatenate([data[s, 0, rows, :], data[s, 1, rows, :]], axis=0) for s in range(3)
        ]
        probs = probabilities(q, k, masks)
        for h in range(4):
            probs_out[4 * t + h] = probs[h]
        mixed = mixture(probs, v)
        act_all[32 * t : 32 * t + 32, :] = mixed[:32]
        act_all[192 + 32 * t : 192 + 32 * t + 32, :] = mixed[32:]
    act[...] = dot_nn(act_all[...], row_hot(place)).astype(BF16)


def group_back_kernel(place, probs_in, data, cot, cot_far, weight, order, back, grads):
    masks = head_masks()
    hot = order[...]
    own_rows = weight[pl.ds(pl.multiple_of(640 * place[3], 128), 640), :]
    g_own = dot_nt(cot[...], own_rows).astype(BF16)
    g_far = dot_nt(cot_far[...], own_rows).astype(BF16)
    for t in range(6):
        rows = slice(32 * t, 32 * t + 32)
        q, k, v = [
            jnp.concatenate([data[s, 0, rows, :], data[s, 1, rows, :]], axis=0) for s in range(3)
        ]
        g = jnp.concatenate([g_own[rows], g_far[rows]], axis=0)
        probs = [probs_in[4 * t + h] for h in range(4)]
        for s, part in enumerate(gradients(probs, q, k, v, g, masks)):
            grads[s, 0, rows, :] = part[:32]
            grads[s, 1, rows, :] = part[32:]
    for group in range(2):
        pieces = [
            grads[s, o, 32 * t + 16 * group : 32 * t + 16 * group + 16, :]
            for s in range(3)
            for o in range(2)
            for t in range(6)
        ]
        whole = jnp.concatenate(pieces, axis=0)
        back[576 * group : 576 * group + 576, :] = dot_nn(hot, whole).astype(BF16)


def weight_parts(a, b, cot, cot_far, own, one, two, three):
    for part in range(5):
        cols = slice(256 * part, 256 * part + 256)
        total = dot_tn(a, cot[:, cols]) + dot_tn(b, cot_far[:, cols])
        own[:, cols] = total[:160]
        for d, ref in ((1, one), (2, two), (3, three)):
            ref[:, cols] = total[160 * d : 160 * d + 160].astype(BF16)


def local_weight_kernel(act, act_far, cot, cot_far, own, one, two, three):
    weight_parts(act[...], act_far[...], cot, cot_far, own, one, two, three)


def group_weight_kernel(act, cot, got_far, order, own, one, two, three, cot_far):
    rows = dot_nn(order[...], got_far[...]).astype(BF16)
    cot_far[:, :640] = rows[:192]
    cot_far[:, 640:] = rows[192:]
    weight_parts(act[:192, :], act[192:, :], cot, cot_far, own, one, two, three)


def sum_of(own, *others):
    total = own[...].astype(F32)
    for other in others:
        total = total + other[...].astype(F32)
    return total


def local_sum_kernel(own, a, b, c, total):
    total[...] = sum_of(own, a, b, c)


def sum_x_kernel(local, own, a, b, c, kept, one, two, three):
    total = sum_of(own, a, b, c)
    for d, ref in enumerate((kept, one, two, three)):
        rows = slice(40 * d, 40 * d + 40)
        ref[:40, :] = local[rows, :].astype(ref.dtype)
        ref[40:, :] = total[rows].astype(ref.dtype)


def sum_y_kernel(own, a, b, c, *chunks):
    total = sum_of(own, a, b, c)
    for d, ref in enumerate(chunks):
        first = total[10 * d : 10 * d + 10]
        second = total[40 + 10 * d : 40 + 10 * d + 10]
        both = jnp.concatenate([first, second, jnp.zeros((4, 1280), F32)], axis=0)
        ref[...] = both.astype(BF16)


def sum_z_kernel(after, a, b, c, d, out):
    total = sum_of(a, b, c, d).astype(BF16)
    for i in range(8):
        out[i] = total


def final_kernel(scale, after, pieces, local, glob):
    for x in range(4):
        both = (pieces[x].astype(F32) + pieces[4 + x].astype(F32)) * scale
        local[10 * x : 10 * x + 10, :] = both[:10]
        glob[10 * x : 10 * x + 10, :] = both[10:20]


def chip(z, y, c):
    return z * 8 + y * 2 + c


def swap_cores(a):
    return lax.ppermute(a, "tok", [(i, i ^ 1) for i in range(32)])


def along_x(a, d):
    pairs = [(z * 4 + x, z * 4 + (x + d) % 4) for z in range(2) for x in range(4)]
    return lax.ppermute(a, "dp", pairs)


def along_y(a, d):
    pairs = [
        (chip(z, y, c), chip(z, (y + d) % 4, c))
        for z in range(4)
        for y in range(4)
        for c in range(2)
    ]
    return lax.ppermute(a, "tok", pairs)


def to_owner(a, d):
    pairs = []
    for z in range(4):
        to = (z + d) % 4
        for y in range(4):
            for c in range(2):
                pairs.append((chip(z, y, c), chip(2 * c + to // 2, y, to % 2)))
    return lax.ppermute(a, "tok", pairs)


CHIPS = [[chip(0, 0, c) + 2 * p for p in range(16)] for c in range(2)]


def exchange(a):
    return lax.all_to_all(
        a, "tok", split_axis=0, concat_axis=0, axis_index_groups=CHIPS, tiled=True
    )


def per_device(qkv_local, qkv_global, positions, slopes, cotangent, w_out_local, w_out_global):
    tokens = 192 * 256
    scale = float(tokens) ** (-0.5)
    dp, tok = lax.axis_index("dp"), lax.axis_index("tok")
    place = jnp.stack([dp % 4, tok // 8, (tok // 2) % 4, tok % 2]).astype(jnp.int32)
    qkv_local = qkv_local.reshape(2, 96, 3840)
    qkv_global = qkv_global.reshape(2, 96, 3840)
    cotangent = cotangent.reshape(2, 96, 1280)
    flat_cot = cotangent.reshape(192, 1280)
    positions = positions.reshape(2, 96)
    partials = [sds((160, 1280), F32)] + [sds((160, 1280), BF16)] * 3

    (other,) = call(
        far_kernel, [sds((2, 96, 1920), BF16)], place, qkv_global, smem=(0,), name="far"
    )
    far = swap_cores(other)
    (packed,) = call(
        pack_kernel,
        [sds((1536, 640), BF16)],
        place,
        qkv_global,
        far,
        cotangent,
        jnp.asarray(HOME, BF16),
        smem=(0,),
        name="pack",
    )
    got = exchange(packed)

    d_local, act_own, act_other = call(
        local_kernel,
        [sds((2, 96, 3840), BF16), sds((192, 640), BF16), sds((192, 640), BF16)],
        place,
        slopes,
        qkv_local,
        cotangent,
        w_out_local,
        positions,
        smem=(0, 1),
        scratch=[pltpu.VMEM((192, 1280), BF16)],
        flops=2 * 10**9,
        name="local",
    )
    own, one, two, three = call(
        local_weight_kernel,
        partials,
        act_own,
        swap_cores(act_other),
        flat_cot,
        swap_cores(flat_cot),
        flops=2 * 640 * 384 * 1280,
        name="local_weight",
    )
    (local_rows,) = call(
        local_sum_kernel,
        [sds((160, 1280), F32)],
        own,
        along_x(one, 1),
        along_x(two, 2),
        along_x(three, 3),
        name="local_sum_x",
    )

    got_far = swap_cores(got.reshape(16, 96, 640)[:, 72:, :]).reshape(384, 640)
    data, cot, probs, act = call(
        group_kernel,
        [
            sds((3, 2, 192, 640), BF16),
            sds((192, 1280), BF16),
            sds((24, 64, 64), F32),
            sds((384, 640), BF16),
        ],
        place,
        local_rows,
        got,
        jnp.asarray(GROUP, BF16),
        smem=(0,),
        unread=(1,),
        scratch=[pltpu.VMEM((384, 640), BF16)],
        flops=10**9,
        name="group",
    )
    own, one, two, three, cot_far = call(
        group_weight_kernel,
        partials + [sds((192, 1280), BF16)],
        act,
        cot,
        got_far,
        jnp.asarray(FAR_COT, BF16),
        flops=2 * 640 * 384 * 1280,
        name="group_weight",
    )
    a, b, c = along_x(one, 1), along_x(two, 2), along_x(three, 3)
    (back,) = call(
        group_back_kernel,
        [sds((1152, 640), BF16)],
        place,
        probs,
        data,
        cot,
        cot_far,
        w_out_global,
        jnp.asarray(BACK, BF16),
        smem=(0,),
        scratch=[pltpu.VMEM((3, 2, 192, 640), BF16)],
        flops=2 * 10**9,
        name="group_back",
    )
    returned = exchange(back)

    own, one, two, three = call(
        sum_x_kernel,
        [sds((80, 1280), F32)] + [sds((80, 1280), BF16)] * 3,
        local_rows,
        own,
        a,
        b,
        c,
        name="sum_x",
    )
    chunks = call(
        sum_y_kernel,
        [sds((24, 1280), BF16)] * 4,
        own,
        along_y(one, 1),
        along_y(two, 2),
        along_y(three, 3),
        name="sum_y",
    )
    mine, other = call(
        unpack_kernel,
        [sds((2, 96, 1920), BF16)] * 2,
        returned,
        jnp.asarray(UNPACK, BF16),
        name="unpack",
    )
    (sums,) = call(
        sum_z_kernel,
        [sds((8, 24, 1280), BF16)],
        returned,
        *[to_owner(chunk, d) for d, chunk in enumerate(chunks)],
        unread=(0,),
        name="sum_z",
    )
    pieces = lax.all_to_all(sums, "dp", split_axis=0, concat_axis=0, tiled=True)
    (d_global,) = call(
        merge_kernel,
        [sds((2, 96, 3840), BF16)],
        place,
        mine,
        swap_cores(other),
        smem=(0,),
        name="merge",
    )
    grad_local, grad_global = call(
        functools.partial(final_kernel, scale),
        [sds((40, 1280), F32), sds((40, 1280), F32)],
        d_global,
        pieces,
        unread=(0,),
        name="final",
    )
    return (
        d_local.reshape(1, 2, 96, 3840),
        d_global.reshape(1, 2, 96, 3840),
        grad_local,
        grad_global,
    )


def solution(mesh):
    placed = (
        P("dp", "tok", None, None),
        P("dp", "tok", None, None),
        P("dp", "tok", None),
        P(),
        P("dp", "tok", None, None),
        P(),
        P(),
    )
    return jax.shard_map(
        per_device,
        mesh=mesh,
        in_specs=placed,
        out_specs=(
            P("dp", "tok", None, None),
            P("dp", "tok", None, None),
            P("tok", None),
            P("tok", None),
        ),
        check_vma=False,
    )
```

time: 168 us -> 195 us (1.16)
  the two profiles are of different devices: /device:TPU:64 before, /device:TPU:1 now
where the time goes in v4:
time: 195 us; the launch traced here: 194 us
  waiting for transfers between devices  67.4 us (35%)
  Pallas kernels  62.9 us (32%)
  starting transfers between devices  54.8 us (28%)
  local copies, waits for them, and re-layouts  7.87 us (4%)
    pallas_call x14, Pallas kernels, call(): pl.pallas_call(kernel, out_shape=outs, in_specs=specs, out_specs=[pl.Bloc...  62.9 us
    all_to_all x2, waiting for transfers between devices, exchange(): lax.all_to_all(a, 'tok', split_axis=0, concat_axis=0, axis_index_groups=C...  22.5 us
    ppermute x6, waiting for transfers between devices, along_x(): return lax.ppermute(a, 'dp', pairs)  17.5 us
    all_to_all x2, starting transfers between devices, exchange(): lax.all_to_all(a, 'tok', split_axis=0, concat_axis=0, axis_index_groups=C...  15.2 us
    ppermute x3, waiting for transfers between devices, along_y(): return lax.ppermute(a, 'tok', pairs)  14 us
    ppermute x4, starting transfers between devices, to_owner(): return lax.ppermute(a, 'tok', pairs)  13 us
    ppermute x6, starting transfers between devices, along_x(): return lax.ppermute(a, 'dp', pairs)  8.97 us
    unnamed x50, local copies, waits for them, and re-layouts  7.82 us
  transfers between devices with their start and end apart: 21, of which 12 were waited for; matrix products, arithmetic and copies ran while one was open for 0% of the time, Pallas kernels for 18%

profile of v4, /device:TPU:1, one launch (start us, length us, event | category | flops | bytes accessed | tf_op | source)
XLA Modules:
  0.0 194.4 jit_solution(15320105034842210236)
XLA Ops:
  1.3 2.3 %far.1 = bf16[2,96,1920]{2,1,0:T(8,128)(2,1)} custom-call(s32[4]{0:T(128)} %pad_add_fusion.place, bf16[2,96,3840]{2,1,0:T(8,128)(2,1)} %bitcast.19), custom_call_target="tpu_custom_call" | custom-call | bytes 2211856 | tf_op jit(solution)/shard_map/far/pallas_call | solution.py:57
  3.6 3.2 %collective-permute-start.5 = (bf16[2,96,1920]{2,1,0:T(8,128)(2,1)}, bf16[2,96,1920]{2,1,0:T(8,128)(2,1)S(1)}, u32[]{:S(2)}, u32[]{:S(2)}) collective-permute-start(bf16[2,96,1920]{2,1,0:T(8,128)(2,1)} %far.1), channel_id=1, source_target_pairs={{0,1},{1,0},{2,3},{3,2},{4,5},{5,4},{6,7},{7,6},{8,9},{9,8},{10,11... | collective-permute-start | bytes 2211848 | tf_op jit(solution)/shard_map/ppermute | solution.py:345
  6.9 2.1 %collective-permute-done.5.far = bf16[2,96,1920]{2,1,0:T(8,128)(2,1)S(1)} collective-permute-done((bf16[2,96,1920]{2,1,0:T(8,128)(2,1)}, bf16[2,96,1920]{2,1,0:T(8,128)(2,1)S(1)}, u32[]{:S(2)}, u32[]{:S(2)}) %collective-permute-start.5) | collective-permute-done | bytes 737312 | tf_op jit(solution)/shard_map/ppermute | solution.py:345
  9.8 4.4 %pack.1 = bf16[1536,640]{1,0:T(8,128)(2,1)} custom-call(s32[4]{0:T(128)} %pad_add_fusion.place, bf16[2,96,3840]{2,1,0:T(8,128)(2,1)} %bitcast.20, bf16[2,96,1920]{2,1,0:T(8,128)(2,1)} %copy-done.3, bf16[2,96,1280]{2,1,0:T(8,128)(2,1)} %bitcast.24, bf16[384,384]{1,0:T(8,128)(2,1)} %constant.67.clone.order), custom_call_target="tpu_custom_call" | custom-call | bytes 4964368 | tf_op jit(solution)/shard_map/pack/pallas_call | solution.py:57
  14.2 9.3 %all-to-all-start = ((bf16[16,96,640]{2,1,0:T(8,128)(2,1)}), bf16[16,96,640]{2,1,0:T(8,128)(2,1)S(1)}, u32[]{:S(2)}, u32[]{:S(2)}) async-start(bf16[16,96,640]{2,1,0:T(8,128)(2,1)} %bitcast.18), calls=%async_computation | async-start | bytes 3932160 | tf_op jit(solution)/shard_map/all_to_all | solution.py:377
  24.2 11.2 %local.1 = (bf16[2,96,3840]{2,1,0:T(8,128)(2,1)}, bf16[192,640]{1,0:T(8,128)(2,1)}, bf16[192,640]{1,0:T(8,128)(2,1)}) custom-call(s32[4]{0:T(128)} %pad_add_fusion.place, f32[8]{0:T(128)} %slopes.1, bf16[2,96,3840]{2,1,0:T(8,128)(2,1)} %bitcast.28, bf16[2,96,1280]{2,1,0:T(8,128)(2,1)} %bitcast.25, bf16[1280,1280]{1,0:T(8,128)(2,1)} %weight.2, s32[2,96]{1,0:T(2,128)} %bitcast.30), custom_call_target="tpu_custom_call" | custom-call | flops 2000000000 | bytes 7209776 | tf_op jit(solution)/shard_map/local/pallas_call | solution.py:57
  38.0 3.7 %local_weight.1 = (f32[160,1280]{1,0:T(8,128)}, bf16[160,1280]{1,0:T(8,128)(2,1)}, bf16[160,1280]{1,0:T(8,128)(2,1)}, bf16[160,1280]{1,0:T(8,128)(2,1)}) custom-call(bf16[192,640]{1,0:T(8,128)(2,1)} %get-tuple-element.33.act, bf16[192,640]{1,0:T(8,128)(2,1)} %copy-done.24, bf16[192,1280]{1,0:T(8,128)(2,1)} %bitcast.26, bf16[192,1280]{1,0:T(8,128)(2,1)} %copy-done.20), custom_call_target="tpu_custom_call" | custom-call | flops 629145600 | bytes 3522560 | tf_op jit(solution)/shard_map/local_weight/pallas_call | solution.py:57
  42.9 2.4 %collective-permute-start.3 = (bf16[160,1280]{1,0:T(8,128)(2,1)}, bf16[160,1280]{1,0:T(8,128)(2,1)S(1)}, u32[]{:S(2)}, u32[]{:S(2)}) collective-permute-start(bf16[160,1280]{1,0:T(8,128)(2,1)} %get-tuple-element.37), channel_id=1, source_target_pairs={{0,64},{32,96},{64,0},{96,32},{128,192},{160,224},{192,128},{224,1... | collective-permute-start | bytes 1228808 | tf_op jit(solution)/shard_map/ppermute | solution.py:350
  46.5 22.5 %all-to-all-done = bf16[16,96,640]{2,1,0:T(8,128)(2,1)S(1)} async-done(((bf16[16,96,640]{2,1,0:T(8,128)(2,1)}), bf16[16,96,640]{2,1,0:T(8,128)(2,1)S(1)}, u32[]{:S(2)}, u32[]{:S(2)}) %all-to-all-start) | async-done | bytes 1966112 | tf_op jit(solution)/shard_map/all_to_all | solution.py:377
  69.0 3.3 %collective-permute-start.6 = (bf16[16,24,640]{2,1,0:T(8,128)(2,1)S(1)}, bf16[16,24,640]{2,1,0:T(8,128)(2,1)S(1)}, u32[]{:S(2)}, u32[]{:S(2)}) collective-permute-start(bf16[16,24,640]{2,1,0:T(8,128)(2,1)S(1)} %slice.4), channel_id=1, source_target_pairs={{0,1},{1,0},{2,3},{3,2},{4,5},{5,4},{6,7},{7,6},{8,9},{9,8},{10,11... | collective-permute-start | bytes 1474568 | tf_op jit(solution)/shard_map/ppermute | solution.py:345
  73.4 2.6 %local_sum_x.1.after.local = f32[160,1280]{1,0:T(8,128)} custom-call(f32[160,1280]{1,0:T(8,128)} %get-tuple-element.35.own, bf16[160,1280]{1,0:T(8,128)(2,1)} %copy-done.6, bf16[160,1280]{1,0:T(8,128)(2,1)} %copy-done.7, bf16[160,1280]{1,0:T(8,128)(2,1)} %copy-done.9), custom_call_target="tpu_custom_call" | custom-call | bytes 2867200 | tf_op jit(solution)/shard_map/local_sum_x/pallas_call | solution.py:57
  75.9 6.4 %group.1 = (bf16[3,2,192,640]{3,2,1,0:T(8,128)(2,1)}, bf16[192,1280]{1,0:T(8,128)(2,1)}, f32[24,64,64]{2,1,0:T(8,128)}, bf16[384,640]{1,0:T(8,128)(2,1)}) custom-call(s32[4]{0:T(128)} %pad_add_fusion.place, f32[160,1280]{1,0:T(8,128)} %local_sum_x.1.after.local, bf16[1536,640]{1,0:T(8,128)(2,1)} %bitcast.23, bf16[384,384]{1,0:T(8,128)(2,1)} %constant.68.clone.order), custom_call_target="tpu_custom_call" | custom-call | flops 1000000000 | bytes 5931024 | tf_op jit(solution)/shard_map/group/pallas_call | solution.py:57
  83.1 4.0 %group_weight.1 = (f32[160,1280]{1,0:T(8,128)}, bf16[160,1280]{1,0:T(8,128)(2,1)}, bf16[160,1280]{1,0:T(8,128)(2,1)}, bf16[160,1280]{1,0:T(8,128)(2,1)}, bf16[192,1280]{1,0:T(8,128)(2,1)}) custom-call(bf16[384,640]{1,0:T(8,128)(2,1)} %get-tuple-element.42.act, bf16[192,1280]{1,0:T(8,128)(2,1)} %get-tuple-element.41.cot, bf16[384,640]{1,0:T(8,128)(2,1)} %bitcast.29, ...), custom_call_target="tpu_custom_call" | custom-call | flops 629145600 | bytes 4308992 | tf_op jit(solution)/shard_map/group_weight/pallas_call | solution.py:57
  87.2 13.4 %group_back.1 = bf16[1152,640]{1,0:T(8,128)(2,1)} custom-call(s32[4]{0:T(128)} %pad_add_fusion.place, f32[24,64,64]{2,1,0:T(8,128)} %get-tuple-element.39.probs_in, bf16[3,2,192,640]{3,2,1,0:T(8,128)(2,1)} %get-tuple-element.40.data, bf16[192,1280]{1,0:T(8,128)(2,1)} %get-tuple-element.41.cot, bf16[192,1280]{1,0:T(8,128)(2,1)} %get-tuple-element.43.cot_far, ...), custom_call_target="tpu_custom_call" | custom-call | flops 2000000000 | bytes 8265744 | tf_op jit(solution)/shard_map/group_back/pallas_call | solution.py:57
  100.5 5.9 %all-to-all-start.1 = ((bf16[16,72,640]{2,1,0:T(8,128)(2,1)}), bf16[16,72,640]{2,1,0:T(8,128)(2,1)S(1)}, u32[]{:S(2)}, u32[]{:S(2)}) async-start(bf16[16,72,640]{2,1,0:T(8,128)(2,1)} %bitcast.22), calls=%async_computation.1 | async-start | bytes 2949120 | tf_op jit(solution)/shard_map/all_to_all | solution.py:377
  108.1 2.5 %collective-permute-start.9 = (bf16[160,1280]{1,0:T(8,128)(2,1)S(1)}, bf16[160,1280]{1,0:T(8,128)(2,1)S(1)}, u32[]{:S(2)}, u32[]{:S(2)}) collective-permute-start(bf16[160,1280]{1,0:T(8,128)(2,1)S(1)} %copy-done.21), channel_id=1, source_target_pairs={{0,64},{32,96},{64,0},{96,32},{128,192},{160,224},{192,128},{224,1... | collective-permute-start | bytes 1228808 | tf_op jit(solution)/shard_map/ppermute | solution.py:350
  110.6 6.4 %collective-permute-done.10.c = bf16[160,1280]{1,0:T(8,128)(2,1)S(1)} collective-permute-done((bf16[160,1280]{1,0:T(8,128)(2,1)S(1)}, bf16[160,1280]{1,0:T(8,128)(2,1)S(1)}, u32[]{:S(2)}, u32[]{:S(2)}) %collective-permute-start.10) | collective-permute-done | bytes 409632 | tf_op jit(solution)/shard_map/ppermute | solution.py:350
  117.0 2.6 %collective-permute-done.8.a = bf16[160,1280]{1,0:T(8,128)(2,1)S(1)} collective-permute-done((bf16[160,1280]{1,0:T(8,128)(2,1)S(1)}, bf16[160,1280]{1,0:T(8,128)(2,1)S(1)}, u32[]{:S(2)}, u32[]{:S(2)}) %collective-permute-start.8) | collective-permute-done | bytes 409632 | tf_op jit(solution)/shard_map/ppermute | solution.py:350
  119.5 8.5 %collective-permute-done.9.b = bf16[160,1280]{1,0:T(8,128)(2,1)S(1)} collective-permute-done((bf16[160,1280]{1,0:T(8,128)(2,1)S(1)}, bf16[160,1280]{1,0:T(8,128)(2,1)S(1)}, u32[]{:S(2)}, u32[]{:S(2)}) %collective-permute-start.9) | collective-permute-done | bytes 409632 | tf_op jit(solution)/shard_map/ppermute | solution.py:350
  128.9 2.8 %sum_x.1 = (f32[80,1280]{1,0:T(8,128)}, bf16[80,1280]{1,0:T(8,128)(2,1)}, bf16[80,1280]{1,0:T(8,128)(2,1)}, bf16[80,1280]{1,0:T(8,128)(2,1)}) custom-call(f32[160,1280]{1,0:T(8,128)} %local_sum_x.1.after.local, f32[160,1280]{1,0:T(8,128)} %get-tuple-element.46.own, bf16[160,1280]{1,0:T(8,128)(2,1)} %copy-done.10, bf16[160,1280]{1,0:T(8,128)(2,1)} %copy-done.11, ...), custom_call_target="tpu_custom_call" | custom-call | bytes 3891200 | tf_op jit(solution)/shard_map/sum_x/pallas_call | solution.py:57
  132.7 2.4 %collective-permute-start.12 = (bf16[80,1280]{1,0:T(8,128)(2,1)}, bf16[80,1280]{1,0:T(8,128)(2,1)S(1)}, u32[]{:S(2)}, u32[]{:S(2)}) collective-permute-start(bf16[80,1280]{1,0:T(8,128)(2,1)} %get-tuple-element.52), channel_id=1, source_target_pairs={{0,4},{1,5},{2,6},{3,7},{4,0},{5,1},{6,2},{7,3},{8,12},{9,13},{10,... | collective-permute-start | bytes 614408 | tf_op jit(solution)/shard_map/ppermute | solution.py:360
  136.2 7.9 %collective-permute-done.11.a = bf16[80,1280]{1,0:T(8,128)(2,1)S(1)} collective-permute-done((bf16[80,1280]{1,0:T(8,128)(2,1)}, bf16[80,1280]{1,0:T(8,128)(2,1)S(1)}, u32[]{:S(2)}, u32[]{:S(2)}) %collective-permute-start.11) | collective-permute-done | bytes 204832 | tf_op jit(solution)/shard_map/ppermute | solution.py:360
  144.1 4.4 %collective-permute-done.12.b = bf16[80,1280]{1,0:T(8,128)(2,1)S(1)} collective-permute-done((bf16[80,1280]{1,0:T(8,128)(2,1)}, bf16[80,1280]{1,0:T(8,128)(2,1)S(1)}, u32[]{:S(2)}, u32[]{:S(2)}) %collective-permute-start.12) | collective-permute-done | bytes 204832 | tf_op jit(solution)/shard_map/ppermute | solution.py:360
  152.9 7.4 %collective-permute-start.14 = (bf16[24,1280]{1,0:T(8,128)(2,1)}, bf16[24,1280]{1,0:T(8,128)(2,1)S(1)}, u32[]{:S(2)}, u32[]{:S(2)}) collective-permute-start(bf16[24,1280]{1,0:T(8,128)(2,1)} %get-tuple-element.54), channel_id=1, source_target_pairs={{0,0},{1,16},{2,2},{3,18},{4,4},{5,20},{6,6},{7,22},{8,1},{9,17},{... | collective-permute-start | bytes 184328 | tf_op jit(solution)/shard_map/ppermute | solution.py:370
  160.3 3.1 %collective-permute-start.15 = (bf16[24,1280]{1,0:T(8,128)(2,1)}, bf16[24,1280]{1,0:T(8,128)(2,1)S(1)}, u32[]{:S(2)}, u32[]{:S(2)}) collective-permute-start(bf16[24,1280]{1,0:T(8,128)(2,1)} %get-tuple-element.55), channel_id=1, source_target_pairs={{0,1},{1,17},{2,3},{3,19},{4,5},{5,21},{6,7},{7,23},{8,8},{9,24},{... | collective-permute-start | bytes 184328 | tf_op jit(solution)/shard_map/ppermute | solution.py:370
  163.5 2.4 %collective-permute-start.17 = (bf16[24,1280]{1,0:T(8,128)(2,1)}, bf16[24,1280]{1,0:T(8,128)(2,1)S(1)}, u32[]{:S(2)}, u32[]{:S(2)}) collective-permute-start(bf16[24,1280]{1,0:T(8,128)(2,1)} %get-tuple-element.57), channel_id=1, source_target_pairs={{0,9},{1,25},{2,11},{3,27},{4,13},{5,29},{6,15},{7,31},{8,0},{9,16... | collective-permute-start | bytes 184328 | tf_op jit(solution)/shard_map/ppermute | solution.py:370
  165.9 3.5 %collective-permute-done.16.c = bf16[24,1280]{1,0:T(8,128)(2,1)S(1)} collective-permute-done((bf16[24,1280]{1,0:T(8,128)(2,1)}, bf16[24,1280]{1,0:T(8,128)(2,1)S(1)}, u32[]{:S(2)}, u32[]{:S(2)}) %collective-permute-start.16) | collective-permute-done | bytes 61472 | tf_op jit(solution)/shard_map/ppermute | solution.py:370
  169.5 3.7 %collective-permute-done.17.d = bf16[24,1280]{1,0:T(8,128)(2,1)S(1)} collective-permute-done((bf16[24,1280]{1,0:T(8,128)(2,1)}, bf16[24,1280]{1,0:T(8,128)(2,1)S(1)}, u32[]{:S(2)}, u32[]{:S(2)}) %collective-permute-start.17) | collective-permute-done | bytes 61472 | tf_op jit(solution)/shard_map/ppermute | solution.py:370
  176.0 5.7 %all-to-all-start.2 = ((bf16[8,24,1280]{2,1,0:T(8,128)(2,1)}), bf16[8,24,1280]{2,1,0:T(8,128)(2,1)S(1)}, u32[]{:S(2)}, u32[]{:S(2)}) async-start(bf16[8,24,1280]{2,1,0:T(8,128)(2,1)} %sum_z.1), calls=%async_computation.2 | async-start | bytes 983040 | tf_op jit(solution)/shard_map/all_to_all | solution.py:526
  181.8 4.1 %unpack.1 = (bf16[2,96,1920]{2,1,0:T(8,128)(2,1)}, bf16[2,96,1920]{2,1,0:T(8,128)(2,1)}) custom-call(bf16[1152,640]{1,0:T(8,128)(2,1)} %bitcast.17, bf16[576,576]{1,0:T(8,128)(2,1)} %constant.71.clone.order), custom_call_target="tpu_custom_call" | custom-call | bytes 3612672 | tf_op jit(solution)/shard_map/unpack/pallas_call | solution.py:57
  185.9 2.4 %collective-permute-done.7.far = bf16[2,96,1920]{2,1,0:T(8,128)(2,1)S(1)} collective-permute-done((bf16[2,96,1920]{2,1,0:T(8,128)(2,1)}, bf16[2,96,1920]{2,1,0:T(8,128)(2,1)S(1)}, u32[]{:S(2)}, u32[]{:S(2)}) %collective-permute-start.7) | collective-permute-done | bytes 737312 | tf_op jit(solution)/shard_map/ppermute | solution.py:345
  189.2 2.6 %merge.1.after = bf16[2,96,3840]{2,1,0:T(8,128)(2,1)} custom-call(s32[4]{0:T(128)} %pad_add_fusion.place, bf16[2,96,1920]{2,1,0:T(8,128)(2,1)} %get-tuple-element.44.mine, bf16[2,96,1920]{2,1,0:T(8,128)(2,1)} %copy-done.4), custom_call_target="tpu_custom_call" | custom-call | bytes 2949136 | tf_op jit(solution)/shard_map/merge/pallas_call | solution.py:57
  (76 shorter events, 24.6 us)
Async XLA Ops:
  3.6 5.3 %collective-permute-start.5 = (bf16[2,96,1920]{2,1,0:T(8,128)(2,1)}, bf16[2,96,1920]{2,1,0:T(8,128)(2,1)S(1)}, u32[]{:S(2)}, u32[]{:S(2)}) collective-permute-start(bf16[2,96,1920]{2,1,0:T(8,128)(2,1)} %far.1), channel_id=1, source_target_pairs={{0,1},{1,0},{2,3},{3,2},{4,5},{5,4},{6,7},{7,6},{8,9},{9,8},{10,11... | collective-permute-start | bytes 2211848 | tf_op jit(solution)/shard_map/ppermute | solution.py:345
  14.2 9.3 %copy-start.5 = (bf16[1,2,96,1280]{3,2,1,0:T(8,128)(2,1)S(1)}, bf16[1,2,96,1280]{3,2,1,0:T(8,128)(2,1)}, u32[]{:S(2)}) copy-start(bf16[1,2,96,1280]{3,2,1,0:T(8,128)(2,1)} %param.16) | copy-start | bytes 1474564
  14.2 54.8 %all-to-all-start = ((bf16[16,96,640]{2,1,0:T(8,128)(2,1)}), bf16[16,96,640]{2,1,0:T(8,128)(2,1)S(1)}, u32[]{:S(2)}, u32[]{:S(2)}) async-start(bf16[16,96,640]{2,1,0:T(8,128)(2,1)} %bitcast.18), calls=%async_computation | async-start | bytes 3932160 | tf_op jit(solution)/shard_map/all_to_all | solution.py:377
  23.5 13.6 %collective-permute-start.1 = (bf16[192,1280]{1,0:T(8,128)(2,1)S(1)}, bf16[192,1280]{1,0:T(8,128)(2,1)S(1)}, u32[]{:S(2)}, u32[]{:S(2)}) collective-permute-start(bf16[192,1280]{1,0:T(8,128)(2,1)S(1)} %bitcast.27), channel_id=1, source_target_pairs={{0,1},{1,0},{2,3},{3,2},{4,5},{5,4},{6,7},{7,6},{8,9},{9,8},{10,11... | collective-permute-start | bytes 1474568 | tf_op jit(solution)/shard_map/ppermute | solution.py:345
  35.4 1.7 collective-permute-start
  41.7 30.7 %collective-permute-start.2 = (bf16[160,1280]{1,0:T(8,128)(2,1)}, bf16[160,1280]{1,0:T(8,128)(2,1)S(1)}, u32[]{:S(2)}, u32[]{:S(2)}) collective-permute-start(bf16[160,1280]{1,0:T(8,128)(2,1)} %get-tuple-element.36), channel_id=1, source_target_pairs={{0,32},{32,64},{64,96},{96,0},{128,160},{160,192},{192,224},{224,1... | collective-permute-start | bytes 1228808 | tf_op jit(solution)/shard_map/ppermute | solution.py:350
  42.9 29.4 %collective-permute-start.3 = (bf16[160,1280]{1,0:T(8,128)(2,1)}, bf16[160,1280]{1,0:T(8,128)(2,1)S(1)}, u32[]{:S(2)}, u32[]{:S(2)}) collective-permute-start(bf16[160,1280]{1,0:T(8,128)(2,1)} %get-tuple-element.37), channel_id=1, source_target_pairs={{0,64},{32,96},{64,0},{96,32},{128,192},{160,224},{192,128},{224,1... | collective-permute-start | bytes 1228808 | tf_op jit(solution)/shard_map/ppermute | solution.py:350
  45.3 27.0 %collective-permute-start.4 = (bf16[160,1280]{1,0:T(8,128)(2,1)}, bf16[160,1280]{1,0:T(8,128)(2,1)S(1)}, u32[]{:S(2)}, u32[]{:S(2)}) collective-permute-start(bf16[160,1280]{1,0:T(8,128)(2,1)} %get-tuple-element.38), channel_id=1, source_target_pairs={{0,96},{32,0},{64,32},{96,64},{128,224},{160,128},{192,160},{224,1... | collective-permute-start | bytes 1228808 | tf_op jit(solution)/shard_map/ppermute | solution.py:350
  69.0 7.0 %copy-start.1 = (bf16[16,96,640]{2,1,0:T(8,128)(2,1)}, bf16[16,96,640]{2,1,0:T(8,128)(2,1)S(1)}, u32[]{:S(2)}) copy-start(bf16[16,96,640]{2,1,0:T(8,128)(2,1)S(1)} %all-to-all-done) | copy-start | bytes 5898244
  69.0 13.3 %collective-permute-start.6 = (bf16[16,24,640]{2,1,0:T(8,128)(2,1)S(1)}, bf16[16,24,640]{2,1,0:T(8,128)(2,1)S(1)}, u32[]{:S(2)}, u32[]{:S(2)}) collective-permute-start(bf16[16,24,640]{2,1,0:T(8,128)(2,1)S(1)} %slice.4), channel_id=1, source_target_pairs={{0,1},{1,0},{2,3},{3,2},{4,5},{5,4},{6,7},{7,6},{8,9},{9,8},{10,11... | collective-permute-start | bytes 1474568 | tf_op jit(solution)/shard_map/ppermute | solution.py:345
  100.5 5.9 %copy-start.23 = (bf16[160,1280]{1,0:T(8,128)(2,1)S(1)}, bf16[160,1280]{1,0:T(8,128)(2,1)}, u32[]{:S(2)}) copy-start(bf16[160,1280]{1,0:T(8,128)(2,1)} %get-tuple-element.49) | copy-start | bytes 1228804
  100.5 7.5 %copy-start.22 = (bf16[160,1280]{1,0:T(8,128)(2,1)S(1)}, bf16[160,1280]{1,0:T(8,128)(2,1)}, u32[]{:S(2)}) copy-start(bf16[160,1280]{1,0:T(8,128)(2,1)} %get-tuple-element.47) | copy-start | bytes 1228804
  100.5 7.5 %copy-start.21 = (bf16[160,1280]{1,0:T(8,128)(2,1)S(1)}, bf16[160,1280]{1,0:T(8,128)(2,1)}, u32[]{:S(2)}) copy-start(bf16[160,1280]{1,0:T(8,128)(2,1)} %get-tuple-element.48) | copy-start | bytes 1228804
  100.5 72.6 %all-to-all-start.1 = ((bf16[16,72,640]{2,1,0:T(8,128)(2,1)}), bf16[16,72,640]{2,1,0:T(8,128)(2,1)S(1)}, u32[]{:S(2)}, u32[]{:S(2)}) async-start(bf16[16,72,640]{2,1,0:T(8,128)(2,1)} %bitcast.22), calls=%async_computation.1 | async-start | bytes 2949120 | tf_op jit(solution)/shard_map/all_to_all | solution.py:377
  106.4 10.5 %collective-permute-start.10 = (bf16[160,1280]{1,0:T(8,128)(2,1)S(1)}, bf16[160,1280]{1,0:T(8,128)(2,1)S(1)}, u32[]{:S(2)}, u32[]{:S(2)}) collective-permute-start(bf16[160,1280]{1,0:T(8,128)(2,1)S(1)} %copy-done.23), channel_id=1, source_target_pairs={{0,96},{32,0},{64,32},{96,64},{128,224},{160,128},{192,160},{224,1... | collective-permute-start | bytes 1228808 | tf_op jit(solution)/shard_map/ppermute | solution.py:350
  108.1 11.5 %collective-permute-start.8 = (bf16[160,1280]{1,0:T(8,128)(2,1)S(1)}, bf16[160,1280]{1,0:T(8,128)(2,1)S(1)}, u32[]{:S(2)}, u32[]{:S(2)}) collective-permute-start(bf16[160,1280]{1,0:T(8,128)(2,1)S(1)} %copy-done.22), channel_id=1, source_target_pairs={{0,32},{32,64},{64,96},{96,0},{128,160},{160,192},{192,224},{224,1... | collective-permute-start | bytes 1228808 | tf_op jit(solution)/shard_map/ppermute | solution.py:350
  108.1 20.0 %collective-permute-start.9 = (bf16[160,1280]{1,0:T(8,128)(2,1)S(1)}, bf16[160,1280]{1,0:T(8,128)(2,1)S(1)}, u32[]{:S(2)}, u32[]{:S(2)}) collective-permute-start(bf16[160,1280]{1,0:T(8,128)(2,1)S(1)} %copy-done.21), channel_id=1, source_target_pairs={{0,64},{32,96},{64,0},{96,32},{128,192},{160,224},{192,128},{224,1... | collective-permute-start | bytes 1228808 | tf_op jit(solution)/shard_map/ppermute | solution.py:350
  117.0 11.1 %copy-start.8 = (bf16[160,1280]{1,0:T(8,128)(2,1)}, bf16[160,1280]{1,0:T(8,128)(2,1)S(1)}, u32[]{:S(2)}) copy-start(bf16[160,1280]{1,0:T(8,128)(2,1)S(1)} %collective-permute-done.10.c) | copy-start | bytes 1228804
  119.5 8.6 %copy-start.10 = (bf16[160,1280]{1,0:T(8,128)(2,1)}, bf16[160,1280]{1,0:T(8,128)(2,1)S(1)}, u32[]{:S(2)}) copy-start(bf16[160,1280]{1,0:T(8,128)(2,1)S(1)} %collective-permute-done.8.a) | copy-start | bytes 1228804
  131.6 12.5 %collective-permute-start.11 = (bf16[80,1280]{1,0:T(8,128)(2,1)}, bf16[80,1280]{1,0:T(8,128)(2,1)S(1)}, u32[]{:S(2)}, u32[]{:S(2)}) collective-permute-start(bf16[80,1280]{1,0:T(8,128)(2,1)} %get-tuple-element.51), channel_id=1, source_target_pairs={{0,2},{1,3},{2,4},{3,5},{4,6},{5,7},{6,0},{7,1},{8,10},{9,11},{10,... | collective-permute-start | bytes 614408 | tf_op jit(solution)/shard_map/ppermute | solution.py:360
  132.7 15.8 %collective-permute-start.12 = (bf16[80,1280]{1,0:T(8,128)(2,1)}, bf16[80,1280]{1,0:T(8,128)(2,1)S(1)}, u32[]{:S(2)}, u32[]{:S(2)}) collective-permute-start(bf16[80,1280]{1,0:T(8,128)(2,1)} %get-tuple-element.52), channel_id=1, source_target_pairs={{0,4},{1,5},{2,6},{3,7},{4,0},{5,1},{6,2},{7,3},{8,12},{9,13},{10,... | collective-permute-start | bytes 614408 | tf_op jit(solution)/shard_map/ppermute | solution.py:360
  135.1 15.2 %collective-permute-start.13 = (bf16[80,1280]{1,0:T(8,128)(2,1)}, bf16[80,1280]{1,0:T(8,128)(2,1)S(1)}, u32[]{:S(2)}, u32[]{:S(2)}) collective-permute-start(bf16[80,1280]{1,0:T(8,128)(2,1)} %get-tuple-element.53), channel_id=1, source_target_pairs={{0,6},{1,7},{2,0},{3,1},{4,2},{5,3},{6,4},{7,5},{8,14},{9,15},{10,... | collective-permute-start | bytes 614408 | tf_op jit(solution)/shard_map/ppermute | solution.py:360
  144.1 6.1 %copy-start.12 = (bf16[80,1280]{1,0:T(8,128)(2,1)}, bf16[80,1280]{1,0:T(8,128)(2,1)S(1)}, u32[]{:S(2)}) copy-start(bf16[80,1280]{1,0:T(8,128)(2,1)S(1)} %collective-permute-done.11.a) | copy-start | bytes 614404
  152.9 13.0 %collective-permute-start.14 = (bf16[24,1280]{1,0:T(8,128)(2,1)}, bf16[24,1280]{1,0:T(8,128)(2,1)S(1)}, u32[]{:S(2)}, u32[]{:S(2)}) collective-permute-start(bf16[24,1280]{1,0:T(8,128)(2,1)} %get-tuple-element.54), channel_id=1, source_target_pairs={{0,0},{1,16},{2,2},{3,18},{4,4},{5,20},{6,6},{7,22},{8,1},{9,17},{... | collective-permute-start | bytes 184328 | tf_op jit(solution)/shard_map/ppermute | solution.py:370
  160.3 5.6 %collective-permute-start.15 = (bf16[24,1280]{1,0:T(8,128)(2,1)}, bf16[24,1280]{1,0:T(8,128)(2,1)S(1)}, u32[]{:S(2)}, u32[]{:S(2)}) collective-permute-start(bf16[24,1280]{1,0:T(8,128)(2,1)} %get-tuple-element.55), channel_id=1, source_target_pairs={{0,1},{1,17},{2,3},{3,19},{4,5},{5,21},{6,7},{7,23},{8,8},{9,24},{... | collective-permute-start | bytes 184328 | tf_op jit(solution)/shard_map/ppermute | solution.py:370
  163.4 6.0 %collective-permute-start.16 = (bf16[24,1280]{1,0:T(8,128)(2,1)}, bf16[24,1280]{1,0:T(8,128)(2,1)S(1)}, u32[]{:S(2)}, u32[]{:S(2)}) collective-permute-start(bf16[24,1280]{1,0:T(8,128)(2,1)} %get-tuple-element.56), channel_id=1, source_target_pairs={{0,8},{1,24},{2,10},{3,26},{4,12},{5,28},{6,14},{7,30},{8,9},{9,25... | collective-permute-start | bytes 184328 | tf_op jit(solution)/shard_map/ppermute | solution.py:370
  163.5 9.7 %collective-permute-start.17 = (bf16[24,1280]{1,0:T(8,128)(2,1)}, bf16[24,1280]{1,0:T(8,128)(2,1)S(1)}, u32[]{:S(2)}, u32[]{:S(2)}) collective-permute-start(bf16[24,1280]{1,0:T(8,128)(2,1)} %get-tuple-element.57), channel_id=1, source_target_pairs={{0,9},{1,25},{2,11},{3,27},{4,13},{5,29},{6,15},{7,31},{8,0},{9,16... | collective-permute-start | bytes 184328 | tf_op jit(solution)/shard_map/ppermute | solution.py:370
  165.9 7.3 %copy-start.15 = (bf16[24,1280]{1,0:T(8,128)(2,1)}, bf16[24,1280]{1,0:T(8,128)(2,1)S(1)}, u32[]{:S(2)}) copy-start(bf16[24,1280]{1,0:T(8,128)(2,1)S(1)} %collective-permute-done.14.a) | copy-start | bytes 184324
  165.9 7.3 %copy-start.16 = (bf16[24,1280]{1,0:T(8,128)(2,1)}, bf16[24,1280]{1,0:T(8,128)(2,1)S(1)}, u32[]{:S(2)}) copy-start(bf16[24,1280]{1,0:T(8,128)(2,1)S(1)} %collective-permute-done.15.b) | copy-start | bytes 184324
  169.5 3.7 %copy-start.17 = (bf16[24,1280]{1,0:T(8,128)(2,1)}, bf16[24,1280]{1,0:T(8,128)(2,1)S(1)}, u32[]{:S(2)}) copy-start(bf16[24,1280]{1,0:T(8,128)(2,1)S(1)} %collective-permute-done.16.c) | copy-start | bytes 184324
  176.0 15.8 %all-to-all-start.2 = ((bf16[8,24,1280]{2,1,0:T(8,128)(2,1)}), bf16[8,24,1280]{2,1,0:T(8,128)(2,1)S(1)}, u32[]{:S(2)}, u32[]{:S(2)}) async-start(bf16[8,24,1280]{2,1,0:T(8,128)(2,1)} %sum_z.1), calls=%async_computation.2 | async-start | bytes 983040 | tf_op jit(solution)/shard_map/all_to_all | solution.py:526
  185.9 2.4 %collective-permute-start.7 = (bf16[2,96,1920]{2,1,0:T(8,128)(2,1)}, bf16[2,96,1920]{2,1,0:T(8,128)(2,1)S(1)}, u32[]{:S(2)}, u32[]{:S(2)}) collective-permute-start(bf16[2,96,1920]{2,1,0:T(8,128)(2,1)} %get-tuple-element.45), channel_id=1, source_target_pairs={{0,1},{1,0},{2,3},{3,2},{4,5},{5,4},{6,7},{7,6},{8,9},{9,8},{10,11... | collective-permute-start | bytes 2211848 | tf_op jit(solution)/shard_map/ppermute | solution.py:345
  (14 other events, 12.6 us)

commit v5 on v4

--- a/solution.py
+++ b/solution.py
@@ -10,7 +10,7 @@
 
 WC = 16
 HW = 160
-VMEM_LIMIT = 56 * 1024 * 1024
+VMEM_LIMIT = 20 * 1024 * 1024
 BF16 = jnp.bfloat16
 F32 = jnp.float32
 
@@ -86,38 +86,50 @@
     return jnp.concatenate(tiles, axis=1)
 
 
-def probabilities(q, k, masks, bias=None):
+def windows(x):
+    return [x[:, 128 * h : 128 * h + 256] for h in range(4)]
+
+
+def head_rows(x):
+    n = x.shape[0] // 4
+    return [x[n * h : n * h + n] for h in range(4)]
+
+
+def against(a, b, masks):
+    parts = [dot_nt(x * m, y) for x, y, m in zip(windows(a), windows(b), masks)]
+    return jnp.concatenate(parts, axis=0)
+
+
+def probabilities(scores):
+    weights = jnp.exp(scores - jnp.max(scores, axis=-1, keepdims=True))
+    return weights / jnp.sum(weights, axis=-1, keepdims=True)
+
+
+def stacked(parts):
+    return jnp.concatenate(parts, axis=0)
+
+
+def score_gradients(probs, grad_probs):
+    inner = jnp.sum(probs * grad_probs, axis=-1, keepdims=True)
+    return (probs * (grad_probs - inner)).astype(BF16)
+
+
+def mixture(low, v):
+    parts = [dot_nn(p, x) for p, x in zip(head_rows(low), windows(v))]
+    return side_by_side(parts).astype(BF16)
+
+
+def gradients(low, grad_scores, q, k, g):
     scaling = HW ** (-0.5)
-    probs = []
-    for h in range(4):
-        win = slice(128 * h, 128 * h + 256)
-        scores = dot_nt(q[:, win] * masks[h], k[:, win]) * scaling
-        if bias is not None:
-            scores = scores + bias(h)
-        weights = jnp.exp(scores - jnp.max(scores, axis=-1, keepdims=True))
-        probs.append(weights / jnp.sum(weights, axis=-1, keepdims=True))
-    return probs
-
-
-def mixture(probs, v):
-    parts = [
-        dot_nn(probs[h].astype(BF16), v[:, 128 * h : 128 * h + 256]) for h in range(4)
+    low, grad_scores = head_rows(low), head_rows(grad_scores)
+    dv = [dot_tn(p, x) for p, x in zip(low, windows(g))]
+    dq = [dot_nn(p, x) for p, x in zip(grad_scores, windows(k))]
+    dk = [dot_tn(p, x) for p, x in zip(grad_scores, windows(q))]
+    return [
+        (side_by_side(dq) * scaling).astype(BF16),
+        (side_by_side(dk) * scaling).astype(BF16),
+        side_by_side(dv).astype(BF16),
     ]
-    return side_by_side(parts).astype(BF16)
-
-
-def gradients(probs, q, k, v, g, masks):
-    scaling = HW ** (-0.5)
-    dq, dk, dv = [], [], []
-    for h in range(4):
-        win = slice(128 * h, 128 * h + 256)
-        grad_probs = dot_nt(g[:, win] * masks[h], v[:, win])
-        inner = jnp.sum(probs[h] * grad_probs, axis=-1, keepdims=True)
-        grad_scores = (probs[h] * (grad_probs - inner)).astype(BF16)
-        dq.append(dot_nn(grad_scores, k[:, win]) * scaling)
-        dk.append(dot_tn(grad_scores, q[:, win]) * scaling)
-        dv.append(dot_tn(probs[h].astype(BF16), g[:, win]))
-    return [side_by_side(x).astype(BF16) for x in (dq, dk, dv)]
 
 
 def row_order(place):
@@ -194,28 +206,42 @@
     masks = head_masks()
     flat = jnp.concatenate([cot[0], cot[1]], axis=0)
     g = dot_nt(flat, weight[...]).astype(BF16)
+    distances = []
     for w in range(2):
         spread = jnp.broadcast_to(positions[w : w + 1, :], (96, 96))
         spread_t = spread.astype(F32).T.astype(jnp.int32)
-        distance = (
-            jnp.abs((spread >> 4) - (spread_t >> 4)) + jnp.abs((spread & 15) - (spread_t & 15))
-        ).astype(F32)
-        for half in range(2):
-            lanes = slice(640 * half, 640 * half + 640)
-            q, k, v = [
-                qkv[w, :, 1280 * s + 640 * half : 1280 * s + 640 * half + 640] for s in range(3)
-            ]
-            probs = probabilities(q, k, masks, lambda h: -(slopes[4 * half + h] * distance))
-            act_all[96 * w : 96 * w + 96, lanes] = mixture(probs, v)
-            grads = gradients(probs, q, k, v, g[96 * w : 96 * w + 96, lanes], masks)
-            for s, part in enumerate(grads):
-                d_out[w, :, 1280 * s + 640 * half : 1280 * s + 640 * half + 640] = part
+        distances.append(
+            (
+                jnp.abs((spread >> 4) - (spread_t >> 4)) + jnp.abs((spread & 15) - (spread_t & 15))
+            ).astype(F32)
+        )
+    parts = [(w, half) for w in range(2) for half in range(2)]
+
+    def section(s):
+        return [
+            qkv[w, :, 1280 * s + 640 * half : 1280 * s + 640 * half + 640] for w, half in parts
+        ]
+
+    q, k, v = section(0), section(1), section(2)
+    g = [g[96 * w : 96 * w + 96, 640 * half : 640 * half + 640] for w, half in parts]
+    bias = stacked([slopes[4 * half + h] * distances[w] for w, half in parts for h in range(4)])
+    scores = stacked([against(a, b, masks) for a, b in zip(q, k)]) * HW ** (-0.5) - bias
+    grad_probs = stacked([against(a, b, masks) for a, b in zip(g, v)])
+    probs = probabilities(scores)
+    low = probs.astype(BF16)
+    grad_scores = score_gradients(probs, grad_probs)
+    for i, (w, half) in enumerate(parts):
+        rows = slice(384 * i, 384 * i + 384)
+        lanes = slice(640 * half, 640 * half + 640)
+        act_all[96 * w : 96 * w + 96, lanes] = mixture(low[rows], v[i])
+        for s, part in enumerate(gradients(low[rows], grad_scores[rows], q[i], k[i], g[i])):
+            d_out[w, :, 1280 * s + 640 * half : 1280 * s + 640 * half + 640] = part
     hot = row_hot(place)
     act_own[...] = dot_nn(act_all[:, lanes_of(0, place[3])], hot).astype(BF16)
     act_other[...] = dot_nn(act_all[:, lanes_of(0, 1 - place[3])], hot).astype(BF16)
 
 
-def group_kernel(place, after, got, order, data, cot, probs_out, act, act_all):
+def group_kernel(place, after, after_too, after_three, got, order, data, cot, probs_out, act, act_all):
     masks = head_masks()
     hot = order[...]
     for group in range(2):
@@ -235,15 +261,20 @@
                             cot[to, 640 * o : 640 * o + 640] = piece
                         else:
                             data[2 * part + s, o, to, :] = piece
+    def section(s):
+        return [
+            stacked([data[s, 0, 32 * t : 32 * t + 32, :], data[s, 1, 32 * t : 32 * t + 32, :]])
+            for t in range(6)
+        ]
+
+    q, k, v = section(0), section(1), section(2)
+    probs = probabilities(
+        stacked([against(a, b, masks) for a, b in zip(q, k)]) * HW ** (-0.5)
+    )
+    probs_out[...] = probs
+    low = probs.astype(BF16)
     for t in range(6):
-        rows = slice(32 * t, 32 * t + 32)
-        q, k, v = [
-            jnp.concatenate([data[s, 0, rows, :], data[s, 1, rows, :]], axis=0) for s in range(3)
-        ]
-        probs = probabilities(q, k, masks)
-        for h in range(4):
-            probs_out[4 * t + h] = probs[h]
-        mixed = mixture(probs, v)
+        mixed = mixture(low[256 * t : 256 * t + 256], v[t])
         act_all[32 * t : 32 * t + 32, :] = mixed[:32]
         act_all[192 + 32 * t : 192 + 32 * t + 32, :] = mixed[32:]
     act[...] = dot_nn(act_all[...], row_hot(place)).astype(BF16)
@@ -255,14 +286,24 @@
     own_rows = weight[pl.ds(pl.multiple_of(640 * place[3], 128), 640), :]
     g_own = dot_nt(cot[...], own_rows).astype(BF16)
     g_far = dot_nt(cot_far[...], own_rows).astype(BF16)
+    def section(s):
+        return [
+            stacked([data[s, 0, 32 * t : 32 * t + 32, :], data[s, 1, 32 * t : 32 * t + 32, :]])
+            for t in range(6)
+        ]
+
+    q, k, v = section(0), section(1), section(2)
+    g = [
+        stacked([g_own[32 * t : 32 * t + 32], g_far[32 * t : 32 * t + 32]]) for t in range(6)
+    ]
+    probs = probs_in[...]
+    low = probs.astype(BF16)
+    grad_scores = score_gradients(
+        probs, stacked([against(a, b, masks) for a, b in zip(g, v)])
+    )
     for t in range(6):
-        rows = slice(32 * t, 32 * t + 32)
-        q, k, v = [
-            jnp.concatenate([data[s, 0, rows, :], data[s, 1, rows, :]], axis=0) for s in range(3)
-        ]
-        g = jnp.concatenate([g_own[rows], g_far[rows]], axis=0)
-        probs = [probs_in[4 * t + h] for h in range(4)]
-        for s, part in enumerate(gradients(probs, q, k, v, g, masks)):
+        rows, stack = slice(32 * t, 32 * t + 32), slice(256 * t, 256 * t + 256)
+        for s, part in enumerate(gradients(low[stack], grad_scores[stack], q[t], k[t], g[t])):
             grads[s, 0, rows, :] = part[:32]
             grads[s, 1, rows, :] = part[32:]
     for group in range(2):
@@ -303,15 +344,11 @@
     return total
 
 
-def local_sum_kernel(own, a, b, c, total):
-    total[...] = sum_of(own, a, b, c)
-
-
-def sum_x_kernel(local, own, a, b, c, kept, one, two, three):
-    total = sum_of(own, a, b, c)
-    for d, ref in enumerate((kept, one, two, three)):
+def sum_x_kernel(*refs):
+    local, total, chunks = sum_of(*refs[:4]), sum_of(*refs[4:8]), refs[8:]
+    for d, ref in enumerate(chunks):
         rows = slice(40 * d, 40 * d + 40)
-        ref[:40, :] = local[rows, :].astype(ref.dtype)
+        ref[:40, :] = local[rows].astype(ref.dtype)
         ref[40:, :] = total[rows].astype(ref.dtype)
 
 
@@ -432,15 +469,7 @@
         flops=2 * 640 * 384 * 1280,
         name="local_weight",
     )
-    (local_rows,) = call(
-        local_sum_kernel,
-        [sds((160, 1280), F32)],
-        own,
-        along_x(one, 1),
-        along_x(two, 2),
-        along_x(three, 3),
-        name="local_sum_x",
-    )
+    local_parts = [own, along_x(one, 1), along_x(two, 2), along_x(three, 3)]
 
     got_far = swap_cores(got.reshape(16, 96, 640)[:, 72:, :]).reshape(384, 640)
     data, cot, probs, act = call(
@@ -448,15 +477,15 @@
         [
             sds((3, 2, 192, 640), BF16),
             sds((192, 1280), BF16),
-            sds((24, 64, 64), F32),
+            sds((1536, 64), F32),
             sds((384, 640), BF16),
         ],
         place,
-        local_rows,
+        *local_parts[1:],
         got,
         jnp.asarray(GROUP, BF16),
         smem=(0,),
-        unread=(1,),
+        unread=(1, 2, 3),
         scratch=[pltpu.VMEM((384, 640), BF16)],
         flops=10**9,
         name="group",
@@ -492,11 +521,12 @@
     own, one, two, three = call(
         sum_x_kernel,
         [sds((80, 1280), F32)] + [sds((80, 1280), BF16)] * 3,
-        local_rows,
+        *local_parts,
         own,
         a,
         b,
         c,
+        flops=10**11,
         name="sum_x",
     )
     chunks = call(

time: 195 us -> 163 us (0.84)
  Pallas kernels: 62.9 us -> 27.9 us
  local copies, waits for them, and re-layouts: 7.87 us -> 12.1 us
    pallas_call x14 -> x13, Pallas kernels: 62.9 us -> 27.9 us  [call(): pl.pallas_call(kernel, out_shape=outs, in_specs=specs, out_specs=[pl.Bloc...]
    ppermute x6, waiting for transfers between devices: 17.5 us -> 8.66 us  [along_x(): return lax.ppermute(a, 'dp', pairs)]
    all_to_all x2, waiting for transfers between devices: 22.5 us -> 27.5 us  [exchange(): lax.all_to_all(a, 'tok', split_axis=0, concat_axis=0, axis_index_groups=C...]
    unnamed x50 -> x36, local copies, waits for them, and re-layouts: 7.82 us -> 12.1 us
    all_to_all x1, waiting for transfers between devices: 0.01 us -> 3.1 us  [per_device(): pieces = lax.all_to_all(sums, 'dp', split_axis=0, concat_axis=0, tiled=True)]
  transfers between devices with their start and end apart: 21 -> 21, of which waited for: 12 -> 12; matrix products, arithmetic and copies ran while one was open for 0% -> 0% of each run, Pallas kernels for 18% -> 12%
where the time goes in v5:
time: 163 us; the launch traced here: 162 us
  waiting for transfers between devices  66.4 us (41%)
  starting transfers between devices  54.6 us (33%)
  Pallas kernels  27.9 us (17%)
  local copies, waits for them, and re-layouts  12.1 us (7%)
    pallas_call x13, Pallas kernels, call(): pl.pallas_call(kernel, out_shape=outs, in_specs=specs, out_specs=[pl.Bloc...  27.9 us
    all_to_all x2, waiting for transfers between devices, exchange(): lax.all_to_all(a, 'tok', split_axis=0, concat_axis=0, axis_index_groups=C...  27.5 us
    all_to_all x2, starting transfers between devices, exchange(): lax.all_to_all(a, 'tok', split_axis=0, concat_axis=0, axis_index_groups=C...  15.1 us
    ppermute x3, waiting for transfers between devices, along_y(): return lax.ppermute(a, 'tok', pairs)  14.6 us
    ppermute x4, starting transfers between devices, to_owner(): return lax.ppermute(a, 'tok', pairs)  12.4 us
    unnamed x36, local copies, waits for them, and re-layouts  12.1 us
    ppermute x6, starting transfers between devices, along_x(): return lax.ppermute(a, 'dp', pairs)  8.79 us
    ppermute x6, waiting for transfers between devices, along_x(): return lax.ppermute(a, 'dp', pairs)  8.66 us
  transfers between devices with their start and end apart: 21, of which 12 were waited for; matrix products, arithmetic and copies ran while one was open for 0% of the time, Pallas kernels for 12%

profile of v5, /device:TPU:1, one launch (start us, length us, event | category | flops | bytes accessed | tf_op | source)
XLA Modules:
  0.0 161.9 jit_solution(15560203344969291063)
XLA Ops:
  2.7 3.3 %collective-permute-start.5 = (bf16[2,96,1920]{2,1,0:T(8,128)(2,1)S(1)}, bf16[2,96,1920]{2,1,0:T(8,128)(2,1)S(1)}, u32[]{:S(2)}, u32[]{:S(2)}) collective-permute-start(bf16[2,96,1920]{2,1,0:T(8,128)(2,1)S(1)} %far.1), channel_id=1, source_target_pairs={{0,1},{1,0},{2,3},{3,2},{4,5},{5,4},{6,7},{7,6},{8,9},{9,8},{10,11... | collective-permute-start | bytes 2211848 | tf_op jit(solution)/shard_map/ppermute | solution.py:382
  6.1 1.8 %collective-permute-done.5.far = bf16[2,96,1920]{2,1,0:T(8,128)(2,1)S(1)} collective-permute-done((bf16[2,96,1920]{2,1,0:T(8,128)(2,1)S(1)}, bf16[2,96,1920]{2,1,0:T(8,128)(2,1)S(1)}, u32[]{:S(2)}, u32[]{:S(2)}) %collective-permute-start.5) | collective-permute-done | bytes 737312 | tf_op jit(solution)/shard_map/ppermute | solution.py:382
  8.9 3.1 %pack.1 = bf16[1536,640]{1,0:T(8,128)(2,1)} custom-call(s32[4]{0:T(128)S(1)} %pad_add_fusion.place, bf16[2,96,3840]{2,1,0:T(8,128)(2,1)S(1)} %bitcast.19, bf16[2,96,1920]{2,1,0:T(8,128)(2,1)S(1)} %collective-permute-done.5.far, bf16[2,96,1280]{2,1,0:T(8,128)(2,1)S(1)} %bitcast.22, bf16[384,384]{1,0:T(8,128)(2,1)S(1)} %copy-done.7), custom_call_target="tpu_custom_call" | custom-call | bytes 4964368 | tf_op jit(solution)/shard_map/pack/pallas_call | solution.py:57
  12.0 9.3 %all-to-all-start = ((bf16[16,96,640]{2,1,0:T(8,128)(2,1)}), bf16[16,96,640]{2,1,0:T(8,128)(2,1)S(1)}, u32[]{:S(2)}, u32[]{:S(2)}) async-start(bf16[16,96,640]{2,1,0:T(8,128)(2,1)} %bitcast.10), calls=%async_computation | async-start | bytes 3932160 | tf_op jit(solution)/shard_map/all_to_all | solution.py:414
  22.1 1.9 %copy-done.8 = bf16[1280,1280]{1,0:T(8,128)(2,1)S(1)} copy-done((bf16[1280,1280]{1,0:T(8,128)(2,1)S(1)}, bf16[1280,1280]{1,0:T(8,128)(2,1)}, u32[]{:S(2)}) %copy-start.8) | copy-done | bytes 3276824
  25.4 4.8 %local.1 = (bf16[2,96,3840]{2,1,0:T(8,128)(2,1)}, bf16[192,640]{1,0:T(8,128)(2,1)S(1)}, bf16[192,640]{1,0:T(8,128)(2,1)S(1)}) custom-call(s32[4]{0:T(128)S(1)} %pad_add_fusion.place, f32[8]{0:T(128)S(1)} %copy-done.11, bf16[2,96,3840]{2,1,0:T(8,128)(2,1)S(1)} %bitcast.26, bf16[2,96,1280]{2,1,0:T(8,128)(2,1)S(1)} %bitcast.24, ...), custom_call_target="tpu_custom_call" | custom-call | flops 2000000000 | bytes 7209776 | tf_op jit(solution)/shard_map/local/pallas_call | solution.py:57
  31.7 2.0 %local_weight.1 = (f32[160,1280]{1,0:T(8,128)S(1)}, bf16[160,1280]{1,0:T(8,128)(2,1)}, bf16[160,1280]{1,0:T(8,128)(2,1)}, bf16[160,1280]{1,0:T(8,128)(2,1)}) custom-call(bf16[192,640]{1,0:T(8,128)(2,1)S(1)} %get-tuple-element.33.act, bf16[192,640]{1,0:T(8,128)(2,1)S(1)} %collective-permute-done.act_far, bf16[192,1280]{1,0:T(8,128)(2,1)S(1)} %bitcast.25, ...), custom_call_target="tpu_custom_call" | custom-call | flops 629145600 | bytes 3522560 | tf_op jit(solution)/shard_map/local_weight/pallas_call | solution.py:57
  35.8 2.4 %collective-permute-start.3 = (bf16[160,1280]{1,0:T(8,128)(2,1)}, bf16[160,1280]{1,0:T(8,128)(2,1)S(1)}, u32[]{:S(2)}, u32[]{:S(2)}) collective-permute-start(bf16[160,1280]{1,0:T(8,128)(2,1)} %get-tuple-element.36), channel_id=1, source_target_pairs={{0,64},{32,96},{64,0},{96,32},{128,192},{160,224},{192,128},{224,1... | collective-permute-start | bytes 1228808 | tf_op jit(solution)/shard_map/ppermute | solution.py:387
  39.4 27.5 %all-to-all-done = bf16[16,96,640]{2,1,0:T(8,128)(2,1)S(1)} async-done(((bf16[16,96,640]{2,1,0:T(8,128)(2,1)}), bf16[16,96,640]{2,1,0:T(8,128)(2,1)S(1)}, u32[]{:S(2)}, u32[]{:S(2)}) %all-to-all-start) | async-done | bytes 1966112 | tf_op jit(solution)/shard_map/all_to_all | solution.py:414
  67.0 3.4 %collective-permute-start.6 = (bf16[16,24,640]{2,1,0:T(8,128)(2,1)S(1)}, bf16[16,24,640]{2,1,0:T(8,128)(2,1)S(1)}, u32[]{:S(2)}, u32[]{:S(2)}) collective-permute-start(bf16[16,24,640]{2,1,0:T(8,128)(2,1)S(1)} %slice.4), channel_id=1, source_target_pairs={{0,1},{1,0},{2,3},{3,2},{4,5},{5,4},{6,7},{7,6},{8,9},{9,8},{10,11... | collective-permute-start | bytes 1474568 | tf_op jit(solution)/shard_map/ppermute | solution.py:382
  71.3 3.1 %group.1 = (bf16[3,2,192,640]{3,2,1,0:T(8,128)(2,1)S(1)}, bf16[192,1280]{1,0:T(8,128)(2,1)S(1)}, f32[1536,64]{1,0:T(8,128)S(1)}, bf16[384,640]{1,0:T(8,128)(2,1)S(1)}) custom-call(s32[4]{0:T(128)S(1)} %pad_add_fusion.place, bf16[160,1280]{1,0:T(8,128)(2,1)S(1)} %collective-permute-done.2.after.refs_1_, ...), custom_call_target="tpu_custom_call" | custom-call | flops 1000000000 | bytes 6340624 | tf_op jit(solution)/shard_map/group/pallas_call | solution.py:57
  74.5 2.3 %group_weight.1 = (f32[160,1280]{1,0:T(8,128)S(1)}, bf16[160,1280]{1,0:T(8,128)(2,1)}, bf16[160,1280]{1,0:T(8,128)(2,1)}, bf16[160,1280]{1,0:T(8,128)(2,1)}, bf16[192,1280]{1,0:T(8,128)(2,1)S(1)}) custom-call(bf16[384,640]{1,0:T(8,128)(2,1)S(1)} %get-tuple-element.41.act, bf16[192,1280]{1,0:T(8,128)(2,1)S(1)} %get-tuple-element.40.cot, ...), custom_call_target="tpu_custom_call" | custom-call | flops 629145600 | bytes 4308992 | tf_op jit(solution)/shard_map/group_weight/pallas_call | solution.py:57
  77.7 2.8 %collective-permute-start.10 = (bf16[160,1280]{1,0:T(8,128)(2,1)}, bf16[160,1280]{1,0:T(8,128)(2,1)S(1)}, u32[]{:S(2)}, u32[]{:S(2)}) collective-permute-start(bf16[160,1280]{1,0:T(8,128)(2,1)} %get-tuple-element.49), channel_id=1, source_target_pairs={{0,96},{32,0},{64,32},{96,64},{128,224},{160,128},{192,160},{224,1... | collective-permute-start | bytes 1228808 | tf_op jit(solution)/shard_map/ppermute | solution.py:387
  81.6 5.4 %group_back.1 = bf16[1152,640]{1,0:T(8,128)(2,1)} custom-call(s32[4]{0:T(128)S(1)} %pad_add_fusion.place, f32[1536,64]{1,0:T(8,128)S(1)} %get-tuple-element.38.probs_in, bf16[3,2,192,640]{3,2,1,0:T(8,128)(2,1)S(1)} %get-tuple-element.39.data, bf16[192,1280]{1,0:T(8,128)(2,1)S(1)} %get-tuple-element.40.cot, bf16[192,1280]{1,0:T(8,128)(2,1)S(1)} %get-tuple-element.42.cot_far, ...), custom_call_target="tpu_custom_call" | custom-call | flops 2000000000 | bytes 8265744 | tf_op jit(solution)/shard_map/group_back/pallas_call | solution.py:57
  87.1 5.8 %all-to-all-start.1 = ((bf16[16,72,640]{2,1,0:T(8,128)(2,1)}), bf16[16,72,640]{2,1,0:T(8,128)(2,1)S(1)}, u32[]{:S(2)}, u32[]{:S(2)}) async-start(bf16[16,72,640]{2,1,0:T(8,128)(2,1)} %bitcast.13), calls=%async_computation.1 | async-start | bytes 2949120 | tf_op jit(solution)/shard_map/all_to_all | solution.py:414
  92.9 5.4 %collective-permute-done.10.refs_7_ = bf16[160,1280]{1,0:T(8,128)(2,1)S(1)} collective-permute-done((bf16[160,1280]{1,0:T(8,128)(2,1)}, bf16[160,1280]{1,0:T(8,128)(2,1)S(1)}, u32[]{:S(2)}, u32[]{:S(2)}) %collective-permute-start.10) | collective-permute-done | bytes 409632 | tf_op jit(solution)/shard_map/ppermute | solution.py:387
  98.3 3.2 %collective-permute-done.8.refs_5_ = bf16[160,1280]{1,0:T(8,128)(2,1)} collective-permute-done((bf16[160,1280]{1,0:T(8,128)(2,1)}, bf16[160,1280]{1,0:T(8,128)(2,1)}, u32[]{:S(2)}, u32[]{:S(2)}) %collective-permute-start.8) | collective-permute-done | bytes 409632 | tf_op jit(solution)/shard_map/ppermute | solution.py:387
  103.8 1.5 sum_x.1
  105.6 2.4 %collective-permute-start.12 = (bf16[80,1280]{1,0:T(8,128)(2,1)S(1)}, bf16[80,1280]{1,0:T(8,128)(2,1)S(1)}, u32[]{:S(2)}, u32[]{:S(2)}) collective-permute-start(bf16[80,1280]{1,0:T(8,128)(2,1)S(1)} %get-tuple-element.52), channel_id=1, source_target_pairs={{0,4},{1,5},{2,6},{3,7},{4,0},{5,1},{6,2},{7,3},{8,12},{9,13},{10,... | collective-permute-start | bytes 614408 | tf_op jit(solution)/shard_map/ppermute | solution.py:397
  108.0 2.0 %collective-permute-start.13 = (bf16[80,1280]{1,0:T(8,128)(2,1)S(1)}, bf16[80,1280]{1,0:T(8,128)(2,1)S(1)}, u32[]{:S(2)}, u32[]{:S(2)}) collective-permute-start(bf16[80,1280]{1,0:T(8,128)(2,1)S(1)} %get-tuple-element.53), channel_id=1, source_target_pairs={{0,6},{1,7},{2,0},{3,1},{4,2},{5,3},{6,4},{7,5},{8,14},{9,15},{10,... | collective-permute-start | bytes 614408 | tf_op jit(solution)/shard_map/ppermute | solution.py:397
  110.0 5.2 %collective-permute-done.11.a = bf16[80,1280]{1,0:T(8,128)(2,1)S(1)} collective-permute-done((bf16[80,1280]{1,0:T(8,128)(2,1)S(1)}, bf16[80,1280]{1,0:T(8,128)(2,1)S(1)}, u32[]{:S(2)}, u32[]{:S(2)}) %collective-permute-start.11) | collective-permute-done | bytes 204832 | tf_op jit(solution)/shard_map/ppermute | solution.py:397
  115.2 4.3 %collective-permute-done.12.b = bf16[80,1280]{1,0:T(8,128)(2,1)S(1)} collective-permute-done((bf16[80,1280]{1,0:T(8,128)(2,1)S(1)}, bf16[80,1280]{1,0:T(8,128)(2,1)S(1)}, u32[]{:S(2)}, u32[]{:S(2)}) %collective-permute-start.12) | collective-permute-done | bytes 204832 | tf_op jit(solution)/shard_map/ppermute | solution.py:397
  119.5 5.1 %collective-permute-done.13.c = bf16[80,1280]{1,0:T(8,128)(2,1)S(1)} collective-permute-done((bf16[80,1280]{1,0:T(8,128)(2,1)S(1)}, bf16[80,1280]{1,0:T(8,128)(2,1)S(1)}, u32[]{:S(2)}, u32[]{:S(2)}) %collective-permute-start.13) | collective-permute-done | bytes 204832 | tf_op jit(solution)/shard_map/ppermute | solution.py:397
  124.7 6.0 %collective-permute-start.14 = (bf16[24,1280]{1,0:T(8,128)(2,1)S(1)}, bf16[24,1280]{1,0:T(8,128)(2,1)S(1)}, u32[]{:S(2)}, u32[]{:S(2)}) collective-permute-start(bf16[24,1280]{1,0:T(8,128)(2,1)S(1)} %get-tuple-element.54), channel_id=1, source_target_pairs={{0,0},{1,16},{2,2},{3,18},{4,4},{5,20},{6,6},{7,22},{8,1},{9,17},{... | collective-permute-start | bytes 184328 | tf_op jit(solution)/shard_map/ppermute | solution.py:407
  130.8 3.8 %collective-permute-start.15 = (bf16[24,1280]{1,0:T(8,128)(2,1)S(1)}, bf16[24,1280]{1,0:T(8,128)(2,1)S(1)}, u32[]{:S(2)}, u32[]{:S(2)}) collective-permute-start(bf16[24,1280]{1,0:T(8,128)(2,1)S(1)} %get-tuple-element.55), channel_id=1, source_target_pairs={{0,1},{1,17},{2,3},{3,19},{4,5},{5,21},{6,7},{7,23},{8,8},{9,24},{... | collective-permute-start | bytes 184328 | tf_op jit(solution)/shard_map/ppermute | solution.py:407
  134.7 2.4 %collective-permute-start.17 = (bf16[24,1280]{1,0:T(8,128)(2,1)S(1)}, bf16[24,1280]{1,0:T(8,128)(2,1)S(1)}, u32[]{:S(2)}, u32[]{:S(2)}) collective-permute-start(bf16[24,1280]{1,0:T(8,128)(2,1)S(1)} %get-tuple-element.57), channel_id=1, source_target_pairs={{0,9},{1,25},{2,11},{3,27},{4,13},{5,29},{6,15},{7,31},{8,0},{9,16... | collective-permute-start | bytes 184328 | tf_op jit(solution)/shard_map/ppermute | solution.py:407
  137.1 4.0 %collective-permute-done.16.c = bf16[24,1280]{1,0:T(8,128)(2,1)S(1)} collective-permute-done((bf16[24,1280]{1,0:T(8,128)(2,1)S(1)}, bf16[24,1280]{1,0:T(8,128)(2,1)S(1)}, u32[]{:S(2)}, u32[]{:S(2)}) %collective-permute-start.16) | collective-permute-done | bytes 61472 | tf_op jit(solution)/shard_map/ppermute | solution.py:407
  141.2 2.9 %collective-permute-done.17.d = bf16[24,1280]{1,0:T(8,128)(2,1)S(1)} collective-permute-done((bf16[24,1280]{1,0:T(8,128)(2,1)S(1)}, bf16[24,1280]{1,0:T(8,128)(2,1)S(1)}, u32[]{:S(2)}, u32[]{:S(2)}) %collective-permute-start.17) | collective-permute-done | bytes 61472 | tf_op jit(solution)/shard_map/ppermute | solution.py:407
  144.9 6.1 %all-to-all-start.2 = ((bf16[8,24,1280]{2,1,0:T(8,128)(2,1)}), bf16[8,24,1280]{2,1,0:T(8,128)(2,1)S(1)}, u32[]{:S(2)}, u32[]{:S(2)}) async-start(bf16[8,24,1280]{2,1,0:T(8,128)(2,1)} %sum_z.1), calls=%async_computation.2 | async-start | bytes 983040 | tf_op jit(solution)/shard_map/all_to_all | solution.py:556
  152.6 2.2 %collective-permute-done.7.far = bf16[2,96,1920]{2,1,0:T(8,128)(2,1)S(1)} collective-permute-done((bf16[2,96,1920]{2,1,0:T(8,128)(2,1)S(1)}, bf16[2,96,1920]{2,1,0:T(8,128)(2,1)S(1)}, u32[]{:S(2)}, u32[]{:S(2)}) %collective-permute-start.7) | collective-permute-done | bytes 737312 | tf_op jit(solution)/shard_map/ppermute | solution.py:382
  154.8 1.8 %merge.1.after = bf16[2,96,3840]{2,1,0:T(8,128)(2,1)} custom-call(s32[4]{0:T(128)S(1)} %pad_add_fusion.place, bf16[2,96,1920]{2,1,0:T(8,128)(2,1)S(1)} %get-tuple-element.43.mine, bf16[2,96,1920]{2,1,0:T(8,128)(2,1)S(1)} %collective-permute-done.7.far), custom_call_target="tpu_custom_call" | custom-call | bytes 2949136 | tf_op jit(solution)/shard_map/merge/pallas_call | solution.py:57
  156.6 3.1 %all-to-all-done.2.pieces = bf16[8,24,1280]{2,1,0:T(8,128)(2,1)S(1)} async-done(((bf16[8,24,1280]{2,1,0:T(8,128)(2,1)}), bf16[8,24,1280]{2,1,0:T(8,128)(2,1)S(1)}, u32[]{:S(2)}, u32[]{:S(2)}) %all-to-all-start.2) | async-done | bytes 491552 | tf_op jit(solution)/shard_map/all_to_all | solution.py:556
  (61 shorter events, 20.5 us)
Async XLA Ops:
  0.8 1.4 copy-start
  2.1 5.8 %copy-start.1 = (bf16[1,2,96,3840]{3,2,1,0:T(8,128)(2,1)S(1)}, bf16[1,2,96,3840]{3,2,1,0:T(8,128)(2,1)}, u32[]{:S(2)}) copy-start(bf16[1,2,96,3840]{3,2,1,0:T(8,128)(2,1)} %param.13) | copy-start | bytes 4423684
  2.1 5.8 %copy-start.6 = (bf16[1,2,96,1280]{3,2,1,0:T(8,128)(2,1)S(1)}, bf16[1,2,96,1280]{3,2,1,0:T(8,128)(2,1)}, u32[]{:S(2)}) copy-start(bf16[1,2,96,1280]{3,2,1,0:T(8,128)(2,1)} %param.16) | copy-start | bytes 1474564
  2.7 5.2 %collective-permute-start.5 = (bf16[2,96,1920]{2,1,0:T(8,128)(2,1)S(1)}, bf16[2,96,1920]{2,1,0:T(8,128)(2,1)S(1)}, u32[]{:S(2)}, u32[]{:S(2)}) collective-permute-start(bf16[2,96,1920]{2,1,0:T(8,128)(2,1)S(1)} %far.1), channel_id=1, source_target_pairs={{0,1},{1,0},{2,3},{3,2},{4,5},{5,4},{6,7},{7,6},{8,9},{9,8},{10,11... | collective-permute-start | bytes 2211848 | tf_op jit(solution)/shard_map/ppermute | solution.py:382
  12.0 10.1 %copy-start.10 = (s32[1,2,96]{2,1,0:T(2,128)S(1)}, s32[1,2,96]{2,1,0:T(2,128)}, u32[]{:S(2)}) copy-start(s32[1,2,96]{2,1,0:T(2,128)} %param.14) | copy-start | bytes 2308
  12.0 10.1 %copy-start.11 = (f32[8]{0:T(128)S(1)}, f32[8]{0:T(128)}, u32[]{:S(2)}) copy-start(f32[8]{0:T(128)} %slopes.1) | copy-start | bytes 100
  12.0 54.9 %all-to-all-start = ((bf16[16,96,640]{2,1,0:T(8,128)(2,1)}), bf16[16,96,640]{2,1,0:T(8,128)(2,1)S(1)}, u32[]{:S(2)}, u32[]{:S(2)}) async-start(bf16[16,96,640]{2,1,0:T(8,128)(2,1)} %bitcast.10), calls=%async_computation | async-start | bytes 3932160 | tf_op jit(solution)/shard_map/all_to_all | solution.py:414
  21.3 10.3 %collective-permute-start.1 = (bf16[192,1280]{1,0:T(8,128)(2,1)S(1)}, bf16[192,1280]{1,0:T(8,128)(2,1)S(1)}, u32[]{:S(2)}, u32[]{:S(2)}) collective-permute-start(bf16[192,1280]{1,0:T(8,128)(2,1)S(1)} %bitcast.23), channel_id=1, source_target_pairs={{0,1},{1,0},{2,3},{3,2},{4,5},{5,4},{6,7},{7,6},{8,9},{9,8},{10,11... | collective-permute-start | bytes 1474568 | tf_op jit(solution)/shard_map/ppermute | solution.py:382
  22.1 1.9 %copy-start.8 = (bf16[1280,1280]{1,0:T(8,128)(2,1)S(1)}, bf16[1280,1280]{1,0:T(8,128)(2,1)}, u32[]{:S(2)}) copy-start(bf16[1280,1280]{1,0:T(8,128)(2,1)} %weight.2) | copy-start | bytes 9830404
  30.1 1.5 collective-permute-start
  34.6 35.8 %collective-permute-start.2 = (bf16[160,1280]{1,0:T(8,128)(2,1)}, bf16[160,1280]{1,0:T(8,128)(2,1)S(1)}, u32[]{:S(2)}, u32[]{:S(2)}) collective-permute-start(bf16[160,1280]{1,0:T(8,128)(2,1)} %get-tuple-element.35), channel_id=1, source_target_pairs={{0,32},{32,64},{64,96},{96,0},{128,160},{160,192},{192,224},{224,1... | collective-permute-start | bytes 1228808 | tf_op jit(solution)/shard_map/ppermute | solution.py:387
  35.8 34.6 %collective-permute-start.3 = (bf16[160,1280]{1,0:T(8,128)(2,1)}, bf16[160,1280]{1,0:T(8,128)(2,1)S(1)}, u32[]{:S(2)}, u32[]{:S(2)}) collective-permute-start(bf16[160,1280]{1,0:T(8,128)(2,1)} %get-tuple-element.36), channel_id=1, source_target_pairs={{0,64},{32,96},{64,0},{96,32},{128,192},{160,224},{192,128},{224,1... | collective-permute-start | bytes 1228808 | tf_op jit(solution)/shard_map/ppermute | solution.py:387
  38.2 32.1 %collective-permute-start.4 = (bf16[160,1280]{1,0:T(8,128)(2,1)}, bf16[160,1280]{1,0:T(8,128)(2,1)S(1)}, u32[]{:S(2)}, u32[]{:S(2)}) collective-permute-start(bf16[160,1280]{1,0:T(8,128)(2,1)} %get-tuple-element.37), channel_id=1, source_target_pairs={{0,96},{32,0},{64,32},{96,64},{128,224},{160,128},{192,160},{224,1... | collective-permute-start | bytes 1228808 | tf_op jit(solution)/shard_map/ppermute | solution.py:387
  67.0 7.5 %collective-permute-start.6 = (bf16[16,24,640]{2,1,0:T(8,128)(2,1)S(1)}, bf16[16,24,640]{2,1,0:T(8,128)(2,1)S(1)}, u32[]{:S(2)}, u32[]{:S(2)}) collective-permute-start(bf16[16,24,640]{2,1,0:T(8,128)(2,1)S(1)} %slice.4), channel_id=1, source_target_pairs={{0,1},{1,0},{2,3},{3,2},{4,5},{5,4},{6,7},{7,6},{8,9},{9,8},{10,11... | collective-permute-start | bytes 1474568 | tf_op jit(solution)/shard_map/ppermute | solution.py:382
  71.3 3.2 %copy-start.12 = (bf16[384,384]{1,0:T(8,128)(2,1)S(1)}, bf16[384,384]{1,0:T(8,128)(2,1)}, u32[]{:S(2)}) copy-start(bf16[384,384]{1,0:T(8,128)(2,1)} %constant.69.clone.order) | copy-start | bytes 884740
  71.3 10.3 %copy-start.3 = (bf16[1280,1280]{1,0:T(8,128)(2,1)S(1)}, bf16[1280,1280]{1,0:T(8,128)(2,1)}, u32[]{:S(2)}) copy-start(bf16[1280,1280]{1,0:T(8,128)(2,1)} %weight.3) | copy-start | bytes 9830404
  74.4 7.2 %copy-start.5 = (bf16[576,576]{1,0:T(8,128)(2,1)S(1)}, bf16[576,576]{1,0:T(8,128)(2,1)}, u32[]{:S(2)}) copy-start(bf16[576,576]{1,0:T(8,128)(2,1)} %constant.70.clone.order) | copy-start | bytes 1990660
  77.7 20.6 %collective-permute-start.10 = (bf16[160,1280]{1,0:T(8,128)(2,1)}, bf16[160,1280]{1,0:T(8,128)(2,1)S(1)}, u32[]{:S(2)}, u32[]{:S(2)}) collective-permute-start(bf16[160,1280]{1,0:T(8,128)(2,1)} %get-tuple-element.49), channel_id=1, source_target_pairs={{0,96},{32,0},{64,32},{96,64},{128,224},{160,128},{192,160},{224,1... | collective-permute-start | bytes 1228808 | tf_op jit(solution)/shard_map/ppermute | solution.py:387
  80.4 21.1 %collective-permute-start.8 = (bf16[160,1280]{1,0:T(8,128)(2,1)}, bf16[160,1280]{1,0:T(8,128)(2,1)}, u32[]{:S(2)}, u32[]{:S(2)}) collective-permute-start(bf16[160,1280]{1,0:T(8,128)(2,1)} %get-tuple-element.47), channel_id=1, source_target_pairs={{0,32},{32,64},{64,96},{96,0},{128,160},{160,192},{192,224},{224,1... | collective-permute-start | bytes 1228808 | tf_op jit(solution)/shard_map/ppermute | solution.py:387
  80.5 21.1 %collective-permute-start.9 = (bf16[160,1280]{1,0:T(8,128)(2,1)}, bf16[160,1280]{1,0:T(8,128)(2,1)}, u32[]{:S(2)}, u32[]{:S(2)}) collective-permute-start(bf16[160,1280]{1,0:T(8,128)(2,1)} %get-tuple-element.48), channel_id=1, source_target_pairs={{0,64},{32,96},{64,0},{96,32},{128,192},{160,224},{192,128},{224,1... | collective-permute-start | bytes 1228808 | tf_op jit(solution)/shard_map/ppermute | solution.py:387
  87.1 57.0 %all-to-all-start.1 = ((bf16[16,72,640]{2,1,0:T(8,128)(2,1)}), bf16[16,72,640]{2,1,0:T(8,128)(2,1)S(1)}, u32[]{:S(2)}, u32[]{:S(2)}) async-start(bf16[16,72,640]{2,1,0:T(8,128)(2,1)} %bitcast.13), calls=%async_computation.1 | async-start | bytes 2949120 | tf_op jit(solution)/shard_map/all_to_all | solution.py:414
  105.3 9.9 %collective-permute-start.11 = (bf16[80,1280]{1,0:T(8,128)(2,1)S(1)}, bf16[80,1280]{1,0:T(8,128)(2,1)S(1)}, u32[]{:S(2)}, u32[]{:S(2)}) collective-permute-start(bf16[80,1280]{1,0:T(8,128)(2,1)S(1)} %get-tuple-element.51), channel_id=1, source_target_pairs={{0,2},{1,3},{2,4},{3,5},{4,6},{5,7},{6,0},{7,1},{8,10},{9,11},{10,... | collective-permute-start | bytes 614408 | tf_op jit(solution)/shard_map/ppermute | solution.py:397
  105.6 13.9 %collective-permute-start.12 = (bf16[80,1280]{1,0:T(8,128)(2,1)S(1)}, bf16[80,1280]{1,0:T(8,128)(2,1)S(1)}, u32[]{:S(2)}, u32[]{:S(2)}) collective-permute-start(bf16[80,1280]{1,0:T(8,128)(2,1)S(1)} %get-tuple-element.52), channel_id=1, source_target_pairs={{0,4},{1,5},{2,6},{3,7},{4,0},{5,1},{6,2},{7,3},{8,12},{9,13},{10,... | collective-permute-start | bytes 614408 | tf_op jit(solution)/shard_map/ppermute | solution.py:397
  108.0 16.6 %collective-permute-start.13 = (bf16[80,1280]{1,0:T(8,128)(2,1)S(1)}, bf16[80,1280]{1,0:T(8,128)(2,1)S(1)}, u32[]{:S(2)}, u32[]{:S(2)}) collective-permute-start(bf16[80,1280]{1,0:T(8,128)(2,1)S(1)} %get-tuple-element.53), channel_id=1, source_target_pairs={{0,6},{1,7},{2,0},{3,1},{4,2},{5,3},{6,4},{7,5},{8,14},{9,15},{10,... | collective-permute-start | bytes 614408 | tf_op jit(solution)/shard_map/ppermute | solution.py:397
  124.7 12.4 %collective-permute-start.14 = (bf16[24,1280]{1,0:T(8,128)(2,1)S(1)}, bf16[24,1280]{1,0:T(8,128)(2,1)S(1)}, u32[]{:S(2)}, u32[]{:S(2)}) collective-permute-start(bf16[24,1280]{1,0:T(8,128)(2,1)S(1)} %get-tuple-element.54), channel_id=1, source_target_pairs={{0,0},{1,16},{2,2},{3,18},{4,4},{5,20},{6,6},{7,22},{8,1},{9,17},{... | collective-permute-start | bytes 184328 | tf_op jit(solution)/shard_map/ppermute | solution.py:407
  130.8 6.3 %collective-permute-start.15 = (bf16[24,1280]{1,0:T(8,128)(2,1)S(1)}, bf16[24,1280]{1,0:T(8,128)(2,1)S(1)}, u32[]{:S(2)}, u32[]{:S(2)}) collective-permute-start(bf16[24,1280]{1,0:T(8,128)(2,1)S(1)} %get-tuple-element.55), channel_id=1, source_target_pairs={{0,1},{1,17},{2,3},{3,19},{4,5},{5,21},{6,7},{7,23},{8,8},{9,24},{... | collective-permute-start | bytes 184328 | tf_op jit(solution)/shard_map/ppermute | solution.py:407
  134.6 6.6 %collective-permute-start.16 = (bf16[24,1280]{1,0:T(8,128)(2,1)S(1)}, bf16[24,1280]{1,0:T(8,128)(2,1)S(1)}, u32[]{:S(2)}, u32[]{:S(2)}) collective-permute-start(bf16[24,1280]{1,0:T(8,128)(2,1)S(1)} %get-tuple-element.56), channel_id=1, source_target_pairs={{0,8},{1,24},{2,10},{3,26},{4,12},{5,28},{6,14},{7,30},{8,9},{9,25... | collective-permute-start | bytes 184328 | tf_op jit(solution)/shard_map/ppermute | solution.py:407
  134.7 9.4 %collective-permute-start.17 = (bf16[24,1280]{1,0:T(8,128)(2,1)S(1)}, bf16[24,1280]{1,0:T(8,128)(2,1)S(1)}, u32[]{:S(2)}, u32[]{:S(2)}) collective-permute-start(bf16[24,1280]{1,0:T(8,128)(2,1)S(1)} %get-tuple-element.57), channel_id=1, source_target_pairs={{0,9},{1,25},{2,11},{3,27},{4,13},{5,29},{6,15},{7,31},{8,0},{9,16... | collective-permute-start | bytes 184328 | tf_op jit(solution)/shard_map/ppermute | solution.py:407
  144.1 6.9 %copy-start.4 = (bf16[576,576]{1,0:T(8,128)(2,1)S(1)}, bf16[576,576]{1,0:T(8,128)(2,1)}, u32[]{:S(2)}) copy-start(bf16[576,576]{1,0:T(8,128)(2,1)} %constant.71.clone.order) | copy-start | bytes 1990660
  144.9 14.7 %all-to-all-start.2 = ((bf16[8,24,1280]{2,1,0:T(8,128)(2,1)}), bf16[8,24,1280]{2,1,0:T(8,128)(2,1)S(1)}, u32[]{:S(2)}, u32[]{:S(2)}) async-start(bf16[8,24,1280]{2,1,0:T(8,128)(2,1)} %sum_z.1), calls=%async_computation.2 | async-start | bytes 983040 | tf_op jit(solution)/shard_map/all_to_all | solution.py:556
  152.5 2.3 %collective-permute-start.7 = (bf16[2,96,1920]{2,1,0:T(8,128)(2,1)S(1)}, bf16[2,96,1920]{2,1,0:T(8,128)(2,1)S(1)}, u32[]{:S(2)}, u32[]{:S(2)}) collective-permute-start(bf16[2,96,1920]{2,1,0:T(8,128)(2,1)S(1)} %get-tuple-element.44), channel_id=1, source_target_pairs={{0,1},{1,0},{2,3},{3,2},{4,5},{5,4},{6,7},{7,6},{8,9},{9,8},{10,11... | collective-permute-start | bytes 2211848 | tf_op jit(solution)/shard_map/ppermute | solution.py:382
  159.7 1.4 copy-start.2
  (7 other events, 7.4 us)

commit v6 on v5

--- a/solution.py
+++ b/solution.py
@@ -2,7 +2,6 @@
 
 import jax
 import jax.numpy as jnp
-import numpy as np
 from jax import lax
 from jax.experimental import pallas as pl
 from jax.experimental.pallas import tpu as pltpu
@@ -10,7 +9,7 @@
 
 WC = 16
 HW = 160
-VMEM_LIMIT = 20 * 1024 * 1024
+VMEM_LIMIT = 12 * 1024 * 1024
 BF16 = jnp.bfloat16
 F32 = jnp.float32
 
@@ -28,21 +27,26 @@
 
 
 def order_matrix(old, new):
-    sizes = dict(old)
-    count = int(np.prod(list(sizes.values())))
-    index = np.arange(count).reshape([s for _, s in old])
-    names = [n for n, _ in old]
-    moved = np.transpose(index, [names.index(n) for n in new]).reshape(-1)
-    hot = np.zeros((count, count), np.float32)
-    hot[np.arange(count), moved] = 1.0
-    return hot
-
-
-HOME = order_matrix([("s", 2), ("o", 2), ("w", 2), ("p", 8), ("t", 6)], ["p", "s", "o", "w", "t"])
-GROUP = order_matrix([("p", 8), ("s", 2), ("o", 2), ("w", 2), ("t", 6)], ["s", "o", "t", "p", "w"])
-FAR_COT = order_matrix([("p", 16), ("o", 2), ("w", 2), ("t", 6)], ["o", "t", "p", "w"])
-BACK = order_matrix([("s", 3), ("o", 2), ("t", 6), ("p", 8), ("w", 2)], ["p", "s", "o", "w", "t"])
-UNPACK = order_matrix([("p", 8), ("s", 3), ("o", 2), ("w", 2), ("t", 6)], ["s", "o", "w", "p", "t"])
+    count = 1
+    for _, size in old:
+        count *= size
+    left = lax.broadcasted_iota(jnp.int32, (8, count), 1).astype(F32)
+    digits = {}
+    for name, size in reversed(old):
+        whole = jnp.floor((left + 0.5) * (1.0 / size))
+        digits[name], left = left - whole * size, whole
+    place, sizes = jnp.zeros_like(left), dict(old)
+    for name in new:
+        place = place * sizes[name] + digits[name]
+    rows = lax.broadcasted_iota(jnp.int32, (count, count), 0)
+    return (rows == place.astype(jnp.int32)[:1]).astype(F32).astype(BF16)
+
+
+HOME = ([("s", 2), ("o", 2), ("w", 2), ("p", 8), ("t", 6)], ["p", "s", "o", "w", "t"])
+GROUP = ([("p", 8), ("s", 2), ("o", 2), ("w", 2), ("t", 6)], ["s", "o", "t", "p", "w"])
+FAR_COT = ([("p", 16), ("o", 2), ("w", 2), ("t", 6)], ["o", "t", "p", "w"])
+BACK = ([("s", 3), ("o", 2), ("t", 6), ("p", 8), ("w", 2)], ["p", "s", "o", "w", "t"])
+UNPACK = ([("p", 8), ("s", 3), ("o", 2), ("w", 2), ("t", 6)], ["s", "o", "w", "p", "t"])
 
 
 def call(kernel, outs, *args, smem=(), unread=(), scratch=(), flops=0, name=None):
@@ -52,8 +56,8 @@
         )
         for i in range(len(args))
     ]
-    size = sum(int(np.prod(a.shape)) * a.dtype.itemsize for a in args)
-    size += sum(int(np.prod(o.shape)) * o.dtype.itemsize for o in outs)
+    size = sum(a.size * a.dtype.itemsize for a in args)
+    size += sum(o.size * o.dtype.itemsize for o in outs)
     return pl.pallas_call(
         kernel,
         out_shape=outs,
@@ -132,7 +136,7 @@
     ]
 
 
-def row_order(place):
+def row_order(place, y_first):
     x, zh, y = place[0], place[1], place[2]
     rem = lax.broadcasted_iota(jnp.int32, (8, 640), 1)
 
@@ -142,15 +146,16 @@
             total = total + jnp.where(value >= k * size, 1, 0)
         return total, value - total * size
 
-    dx, rem = digit(rem, 160)
-    dy, rem = digit(rem, 40)
+    first, rem = digit(rem, 160)
+    second, rem = digit(rem, 40)
+    dx, dy = (second, first) if y_first else (first, second)
     df, rem = digit(rem, 10)
     to = (zh + df) & 3
     return (((to >> 1) * 4 + ((y + dy) & 3)) * 2 + (to & 1)) * 40 + ((x + dx) & 3) * 10 + rem
 
 
-def row_hot(place):
-    lane = row_order(place)[:1]
+def row_hot(place, y_first):
+    lane = row_order(place, y_first)[:1]
     rows = lax.broadcasted_iota(jnp.int32, (640, 640), 0)
     return (rows == lane).astype(F32).astype(BF16)
 
@@ -165,8 +170,8 @@
             out[w, :, 640 * s : 640 * s + 640] = qkv[w, :, lanes_of(s, 1 - place[3])]
 
 
-def pack_kernel(place, qkv, far, cot, order, out):
-    hot = order[...]
+def pack_kernel(place, qkv, far, cot, out):
+    hot = order_matrix(*HOME)
     for group in range(2):
         rows = slice(48 * group, 48 * group + 48)
 
@@ -182,8 +187,8 @@
                 out[start : start + 48, :] = sent[48 * p : 48 * p + 48, :]
 
 
-def unpack_kernel(got, order, mine, other):
-    hot = order[...]
+def unpack_kernel(got, mine, other):
+    hot = order_matrix(*UNPACK)
     for group in range(2):
         rows = dot_nn(hot, got[576 * group : 576 * group + 576, :]).astype(BF16)
         for s in range(3):
@@ -236,14 +241,14 @@
         act_all[96 * w : 96 * w + 96, lanes] = mixture(low[rows], v[i])
         for s, part in enumerate(gradients(low[rows], grad_scores[rows], q[i], k[i], g[i])):
             d_out[w, :, 1280 * s + 640 * half : 1280 * s + 640 * half + 640] = part
-    hot = row_hot(place)
+    hot = row_hot(place, False)
     act_own[...] = dot_nn(act_all[:, lanes_of(0, place[3])], hot).astype(BF16)
     act_other[...] = dot_nn(act_all[:, lanes_of(0, 1 - place[3])], hot).astype(BF16)
 
 
-def group_kernel(place, after, after_too, after_three, got, order, data, cot, probs_out, act, act_all):
+def group_kernel(place, after, after_too, after_three, got, data, cot, probs_out, act, act_all):
     masks = head_masks()
-    hot = order[...]
+    hot = order_matrix(*GROUP)
     for group in range(2):
         for part in range(2):
             pieces = [
@@ -277,12 +282,12 @@
         mixed = mixture(low[256 * t : 256 * t + 256], v[t])
         act_all[32 * t : 32 * t + 32, :] = mixed[:32]
         act_all[192 + 32 * t : 192 + 32 * t + 32, :] = mixed[32:]
-    act[...] = dot_nn(act_all[...], row_hot(place)).astype(BF16)
-
-
-def group_back_kernel(place, probs_in, data, cot, cot_far, weight, order, back, grads):
+    act[...] = dot_nn(act_all[...], row_hot(place, True)).astype(BF16)
+
+
+def group_back_kernel(place, probs_in, data, cot, cot_far, weight, back, grads):
     masks = head_masks()
-    hot = order[...]
+    hot = order_matrix(*BACK)
     own_rows = weight[pl.ds(pl.multiple_of(640 * place[3], 128), 640), :]
     g_own = dot_nt(cot[...], own_rows).astype(BF16)
     g_far = dot_nt(cot_far[...], own_rows).astype(BF16)
@@ -330,8 +335,8 @@
     weight_parts(act[...], act_far[...], cot, cot_far, own, one, two, three)
 
 
-def group_weight_kernel(act, cot, got_far, order, own, one, two, three, cot_far):
-    rows = dot_nn(order[...], got_far[...]).astype(BF16)
+def group_weight_kernel(act, cot, got_far, own, one, two, three, cot_far):
+    rows = dot_nn(order_matrix(*FAR_COT), got_far[...]).astype(BF16)
     cot_far[:, :640] = rows[:192]
     cot_far[:, 640:] = rows[192:]
     weight_parts(act[:192, :], act[192:, :], cot, cot_far, own, one, two, three)
@@ -344,20 +349,17 @@
     return total
 
 
-def sum_x_kernel(*refs):
+def first_sum_kernel(own, a, b, c, *chunks):
+    total = sum_of(own, a, b, c)
+    for d, ref in enumerate(chunks):
+        ref[...] = total[40 * d : 40 * d + 40].astype(ref.dtype)
+
+
+def second_sum_kernel(*refs):
     local, total, chunks = sum_of(*refs[:4]), sum_of(*refs[4:8]), refs[8:]
     for d, ref in enumerate(chunks):
-        rows = slice(40 * d, 40 * d + 40)
-        ref[:40, :] = local[rows].astype(ref.dtype)
-        ref[40:, :] = total[rows].astype(ref.dtype)
-
-
-def sum_y_kernel(own, a, b, c, *chunks):
-    total = sum_of(own, a, b, c)
-    for d, ref in enumerate(chunks):
-        first = total[10 * d : 10 * d + 10]
-        second = total[40 + 10 * d : 40 + 10 * d + 10]
-        both = jnp.concatenate([first, second, jnp.zeros((4, 1280), F32)], axis=0)
+        rows = slice(10 * d, 10 * d + 10)
+        both = jnp.concatenate([local[rows], total[rows], jnp.zeros((4, 1280), F32)], axis=0)
         ref[...] = both.astype(BF16)
 
 
@@ -426,6 +428,7 @@
     cotangent = cotangent.reshape(2, 96, 1280)
     flat_cot = cotangent.reshape(192, 1280)
     positions = positions.reshape(2, 96)
+    first_sums = [sds((40, 1280), F32)] + [sds((40, 1280), BF16)] * 3
     partials = [sds((160, 1280), F32)] + [sds((160, 1280), BF16)] * 3
 
     (other,) = call(
@@ -439,7 +442,6 @@
         qkv_global,
         far,
         cotangent,
-        jnp.asarray(HOME, BF16),
         smem=(0,),
         name="pack",
     )
@@ -469,7 +471,16 @@
         flops=2 * 640 * 384 * 1280,
         name="local_weight",
     )
-    local_parts = [own, along_x(one, 1), along_x(two, 2), along_x(three, 3)]
+    own, one, two, three = call(
+        first_sum_kernel,
+        first_sums,
+        own,
+        along_x(one, 1),
+        along_x(two, 2),
+        along_x(three, 3),
+        name="local_sum_x",
+    )
+    local_parts = [own, along_y(one, 1), along_y(two, 2), along_y(three, 3)]
 
     got_far = swap_cores(got.reshape(16, 96, 640)[:, 72:, :]).reshape(384, 640)
     data, cot, probs, act = call(
@@ -483,11 +494,10 @@
         place,
         *local_parts[1:],
         got,
-        jnp.asarray(GROUP, BF16),
         smem=(0,),
         unread=(1, 2, 3),
         scratch=[pltpu.VMEM((384, 640), BF16)],
-        flops=10**9,
+        flops=10**11,
         name="group",
     )
     own, one, two, three, cot_far = call(
@@ -496,11 +506,10 @@
         act,
         cot,
         got_far,
-        jnp.asarray(FAR_COT, BF16),
         flops=2 * 640 * 384 * 1280,
         name="group_weight",
     )
-    a, b, c = along_x(one, 1), along_x(two, 2), along_x(three, 3)
+    a, b, c = along_y(one, 1), along_y(two, 2), along_y(three, 3)
     (back,) = call(
         group_back_kernel,
         [sds((1152, 640), BF16)],
@@ -510,7 +519,6 @@
         cot,
         cot_far,
         w_out_global,
-        jnp.asarray(BACK, BF16),
         smem=(0,),
         scratch=[pltpu.VMEM((3, 2, 192, 640), BF16)],
         flops=2 * 10**9,
@@ -519,30 +527,29 @@
     returned = exchange(back)
 
     own, one, two, three = call(
-        sum_x_kernel,
-        [sds((80, 1280), F32)] + [sds((80, 1280), BF16)] * 3,
-        *local_parts,
+        first_sum_kernel,
+        first_sums,
         own,
         a,
         b,
         c,
         flops=10**11,
+        name="sum_y",
+    )
+    chunks = call(
+        second_sum_kernel,
+        [sds((24, 1280), BF16)] * 4,
+        *local_parts,
+        own,
+        along_x(one, 1),
+        along_x(two, 2),
+        along_x(three, 3),
         name="sum_x",
-    )
-    chunks = call(
-        sum_y_kernel,
-        [sds((24, 1280), BF16)] * 4,
-        own,
-        along_y(one, 1),
-        along_y(two, 2),
-        along_y(three, 3),
-        name="sum_y",
     )
     mine, other = call(
         unpack_kernel,
         [sds((2, 96, 1920), BF16)] * 2,
         returned,
-        jnp.asarray(UNPACK, BF16),
         name="unpack",
     )
     (sums,) = call(

time: 163 us -> 153 us (0.939)
  waiting for transfers between devices: 66.4 us -> 48.3 us
  starting transfers between devices: 54.6 us -> 69.1 us
  local copies, waits for them, and re-layouts: 12.1 us -> 7.26 us
    all_to_all x2, waiting for transfers between devices: 27.5 us -> 6.69 us  [exchange(): lax.all_to_all(a, 'tok', split_axis=0, concat_axis=0, axis_index_groups=C...]
    ppermute x4, starting transfers between devices: 12.4 us -> 23.3 us  [to_owner(): return lax.ppermute(a, 'tok', pairs)]
    ppermute x6, waiting for transfers between devices: 8.66 us -> 19.1 us  [along_x(): return lax.ppermute(a, 'dp', pairs)]
    ppermute x3 -> x6, waiting for transfers between devices: 14.6 us -> 7.07 us  [along_y(): return lax.ppermute(a, 'tok', pairs)]
    ppermute x3 -> x6, starting transfers between devices: 4.7 us -> 9.64 us  [along_y(): return lax.ppermute(a, 'tok', pairs)]
    unnamed x36 -> x22, local copies, waits for them, and re-layouts: 12.1 us -> 7.22 us
    all_to_all x1, starting transfers between devices: 6.09 us -> 3.48 us  [per_device(): pieces = lax.all_to_all(sums, 'dp', split_axis=0, concat_axis=0, tiled=True)]
    ppermute x6, starting transfers between devices: 8.79 us -> 11.1 us  [along_x(): return lax.ppermute(a, 'dp', pairs)]
  transfers between devices with their start and end apart: 21 -> 24, of which waited for: 12 -> 13; matrix products, arithmetic and copies ran while one was open for 0% -> 0% of each run, Pallas kernels for 12% -> 13%
where the time goes in v6:
time: 153 us; the launch traced here: 152 us
  starting transfers between devices  69.1 us (45%)
  waiting for transfers between devices  48.3 us (32%)
  Pallas kernels  26.7 us (17%)
  local copies, waits for them, and re-layouts  7.26 us (5%)
    pallas_call x14, Pallas kernels, call(): pl.pallas_call(kernel, out_shape=outs, in_specs=specs, out_specs=[pl.Bloc...  26.7 us
    ppermute x4, starting transfers between devices, to_owner(): return lax.ppermute(a, 'tok', pairs)  23.3 us
    ppermute x6, waiting for transfers between devices, along_x(): return lax.ppermute(a, 'dp', pairs)  19.1 us
    all_to_all x2, starting transfers between devices, exchange(): lax.all_to_all(a, 'tok', split_axis=0, concat_axis=0, axis_index_groups=C...  14.2 us
    ppermute x6, starting transfers between devices, along_x(): return lax.ppermute(a, 'dp', pairs)  11.1 us
    ppermute x6, starting transfers between devices, along_y(): return lax.ppermute(a, 'tok', pairs)  9.64 us
    ppermute x5, starting transfers between devices, swap_cores(): return lax.ppermute(a, 'tok', [(i, i ^ 1) for i in range(32)])  7.37 us
    ppermute x4, waiting for transfers between devices, to_owner(): return lax.ppermute(a, 'tok', pairs)  7.24 us
  transfers between devices with their start and end apart: 24, of which 13 were waited for; matrix products, arithmetic and copies ran while one was open for 0% of the time, Pallas kernels for 13%

profile of v6, /device:TPU:1, one launch (start us, length us, event | category | flops | bytes accessed | tf_op | source)
XLA Modules:
  0.0 152.3 jit_solution(9769039109309717520)
XLA Ops:
  2.7 3.3 %collective-permute-start.8 = (bf16[2,96,1920]{2,1,0:T(8,128)(2,1)S(1)}, bf16[2,96,1920]{2,1,0:T(8,128)(2,1)S(1)}, u32[]{:S(2)}, u32[]{:S(2)}) collective-permute-start(bf16[2,96,1920]{2,1,0:T(8,128)(2,1)S(1)} %far.1), channel_id=1, source_target_pairs={{0,1},{1,0},{2,3},{3,2},{4,5},{5,4},{6,7},{7,6},{8,9},{9,8},{10,11... | collective-permute-start | bytes 2211848 | tf_op jit(solution)/shard_map/ppermute | solution.py:384
  6.1 1.8 %collective-permute-done.8.far = bf16[2,96,1920]{2,1,0:T(8,128)(2,1)S(1)} collective-permute-done((bf16[2,96,1920]{2,1,0:T(8,128)(2,1)S(1)}, bf16[2,96,1920]{2,1,0:T(8,128)(2,1)S(1)}, u32[]{:S(2)}, u32[]{:S(2)}) %collective-permute-start.8) | collective-permute-done | bytes 737312 | tf_op jit(solution)/shard_map/ppermute | solution.py:384
  7.9 3.2 %pack.1 = bf16[1536,640]{1,0:T(8,128)(2,1)} custom-call(s32[4]{0:T(128)S(1)} %pad_add_fusion.place, bf16[2,96,3840]{2,1,0:T(8,128)(2,1)S(1)} %bitcast.19, bf16[2,96,1920]{2,1,0:T(8,128)(2,1)S(1)} %collective-permute-done.8.far, bf16[2,96,1280]{2,1,0:T(8,128)(2,1)S(1)} %bitcast.22), custom_call_target="tpu_custom_call" | custom-call | bytes 4669456 | tf_op jit(solution)/shard_map/pack/pallas_call | solution.py:61
  11.1 9.3 %all-to-all-start = ((bf16[16,96,640]{2,1,0:T(8,128)(2,1)}), bf16[16,96,640]{2,1,0:T(8,128)(2,1)S(1)}, u32[]{:S(2)}, u32[]{:S(2)}) async-start(bf16[16,96,640]{2,1,0:T(8,128)(2,1)} %bitcast.10), calls=%async_computation | async-start | bytes 3932160 | tf_op jit(solution)/shard_map/all_to_all | solution.py:416
  21.2 1.9 %copy-done.5 = bf16[1280,1280]{1,0:T(8,128)(2,1)S(1)} copy-done((bf16[1280,1280]{1,0:T(8,128)(2,1)S(1)}, bf16[1280,1280]{1,0:T(8,128)(2,1)}, u32[]{:S(2)}) %copy-start.5) | copy-done | bytes 3276824
  24.5 4.8 %local.1 = (bf16[2,96,3840]{2,1,0:T(8,128)(2,1)}, bf16[192,640]{1,0:T(8,128)(2,1)S(1)}, bf16[192,640]{1,0:T(8,128)(2,1)S(1)}) custom-call(s32[4]{0:T(128)S(1)} %pad_add_fusion.place, f32[8]{0:T(128)S(1)} %copy-done.8, bf16[2,96,3840]{2,1,0:T(8,128)(2,1)S(1)} %bitcast.26, bf16[2,96,1280]{2,1,0:T(8,128)(2,1)S(1)} %bitcast.24, ...), custom_call_target="tpu_custom_call" | custom-call | flops 2000000000 | bytes 7209776 | tf_op jit(solution)/shard_map/local/pallas_call | solution.py:61
  33.1 2.4 %collective-permute-start.3 = (bf16[160,1280]{1,0:T(8,128)(2,1)S(1)}, bf16[160,1280]{1,0:T(8,128)(2,1)S(1)}, u32[]{:S(2)}, u32[]{:S(2)}) collective-permute-start(bf16[160,1280]{1,0:T(8,128)(2,1)S(1)} %get-tuple-element.41), channel_id=1, source_target_pairs={{0,64},{32,96},{64,0},{96,32},{128,192},{160,224},{192,128},{224,1... | collective-permute-start | bytes 1228808 | tf_op jit(solution)/shard_map/ppermute | solution.py:389
  36.7 7.3 %collective-permute-done.2.a = bf16[160,1280]{1,0:T(8,128)(2,1)S(1)} collective-permute-done((bf16[160,1280]{1,0:T(8,128)(2,1)S(1)}, bf16[160,1280]{1,0:T(8,128)(2,1)S(1)}, u32[]{:S(2)}, u32[]{:S(2)}) %collective-permute-start.2) | collective-permute-done | bytes 409632 | tf_op jit(solution)/shard_map/ppermute | solution.py:389
  44.0 9.8 %collective-permute-done.3.b = bf16[160,1280]{1,0:T(8,128)(2,1)S(1)} collective-permute-done((bf16[160,1280]{1,0:T(8,128)(2,1)S(1)}, bf16[160,1280]{1,0:T(8,128)(2,1)S(1)}, u32[]{:S(2)}, u32[]{:S(2)}) %collective-permute-start.3) | collective-permute-done | bytes 409632 | tf_op jit(solution)/shard_map/ppermute | solution.py:389
  55.6 2.4 %collective-permute-start.6 = (bf16[40,1280]{1,0:T(8,128)(2,1)S(1)}, bf16[40,1280]{1,0:T(8,128)(2,1)S(1)}, u32[]{:S(2)}, u32[]{:S(2)}) collective-permute-start(bf16[40,1280]{1,0:T(8,128)(2,1)S(1)} %get-tuple-element.44), channel_id=1, source_target_pairs={{0,4},{1,5},{2,6},{3,7},{4,0},{5,1},{6,2},{7,3},{8,12},{9,13},{10,... | collective-permute-start | bytes 307208 | tf_op jit(solution)/shard_map/ppermute | solution.py:399
  59.2 6.7 %all-to-all-done = bf16[16,96,640]{2,1,0:T(8,128)(2,1)S(1)} async-done(((bf16[16,96,640]{2,1,0:T(8,128)(2,1)}), bf16[16,96,640]{2,1,0:T(8,128)(2,1)S(1)}, u32[]{:S(2)}, u32[]{:S(2)}) %all-to-all-start) | async-done | bytes 1966112 | tf_op jit(solution)/shard_map/all_to_all | solution.py:416
  65.9 3.2 %collective-permute-start.9 = (bf16[16,24,640]{2,1,0:T(8,128)(2,1)S(1)}, bf16[16,24,640]{2,1,0:T(8,128)(2,1)S(1)}, u32[]{:S(2)}, u32[]{:S(2)}) collective-permute-start(bf16[16,24,640]{2,1,0:T(8,128)(2,1)S(1)} %slice.4), channel_id=1, source_target_pairs={{0,1},{1,0},{2,3},{3,2},{4,5},{5,4},{6,7},{7,6},{8,9},{9,8},{10,11... | collective-permute-start | bytes 1474568 | tf_op jit(solution)/shard_map/ppermute | solution.py:384
  69.9 3.1 %group.1 = (bf16[3,2,192,640]{3,2,1,0:T(8,128)(2,1)S(1)}, bf16[192,1280]{1,0:T(8,128)(2,1)S(1)}, f32[1536,64]{1,0:T(8,128)S(1)}, bf16[384,640]{1,0:T(8,128)(2,1)S(1)}) custom-call(s32[4]{0:T(128)S(1)} %pad_add_fusion.place, bf16[40,1280]{1,0:T(8,128)(2,1)S(1)} %collective-permute-done.5.after.refs_1_, ...), custom_call_target="tpu_custom_call" | custom-call | flops 99999997952 | bytes 5124112 | tf_op jit(solution)/shard_map/group/pallas_call | solution.py:61
  73.1 2.2 %group_weight.1 = (f32[160,1280]{1,0:T(8,128)S(1)}, bf16[160,1280]{1,0:T(8,128)(2,1)}, bf16[160,1280]{1,0:T(8,128)(2,1)}, bf16[160,1280]{1,0:T(8,128)(2,1)S(1)}, bf16[192,1280]{1,0:T(8,128)(2,1)S(1)}) custom-call(bf16[384,640]{1,0:T(8,128)(2,1)S(1)} %get-tuple-element.49.act, bf16[192,1280]{1,0:T(8,128)(2,1)S(1)} %get-tuple-element.48.cot, ...), custom_call_target="tpu_custom_call" | custom-call | flops 629145600 | bytes 4014080 | tf_op jit(solution)/shard_map/group_weight/pallas_call | solution.py:61
  75.2 2.4 %collective-permute-start.12 = (bf16[160,1280]{1,0:T(8,128)(2,1)}, bf16[160,1280]{1,0:T(8,128)(2,1)S(1)}, u32[]{:S(2)}, u32[]{:S(2)}) collective-permute-start(bf16[160,1280]{1,0:T(8,128)(2,1)} %get-tuple-element.56), channel_id=1, source_target_pairs={{0,4},{1,5},{2,6},{3,7},{4,0},{5,1},{6,2},{7,3},{8,12},{9,13},{10,... | collective-permute-start | bytes 1228808 | tf_op jit(solution)/shard_map/ppermute | solution.py:399
  77.6 2.1 %collective-permute-start.13 = (bf16[160,1280]{1,0:T(8,128)(2,1)S(1)}, bf16[160,1280]{1,0:T(8,128)(2,1)}, u32[]{:S(2)}, u32[]{:S(2)}) collective-permute-start(bf16[160,1280]{1,0:T(8,128)(2,1)S(1)} %get-tuple-element.57), channel_id=1, source_target_pairs={{0,6},{1,7},{2,0},{3,1},{4,2},{5,3},{6,4},{7,5},{8,14},{9,15},{10,... | collective-permute-start | bytes 1228808 | tf_op jit(solution)/shard_map/ppermute | solution.py:399
  79.7 5.4 %group_back.1 = bf16[1152,640]{1,0:T(8,128)(2,1)} custom-call(s32[4]{0:T(128)S(1)} %pad_add_fusion.place, f32[1536,64]{1,0:T(8,128)S(1)} %get-tuple-element.46.probs_in, bf16[3,2,192,640]{3,2,1,0:T(8,128)(2,1)S(1)} %get-tuple-element.47.data, bf16[192,1280]{1,0:T(8,128)(2,1)S(1)} %get-tuple-element.48.cot, bf16[192,1280]{1,0:T(8,128)(2,1)S(1)} %get-tuple-element.50.cot_far, ...), custom_call_target="tpu_custom_call" | custom-call | flops 2000000000 | bytes 7602192 | tf_op jit(solution)/shard_map/group_back/pallas_call | solution.py:61
  85.1 4.9 %all-to-all-start.1 = ((bf16[16,72,640]{2,1,0:T(8,128)(2,1)}), bf16[16,72,640]{2,1,0:T(8,128)(2,1)S(1)}, u32[]{:S(2)}, u32[]{:S(2)}) async-start(bf16[16,72,640]{2,1,0:T(8,128)(2,1)} %bitcast.13), calls=%async_computation.1 | async-start | bytes 2949120 | tf_op jit(solution)/shard_map/all_to_all | solution.py:416
  90.0 6.2 %collective-permute-done.12.b = bf16[160,1280]{1,0:T(8,128)(2,1)S(1)} collective-permute-done((bf16[160,1280]{1,0:T(8,128)(2,1)}, bf16[160,1280]{1,0:T(8,128)(2,1)S(1)}, u32[]{:S(2)}, u32[]{:S(2)}) %collective-permute-start.12) | collective-permute-done | bytes 409632 | tf_op jit(solution)/shard_map/ppermute | solution.py:399
  98.6 2.3 %collective-permute-start.14 = (bf16[40,1280]{1,0:T(8,128)(2,1)S(1)}, bf16[40,1280]{1,0:T(8,128)(2,1)S(1)}, u32[]{:S(2)}, u32[]{:S(2)}) collective-permute-start(bf16[40,1280]{1,0:T(8,128)(2,1)S(1)} %get-tuple-element.59), channel_id=1, source_target_pairs={{0,32},{32,64},{64,96},{96,0},{128,160},{160,192},{192,224},{224,1... | collective-permute-start | bytes 307208 | tf_op jit(solution)/shard_map/ppermute | solution.py:389
  101.0 2.1 %collective-permute-start.15 = (bf16[40,1280]{1,0:T(8,128)(2,1)S(1)}, bf16[40,1280]{1,0:T(8,128)(2,1)S(1)}, u32[]{:S(2)}, u32[]{:S(2)}) collective-permute-start(bf16[40,1280]{1,0:T(8,128)(2,1)S(1)} %get-tuple-element.60), channel_id=1, source_target_pairs={{0,64},{32,96},{64,0},{96,32},{128,192},{160,224},{192,128},{224,1... | collective-permute-start | bytes 307208 | tf_op jit(solution)/shard_map/ppermute | solution.py:389
  103.1 1.7 %collective-permute-start.16 = (bf16[40,1280]{1,0:T(8,128)(2,1)S(1)}, bf16[40,1280]{1,0:T(8,128)(2,1)S(1)}, u32[]{:S(2)}, u32[]{:S(2)}) collective-permute-start(bf16[40,1280]{1,0:T(8,128)(2,1)S(1)} %get-tuple-element.61), channel_id=1, source_target_pairs={{0,96},{32,0},{64,32},{96,64},{128,224},{160,128},{192,160},{224,1... | collective-permute-start | bytes 307208 | tf_op jit(solution)/shard_map/ppermute | solution.py:389
  104.9 1.7 %collective-permute-done.15.refs_6_ = bf16[40,1280]{1,0:T(8,128)(2,1)S(1)} collective-permute-done((bf16[40,1280]{1,0:T(8,128)(2,1)S(1)}, bf16[40,1280]{1,0:T(8,128)(2,1)S(1)}, u32[]{:S(2)}, u32[]{:S(2)}) %collective-permute-start.15) | collective-permute-done | bytes 102432 | tf_op jit(solution)/shard_map/ppermute | solution.py:389
  107.1 16.8 %collective-permute-start.17 = (bf16[24,1280]{1,0:T(8,128)(2,1)S(1)}, bf16[24,1280]{1,0:T(8,128)(2,1)S(1)}, u32[]{:S(2)}, u32[]{:S(2)}) collective-permute-start(bf16[24,1280]{1,0:T(8,128)(2,1)S(1)} %get-tuple-element.62), channel_id=1, source_target_pairs={{0,0},{1,16},{2,2},{3,18},{4,4},{5,20},{6,6},{7,22},{8,1},{9,17},{... | collective-permute-start | bytes 184328 | tf_op jit(solution)/shard_map/ppermute | solution.py:409
  123.9 4.2 %collective-permute-start.18 = (bf16[24,1280]{1,0:T(8,128)(2,1)S(1)}, bf16[24,1280]{1,0:T(8,128)(2,1)S(1)}, u32[]{:S(2)}, u32[]{:S(2)}) collective-permute-start(bf16[24,1280]{1,0:T(8,128)(2,1)S(1)} %get-tuple-element.63), channel_id=1, source_target_pairs={{0,1},{1,17},{2,3},{3,19},{4,5},{5,21},{6,7},{7,23},{8,8},{9,24},{... | collective-permute-start | bytes 184328 | tf_op jit(solution)/shard_map/ppermute | solution.py:409
  128.1 2.2 %collective-permute-start.20 = (bf16[24,1280]{1,0:T(8,128)(2,1)S(1)}, bf16[24,1280]{1,0:T(8,128)(2,1)S(1)}, u32[]{:S(2)}, u32[]{:S(2)}) collective-permute-start(bf16[24,1280]{1,0:T(8,128)(2,1)S(1)} %get-tuple-element.65), channel_id=1, source_target_pairs={{0,9},{1,25},{2,11},{3,27},{4,13},{5,29},{6,15},{7,31},{8,0},{9,16... | collective-permute-start | bytes 184328 | tf_op jit(solution)/shard_map/ppermute | solution.py:409
  130.4 4.2 %collective-permute-done.19.c = bf16[24,1280]{1,0:T(8,128)(2,1)S(1)} collective-permute-done((bf16[24,1280]{1,0:T(8,128)(2,1)S(1)}, bf16[24,1280]{1,0:T(8,128)(2,1)S(1)}, u32[]{:S(2)}, u32[]{:S(2)}) %collective-permute-start.19) | collective-permute-done | bytes 61472 | tf_op jit(solution)/shard_map/ppermute | solution.py:409
  134.5 3.1 %collective-permute-done.20.d = bf16[24,1280]{1,0:T(8,128)(2,1)S(1)} collective-permute-done((bf16[24,1280]{1,0:T(8,128)(2,1)S(1)}, bf16[24,1280]{1,0:T(8,128)(2,1)S(1)}, u32[]{:S(2)}, u32[]{:S(2)}) %collective-permute-start.20) | collective-permute-done | bytes 61472 | tf_op jit(solution)/shard_map/ppermute | solution.py:409
  138.4 3.5 %all-to-all-start.2 = ((bf16[8,24,1280]{2,1,0:T(8,128)(2,1)}), bf16[8,24,1280]{2,1,0:T(8,128)(2,1)S(1)}, u32[]{:S(2)}, u32[]{:S(2)}) async-start(bf16[8,24,1280]{2,1,0:T(8,128)(2,1)} %sum_z.1), calls=%async_computation.2 | async-start | bytes 983040 | tf_op jit(solution)/shard_map/all_to_all | solution.py:563
  143.5 2.2 %collective-permute-done.10.far = bf16[2,96,1920]{2,1,0:T(8,128)(2,1)S(1)} collective-permute-done((bf16[2,96,1920]{2,1,0:T(8,128)(2,1)S(1)}, bf16[2,96,1920]{2,1,0:T(8,128)(2,1)S(1)}, u32[]{:S(2)}, u32[]{:S(2)}) %collective-permute-start.10) | collective-permute-done | bytes 737312 | tf_op jit(solution)/shard_map/ppermute | solution.py:384
  145.7 1.8 %merge.1.after = bf16[2,96,3840]{2,1,0:T(8,128)(2,1)} custom-call(s32[4]{0:T(128)S(1)} %pad_add_fusion.place, bf16[2,96,1920]{2,1,0:T(8,128)(2,1)S(1)} %get-tuple-element.51.mine, bf16[2,96,1920]{2,1,0:T(8,128)(2,1)S(1)} %collective-permute-done.10.far), custom_call_target="tpu_custom_call" | custom-call | bytes 2949136 | tf_op jit(solution)/shard_map/merge/pallas_call | solution.py:61
  147.5 2.7 %all-to-all-done.2.pieces = bf16[8,24,1280]{2,1,0:T(8,128)(2,1)S(1)} async-done(((bf16[8,24,1280]{2,1,0:T(8,128)(2,1)}), bf16[8,24,1280]{2,1,0:T(8,128)(2,1)S(1)}, u32[]{:S(2)}, u32[]{:S(2)}) %all-to-all-start.2) | async-done | bytes 491552 | tf_op jit(solution)/shard_map/all_to_all | solution.py:563
  (54 shorter events, 20.6 us)
Async XLA Ops:
  0.8 1.4 copy-start
  2.1 5.8 %copy-start.1 = (bf16[1,2,96,3840]{3,2,1,0:T(8,128)(2,1)S(1)}, bf16[1,2,96,3840]{3,2,1,0:T(8,128)(2,1)}, u32[]{:S(2)}) copy-start(bf16[1,2,96,3840]{3,2,1,0:T(8,128)(2,1)} %param.8) | copy-start | bytes 4423684
  2.1 5.8 %copy-start.4 = (bf16[1,2,96,1280]{3,2,1,0:T(8,128)(2,1)S(1)}, bf16[1,2,96,1280]{3,2,1,0:T(8,128)(2,1)}, u32[]{:S(2)}) copy-start(bf16[1,2,96,1280]{3,2,1,0:T(8,128)(2,1)} %param.11) | copy-start | bytes 1474564
  2.7 5.2 %collective-permute-start.8 = (bf16[2,96,1920]{2,1,0:T(8,128)(2,1)S(1)}, bf16[2,96,1920]{2,1,0:T(8,128)(2,1)S(1)}, u32[]{:S(2)}, u32[]{:S(2)}) collective-permute-start(bf16[2,96,1920]{2,1,0:T(8,128)(2,1)S(1)} %far.1), channel_id=1, source_target_pairs={{0,1},{1,0},{2,3},{3,2},{4,5},{5,4},{6,7},{7,6},{8,9},{9,8},{10,11... | collective-permute-start | bytes 2211848 | tf_op jit(solution)/shard_map/ppermute | solution.py:384
  11.1 10.1 %copy-start.7 = (s32[1,2,96]{2,1,0:T(2,128)S(1)}, s32[1,2,96]{2,1,0:T(2,128)}, u32[]{:S(2)}) copy-start(s32[1,2,96]{2,1,0:T(2,128)} %param.9) | copy-start | bytes 2308
  11.1 10.1 %copy-start.8 = (f32[8]{0:T(128)S(1)}, f32[8]{0:T(128)}, u32[]{:S(2)}) copy-start(f32[8]{0:T(128)} %slopes.1) | copy-start | bytes 100
  11.1 54.8 %all-to-all-start = ((bf16[16,96,640]{2,1,0:T(8,128)(2,1)}), bf16[16,96,640]{2,1,0:T(8,128)(2,1)S(1)}, u32[]{:S(2)}, u32[]{:S(2)}) async-start(bf16[16,96,640]{2,1,0:T(8,128)(2,1)} %bitcast.10), calls=%async_computation | async-start | bytes 3932160 | tf_op jit(solution)/shard_map/all_to_all | solution.py:416
  20.4 10.3 %collective-permute-start.1 = (bf16[192,1280]{1,0:T(8,128)(2,1)S(1)}, bf16[192,1280]{1,0:T(8,128)(2,1)S(1)}, u32[]{:S(2)}, u32[]{:S(2)}) collective-permute-start(bf16[192,1280]{1,0:T(8,128)(2,1)S(1)} %bitcast.23), channel_id=1, source_target_pairs={{0,1},{1,0},{2,3},{3,2},{4,5},{5,4},{6,7},{7,6},{8,9},{9,8},{10,11... | collective-permute-start | bytes 1474568 | tf_op jit(solution)/shard_map/ppermute | solution.py:384
  21.2 1.9 %copy-start.5 = (bf16[1280,1280]{1,0:T(8,128)(2,1)S(1)}, bf16[1280,1280]{1,0:T(8,128)(2,1)}, u32[]{:S(2)}) copy-start(bf16[1280,1280]{1,0:T(8,128)(2,1)} %weight.2) | copy-start | bytes 9830404
  29.2 1.5 collective-permute-start
  31.8 12.2 %collective-permute-start.2 = (bf16[160,1280]{1,0:T(8,128)(2,1)S(1)}, bf16[160,1280]{1,0:T(8,128)(2,1)S(1)}, u32[]{:S(2)}, u32[]{:S(2)}) collective-permute-start(bf16[160,1280]{1,0:T(8,128)(2,1)S(1)} %get-tuple-element.40), channel_id=1, source_target_pairs={{0,32},{32,64},{64,96},{96,0},{128,160},{160,192},{192,224},{224,1... | collective-permute-start | bytes 1228808 | tf_op jit(solution)/shard_map/ppermute | solution.py:389
  33.1 20.7 %collective-permute-start.3 = (bf16[160,1280]{1,0:T(8,128)(2,1)S(1)}, bf16[160,1280]{1,0:T(8,128)(2,1)S(1)}, u32[]{:S(2)}, u32[]{:S(2)}) collective-permute-start(bf16[160,1280]{1,0:T(8,128)(2,1)S(1)} %get-tuple-element.41), channel_id=1, source_target_pairs={{0,64},{32,96},{64,0},{96,32},{128,192},{160,224},{192,128},{224,1... | collective-permute-start | bytes 1228808 | tf_op jit(solution)/shard_map/ppermute | solution.py:389
  35.6 18.2 %collective-permute-start.4 = (bf16[160,1280]{1,0:T(8,128)(2,1)S(1)}, bf16[160,1280]{1,0:T(8,128)(2,1)S(1)}, u32[]{:S(2)}, u32[]{:S(2)}) collective-permute-start(bf16[160,1280]{1,0:T(8,128)(2,1)S(1)} %get-tuple-element.42), channel_id=1, source_target_pairs={{0,96},{32,0},{64,32},{96,64},{128,224},{160,128},{192,160},{224,1... | collective-permute-start | bytes 1228808 | tf_op jit(solution)/shard_map/ppermute | solution.py:389
  54.0 15.1 %collective-permute-start.5 = (bf16[40,1280]{1,0:T(8,128)(2,1)S(1)}, bf16[40,1280]{1,0:T(8,128)(2,1)S(1)}, u32[]{:S(2)}, u32[]{:S(2)}) collective-permute-start(bf16[40,1280]{1,0:T(8,128)(2,1)S(1)} %get-tuple-element.43), channel_id=1, source_target_pairs={{0,2},{1,3},{2,4},{3,5},{4,6},{5,7},{6,0},{7,1},{8,10},{9,11},{10,... | collective-permute-start | bytes 307208 | tf_op jit(solution)/shard_map/ppermute | solution.py:399
  55.6 14.3 %collective-permute-start.6 = (bf16[40,1280]{1,0:T(8,128)(2,1)S(1)}, bf16[40,1280]{1,0:T(8,128)(2,1)S(1)}, u32[]{:S(2)}, u32[]{:S(2)}) collective-permute-start(bf16[40,1280]{1,0:T(8,128)(2,1)S(1)} %get-tuple-element.44), channel_id=1, source_target_pairs={{0,4},{1,5},{2,6},{3,7},{4,0},{5,1},{6,2},{7,3},{8,12},{9,13},{10,... | collective-permute-start | bytes 307208 | tf_op jit(solution)/shard_map/ppermute | solution.py:399
  58.0 11.9 %collective-permute-start.7 = (bf16[40,1280]{1,0:T(8,128)(2,1)S(1)}, bf16[40,1280]{1,0:T(8,128)(2,1)S(1)}, u32[]{:S(2)}, u32[]{:S(2)}) collective-permute-start(bf16[40,1280]{1,0:T(8,128)(2,1)S(1)} %get-tuple-element.45), channel_id=1, source_target_pairs={{0,6},{1,7},{2,0},{3,1},{4,2},{5,3},{6,4},{7,5},{8,14},{9,15},{10,... | collective-permute-start | bytes 307208 | tf_op jit(solution)/shard_map/ppermute | solution.py:399
  65.9 7.1 %collective-permute-start.9 = (bf16[16,24,640]{2,1,0:T(8,128)(2,1)S(1)}, bf16[16,24,640]{2,1,0:T(8,128)(2,1)S(1)}, u32[]{:S(2)}, u32[]{:S(2)}) collective-permute-start(bf16[16,24,640]{2,1,0:T(8,128)(2,1)S(1)} %slice.4), channel_id=1, source_target_pairs={{0,1},{1,0},{2,3},{3,2},{4,5},{5,4},{6,7},{7,6},{8,9},{9,8},{10,11... | collective-permute-start | bytes 1474568 | tf_op jit(solution)/shard_map/ppermute | solution.py:384
  69.9 9.7 %copy-start.3 = (bf16[1280,1280]{1,0:T(8,128)(2,1)S(1)}, bf16[1280,1280]{1,0:T(8,128)(2,1)}, u32[]{:S(2)}) copy-start(bf16[1280,1280]{1,0:T(8,128)(2,1)} %weight.3) | copy-start | bytes 9830404
  75.2 9.9 %copy-start.9 = (f32[160,1280]{1,0:T(8,128)}, f32[160,1280]{1,0:T(8,128)S(1)}, u32[]{:S(2)}) copy-start(f32[160,1280]{1,0:T(8,128)S(1)} %get-tuple-element.54.own) | copy-start | bytes 2457604
  75.2 14.8 %collective-permute-start.11 = (bf16[160,1280]{1,0:T(8,128)(2,1)}, bf16[160,1280]{1,0:T(8,128)(2,1)S(1)}, u32[]{:S(2)}, u32[]{:S(2)}) collective-permute-start(bf16[160,1280]{1,0:T(8,128)(2,1)} %get-tuple-element.55), channel_id=1, source_target_pairs={{0,2},{1,3},{2,4},{3,5},{4,6},{5,7},{6,0},{7,1},{8,10},{9,11},{10,... | collective-permute-start | bytes 1228808 | tf_op jit(solution)/shard_map/ppermute | solution.py:399
  75.2 21.0 %collective-permute-start.12 = (bf16[160,1280]{1,0:T(8,128)(2,1)}, bf16[160,1280]{1,0:T(8,128)(2,1)S(1)}, u32[]{:S(2)}, u32[]{:S(2)}) collective-permute-start(bf16[160,1280]{1,0:T(8,128)(2,1)} %get-tuple-element.56), channel_id=1, source_target_pairs={{0,4},{1,5},{2,6},{3,7},{4,0},{5,1},{6,2},{7,3},{8,12},{9,13},{10,... | collective-permute-start | bytes 1228808 | tf_op jit(solution)/shard_map/ppermute | solution.py:399
  77.6 18.7 %collective-permute-start.13 = (bf16[160,1280]{1,0:T(8,128)(2,1)S(1)}, bf16[160,1280]{1,0:T(8,128)(2,1)}, u32[]{:S(2)}, u32[]{:S(2)}) collective-permute-start(bf16[160,1280]{1,0:T(8,128)(2,1)S(1)} %get-tuple-element.57), channel_id=1, source_target_pairs={{0,6},{1,7},{2,0},{3,1},{4,2},{5,3},{6,4},{7,5},{8,14},{9,15},{10,... | collective-permute-start | bytes 1228808 | tf_op jit(solution)/shard_map/ppermute | solution.py:399
  85.1 52.5 %all-to-all-start.1 = ((bf16[16,72,640]{2,1,0:T(8,128)(2,1)}), bf16[16,72,640]{2,1,0:T(8,128)(2,1)S(1)}, u32[]{:S(2)}, u32[]{:S(2)}) async-start(bf16[16,72,640]{2,1,0:T(8,128)(2,1)} %bitcast.13), calls=%async_computation.1 | async-start | bytes 2949120 | tf_op jit(solution)/shard_map/all_to_all | solution.py:416
  98.6 6.2 %collective-permute-start.14 = (bf16[40,1280]{1,0:T(8,128)(2,1)S(1)}, bf16[40,1280]{1,0:T(8,128)(2,1)S(1)}, u32[]{:S(2)}, u32[]{:S(2)}) collective-permute-start(bf16[40,1280]{1,0:T(8,128)(2,1)S(1)} %get-tuple-element.59), channel_id=1, source_target_pairs={{0,32},{32,64},{64,96},{96,0},{128,160},{160,192},{192,224},{224,1... | collective-permute-start | bytes 307208 | tf_op jit(solution)/shard_map/ppermute | solution.py:389
  101.0 5.6 %collective-permute-start.15 = (bf16[40,1280]{1,0:T(8,128)(2,1)S(1)}, bf16[40,1280]{1,0:T(8,128)(2,1)S(1)}, u32[]{:S(2)}, u32[]{:S(2)}) collective-permute-start(bf16[40,1280]{1,0:T(8,128)(2,1)S(1)} %get-tuple-element.60), channel_id=1, source_target_pairs={{0,64},{32,96},{64,0},{96,32},{128,192},{160,224},{192,128},{224,1... | collective-permute-start | bytes 307208 | tf_op jit(solution)/shard_map/ppermute | solution.py:389
  103.1 3.8 %collective-permute-start.16 = (bf16[40,1280]{1,0:T(8,128)(2,1)S(1)}, bf16[40,1280]{1,0:T(8,128)(2,1)S(1)}, u32[]{:S(2)}, u32[]{:S(2)}) collective-permute-start(bf16[40,1280]{1,0:T(8,128)(2,1)S(1)} %get-tuple-element.61), channel_id=1, source_target_pairs={{0,96},{32,0},{64,32},{96,64},{128,224},{160,128},{192,160},{224,1... | collective-permute-start | bytes 307208 | tf_op jit(solution)/shard_map/ppermute | solution.py:389
  107.1 23.3 %collective-permute-start.17 = (bf16[24,1280]{1,0:T(8,128)(2,1)S(1)}, bf16[24,1280]{1,0:T(8,128)(2,1)S(1)}, u32[]{:S(2)}, u32[]{:S(2)}) collective-permute-start(bf16[24,1280]{1,0:T(8,128)(2,1)S(1)} %get-tuple-element.62), channel_id=1, source_target_pairs={{0,0},{1,16},{2,2},{3,18},{4,4},{5,20},{6,6},{7,22},{8,1},{9,17},{... | collective-permute-start | bytes 184328 | tf_op jit(solution)/shard_map/ppermute | solution.py:409
  123.9 6.5 %collective-permute-start.18 = (bf16[24,1280]{1,0:T(8,128)(2,1)S(1)}, bf16[24,1280]{1,0:T(8,128)(2,1)S(1)}, u32[]{:S(2)}, u32[]{:S(2)}) collective-permute-start(bf16[24,1280]{1,0:T(8,128)(2,1)S(1)} %get-tuple-element.63), channel_id=1, source_target_pairs={{0,1},{1,17},{2,3},{3,19},{4,5},{5,21},{6,7},{7,23},{8,8},{9,24},{... | collective-permute-start | bytes 184328 | tf_op jit(solution)/shard_map/ppermute | solution.py:409
  128.1 6.5 %collective-permute-start.19 = (bf16[24,1280]{1,0:T(8,128)(2,1)S(1)}, bf16[24,1280]{1,0:T(8,128)(2,1)S(1)}, u32[]{:S(2)}, u32[]{:S(2)}) collective-permute-start(bf16[24,1280]{1,0:T(8,128)(2,1)S(1)} %get-tuple-element.64), channel_id=1, source_target_pairs={{0,8},{1,24},{2,10},{3,26},{4,12},{5,28},{6,14},{7,30},{8,9},{9,25... | collective-permute-start | bytes 184328 | tf_op jit(solution)/shard_map/ppermute | solution.py:409
  128.1 9.4 %collective-permute-start.20 = (bf16[24,1280]{1,0:T(8,128)(2,1)S(1)}, bf16[24,1280]{1,0:T(8,128)(2,1)S(1)}, u32[]{:S(2)}, u32[]{:S(2)}) collective-permute-start(bf16[24,1280]{1,0:T(8,128)(2,1)S(1)} %get-tuple-element.65), channel_id=1, source_target_pairs={{0,9},{1,25},{2,11},{3,27},{4,13},{5,29},{6,15},{7,31},{8,0},{9,16... | collective-permute-start | bytes 184328 | tf_op jit(solution)/shard_map/ppermute | solution.py:409
  138.4 11.7 %all-to-all-start.2 = ((bf16[8,24,1280]{2,1,0:T(8,128)(2,1)}), bf16[8,24,1280]{2,1,0:T(8,128)(2,1)S(1)}, u32[]{:S(2)}, u32[]{:S(2)}) async-start(bf16[8,24,1280]{2,1,0:T(8,128)(2,1)} %sum_z.1), calls=%async_computation.2 | async-start | bytes 983040 | tf_op jit(solution)/shard_map/all_to_all | solution.py:563
  143.4 2.3 %collective-permute-start.10 = (bf16[2,96,1920]{2,1,0:T(8,128)(2,1)S(1)}, bf16[2,96,1920]{2,1,0:T(8,128)(2,1)S(1)}, u32[]{:S(2)}, u32[]{:S(2)}) collective-permute-start(bf16[2,96,1920]{2,1,0:T(8,128)(2,1)S(1)} %get-tuple-element.52), channel_id=1, source_target_pairs={{0,1},{1,0},{2,3},{3,2},{4,5},{5,4},{6,7},{7,6},{8,9},{9,8},{10,11... | collective-permute-start | bytes 2211848 | tf_op jit(solution)/shard_map/ppermute | solution.py:384
  (3 other events, 3.9 us)

commit v7 on v6

--- a/solution.py
+++ b/solution.py
@@ -49,7 +49,7 @@
 UNPACK = ([("p", 8), ("s", 3), ("o", 2), ("w", 2), ("t", 6)], ["s", "o", "w", "p", "t"])
 
 
-def call(kernel, outs, *args, smem=(), unread=(), scratch=(), flops=0, name=None):
+def call(kernel, outs, *args, smem=(), unread=(), sent=False, scratch=(), flops=0, name=None):
     specs = [
         pl.BlockSpec(
             memory_space=pltpu.SMEM if i in smem else pl.ANY if i in unread else pltpu.VMEM
@@ -62,7 +62,10 @@
         kernel,
         out_shape=outs,
         in_specs=specs,
-        out_specs=[pl.BlockSpec(memory_space=pltpu.VMEM) for _ in outs],
+        out_specs=[
+            pl.BlockSpec(memory_space=pl.ANY if sent and i == 0 else pltpu.VMEM)
+            for i in range(len(outs))
+        ],
         scratch_shapes=scratch,
         compiler_params=pltpu.CompilerParams(vmem_limit_bytes=VMEM_LIMIT),
         cost_estimate=pl.CostEstimate(flops=flops, bytes_accessed=size, transcendentals=0),
@@ -164,14 +167,32 @@
     return pl.ds(pl.multiple_of(1280 * section + 640 * core, 128), 640)
 
 
-def far_kernel(place, qkv, out):
-    for s in range(3):
-        for w in range(2):
-            out[w, :, 640 * s : 640 * s + 640] = qkv[w, :, lanes_of(s, 1 - place[3])]
-
-
-def pack_kernel(place, qkv, far, cot, out):
+def far_kernel(place, qkv, out, sems):
+    sends = [
+        pltpu.make_async_copy(
+            qkv.at[:, :, lanes_of(s, 1 - place[3])],
+            out.at[:, :, pl.ds(640 * s, 640)],
+            sems.at[s],
+        )
+        for s in range(3)
+    ]
+    for send in sends:
+        send.start()
+    for send in sends:
+        send.wait()
+
+
+def copies(held, out, sems):
+    rows = out.shape[0] // 2
+    return [
+        pltpu.make_async_copy(held.at[i], out.at[pl.ds(rows * i, rows)], sems.at[i])
+        for i in range(2)
+    ]
+
+
+def pack_kernel(place, qkv, far, cot, out, held, sems):
     hot = order_matrix(*HOME)
+    sends = copies(held, out, sems)
     for group in range(2):
         rows = slice(48 * group, 48 * group + 48)
 
@@ -183,8 +204,11 @@
         for part, pieces in enumerate((section(0) + section(1), section(2) + cots)):
             sent = dot_nn(hot, jnp.concatenate(pieces, axis=0)).astype(BF16)
             for p in range(8):
-                start = 96 * (8 * group + p) + 48 * part
-                out[start : start + 48, :] = sent[48 * p : 48 * p + 48, :]
+                start = 96 * p + 48 * part
+                held[group, start : start + 48, :] = sent[48 * p : 48 * p + 48, :]
+        sends[group].start()
+    for send in sends:
+        send.wait()
 
 
 def unpack_kernel(got, mine, other):
@@ -200,11 +224,22 @@
                     ]
 
 
-def merge_kernel(place, mine, far, out):
+def merge_kernel(place, mine, far, out, done, sems):
+    done[...] = jnp.zeros_like(done)
+    sends = []
     for s in range(3):
-        for w in range(2):
-            out[w, :, lanes_of(s, place[3])] = mine[w, :, 640 * s : 640 * s + 640]
-            out[w, :, lanes_of(s, 1 - place[3])] = far[w, :, 640 * s : 640 * s + 640]
+        for i, (ref, core) in enumerate(((mine, place[3]), (far, 1 - place[3]))):
+            sends.append(
+                pltpu.make_async_copy(
+                    ref.at[:, :, pl.ds(640 * s, 640)],
+                    out.at[:, :, lanes_of(s, core)],
+                    sems.at[2 * s + i],
+                )
+            )
+    for send in sends:
+        send.start()
+    for send in sends:
+        send.wait()
 
 
 def local_kernel(place, slopes, qkv, cot, weight, positions, d_out, act_own, act_other, act_all):
@@ -285,9 +320,10 @@
     act[...] = dot_nn(act_all[...], row_hot(place, True)).astype(BF16)
 
 
-def group_back_kernel(place, probs_in, data, cot, cot_far, weight, back, grads):
+def group_back_kernel(place, probs_in, data, cot, cot_far, weight, back, grads, held, sems):
     masks = head_masks()
     hot = order_matrix(*BACK)
+    sends = copies(held, back, sems)
     own_rows = weight[pl.ds(pl.multiple_of(640 * place[3], 128), 640), :]
     g_own = dot_nt(cot[...], own_rows).astype(BF16)
     g_far = dot_nt(cot_far[...], own_rows).astype(BF16)
@@ -319,7 +355,10 @@
             for t in range(6)
         ]
         whole = jnp.concatenate(pieces, axis=0)
-        back[576 * group : 576 * group + 576, :] = dot_nn(hot, whole).astype(BF16)
+        held[group] = dot_nn(hot, whole).astype(BF16)
+        sends[group].start()
+    for send in sends:
+        send.wait()
 
 
 def weight_parts(a, b, cot, cot_far, own, one, two, three):
@@ -409,7 +448,7 @@
     return lax.ppermute(a, "tok", pairs)
 
 
-CHIPS = [[chip(0, 0, c) + 2 * p for p in range(16)] for c in range(2)]
+CHIPS = [[chip(i % 4, (i // 4 + i) % 4, c) for i in range(16)] for c in range(2)]
 
 
 def exchange(a):
@@ -432,7 +471,15 @@
     partials = [sds((160, 1280), F32)] + [sds((160, 1280), BF16)] * 3
 
     (other,) = call(
-        far_kernel, [sds((2, 96, 1920), BF16)], place, qkv_global, smem=(0,), name="far"
+        far_kernel,
+        [sds((2, 96, 1920), BF16)],
+        place,
+        qkv_global,
+        smem=(0,),
+        unread=(1,),
+        sent=True,
+        scratch=[pltpu.SemaphoreType.DMA((3,))],
+        name="far",
     )
     far = swap_cores(other)
     (packed,) = call(
@@ -443,6 +490,8 @@
         far,
         cotangent,
         smem=(0,),
+        sent=True,
+        scratch=[pltpu.VMEM((2, 768, 640), BF16), pltpu.SemaphoreType.DMA((2,))],
         name="pack",
     )
     got = exchange(packed)
@@ -520,7 +569,12 @@
         cot_far,
         w_out_global,
         smem=(0,),
-        scratch=[pltpu.VMEM((3, 2, 192, 640), BF16)],
+        sent=True,
+        scratch=[
+            pltpu.VMEM((3, 2, 192, 640), BF16),
+            pltpu.VMEM((2, 576, 640), BF16),
+            pltpu.SemaphoreType.DMA((2,)),
+        ],
         flops=2 * 10**9,
         name="group_back",
     )
@@ -555,25 +609,28 @@
     (sums,) = call(
         sum_z_kernel,
         [sds((8, 24, 1280), BF16)],
-        returned,
+        mine,
         *[to_owner(chunk, d) for d, chunk in enumerate(chunks)],
         unread=(0,),
         name="sum_z",
     )
     pieces = lax.all_to_all(sums, "dp", split_axis=0, concat_axis=0, tiled=True)
-    (d_global,) = call(
+    d_global, done = call(
         merge_kernel,
-        [sds((2, 96, 3840), BF16)],
+        [sds((2, 96, 3840), BF16), sds((8, 128), F32)],
         place,
         mine,
         swap_cores(other),
         smem=(0,),
+        unread=(1, 2),
+        sent=True,
+        scratch=[pltpu.SemaphoreType.DMA((6,))],
         name="merge",
     )
     grad_local, grad_global = call(
         functools.partial(final_kernel, scale),
         [sds((40, 1280), F32), sds((40, 1280), F32)],
-        d_global,
+        done,
         pieces,
         unread=(0,),
         name="final",

time: 153 us -> 147 us (0.961)
  starting transfers between devices: 69.1 us -> 62.6 us
  waiting for transfers between devices: 48.3 us -> 50.7 us
    ppermute x4, starting transfers between devices: 23.3 us -> 16.7 us  [to_owner(): return lax.ppermute(a, 'tok', pairs)]
    ppermute x5, starting transfers between devices: 7.37 us -> 9.63 us  [swap_cores(): return lax.ppermute(a, 'tok', [(i, i ^ 1) for i in range(32)])]
    all_to_all x1, waiting for transfers between devices: 2.67 us -> 4.75 us  [per_device(): pieces = lax.all_to_all(sums, 'dp', split_axis=0, concat_axis=0, tiled=True)]
    ppermute x6, starting transfers between devices: 9.64 us -> 8.07 us  [along_y(): return lax.ppermute(a, 'tok', pairs)]
    unnamed x22 -> x20, local copies, waits for them, and re-layouts: 7.22 us -> 5.85 us
  transfers between devices with their start and end apart: 24 -> 24, of which waited for: 13 -> 15; matrix products, arithmetic and copies ran while one was open for 0% -> 0% of each run, Pallas kernels for 13% -> 13%
where the time goes in v7:
time: 147 us; the launch traced here: 146 us
  starting transfers between devices  62.6 us (43%)
  waiting for transfers between devices  50.7 us (34%)
  Pallas kernels  26.1 us (18%)
  local copies, waits for them, and re-layouts  5.89 us (4%)
    pallas_call x14, Pallas kernels, call(): pl.pallas_call(kernel, out_shape=outs, in_specs=specs, out_specs=[pl.Bloc...  26.1 us
    ppermute x6, waiting for transfers between devices, along_x(): return lax.ppermute(a, 'dp', pairs)  20.1 us
    ppermute x4, starting transfers between devices, to_owner(): return lax.ppermute(a, 'tok', pairs)  16.7 us
    all_to_all x2, starting transfers between devices, exchange(): lax.all_to_all(a, 'tok', split_axis=0, concat_axis=0, axis_index_groups=C...  14.3 us
    ppermute x6, starting transfers between devices, along_x(): return lax.ppermute(a, 'dp', pairs)  9.78 us
    ppermute x5, starting transfers between devices, swap_cores(): return lax.ppermute(a, 'tok', [(i, i ^ 1) for i in range(32)])  9.63 us
    ppermute x6, waiting for transfers between devices, along_y(): return lax.ppermute(a, 'tok', pairs)  8.44 us
    ppermute x6, starting transfers between devices, along_y(): return lax.ppermute(a, 'tok', pairs)  8.07 us
  transfers between devices with their start and end apart: 24, of which 15 were waited for; matrix products, arithmetic and copies ran while one was open for 0% of the time, Pallas kernels for 13%

profile of v7, /device:TPU:1, one launch (start us, length us, event | category | flops | bytes accessed | tf_op | source)
XLA Modules:
  0.0 146.3 jit_solution(5406907729931194692)
XLA Ops:
  2.8 3.3 %collective-permute-start.8 = (bf16[2,96,1920]{2,1,0:T(8,128)(2,1)S(1)}, bf16[2,96,1920]{2,1,0:T(8,128)(2,1)S(1)}, u32[]{:S(2)}, u32[]{:S(2)}) collective-permute-start(bf16[2,96,1920]{2,1,0:T(8,128)(2,1)S(1)} %far.1), channel_id=1, source_target_pairs={{0,1},{1,0},{2,3},{3,2},{4,5},{5,4},{6,7},{7,6},{8,9},{9,8},{10,11... | collective-permute-start | bytes 2211848 | tf_op jit(solution)/shard_map/ppermute | solution.py:423
  6.1 1.8 %collective-permute-done.8.far = bf16[2,96,1920]{2,1,0:T(8,128)(2,1)S(1)} collective-permute-done((bf16[2,96,1920]{2,1,0:T(8,128)(2,1)S(1)}, bf16[2,96,1920]{2,1,0:T(8,128)(2,1)S(1)}, u32[]{:S(2)}, u32[]{:S(2)}) %collective-permute-start.8) | collective-permute-done | bytes 737312 | tf_op jit(solution)/shard_map/ppermute | solution.py:423
  8.0 2.8 %pack.1 = bf16[1536,640]{1,0:T(8,128)(2,1)} custom-call(s32[4]{0:T(128)S(1)} %pad_add_fusion.place, bf16[2,96,3840]{2,1,0:T(8,128)(2,1)S(1)} %bitcast.17, bf16[2,96,1920]{2,1,0:T(8,128)(2,1)S(1)} %collective-permute-done.8.far, bf16[2,96,1280]{2,1,0:T(8,128)(2,1)S(1)} %bitcast.20), custom_call_target="tpu_custom_call" | custom-call | bytes 4669456 | tf_op jit(solution)/shard_map/pack/pallas_call | solution.py:61
  10.8 9.2 %all-to-all-start = ((bf16[16,96,640]{2,1,0:T(8,128)(2,1)}), bf16[16,96,640]{2,1,0:T(8,128)(2,1)S(1)}, u32[]{:S(2)}, u32[]{:S(2)}) async-start(bf16[16,96,640]{2,1,0:T(8,128)(2,1)} %bitcast.10), calls=%async_computation | async-start | bytes 3932160 | tf_op jit(solution)/shard_map/all_to_all | solution.py:455
  20.8 1.9 %copy-done.4 = bf16[1280,1280]{1,0:T(8,128)(2,1)S(1)} copy-done((bf16[1280,1280]{1,0:T(8,128)(2,1)S(1)}, bf16[1280,1280]{1,0:T(8,128)(2,1)}, u32[]{:S(2)}) %copy-start.4) | copy-done | bytes 3276824
  24.1 4.8 %local.1 = (bf16[2,96,3840]{2,1,0:T(8,128)(2,1)}, bf16[192,640]{1,0:T(8,128)(2,1)S(1)}, bf16[192,640]{1,0:T(8,128)(2,1)S(1)}) custom-call(s32[4]{0:T(128)S(1)} %pad_add_fusion.place, f32[8]{0:T(128)S(1)} %copy-done.7, bf16[2,96,3840]{2,1,0:T(8,128)(2,1)S(1)} %bitcast.24, bf16[2,96,1280]{2,1,0:T(8,128)(2,1)S(1)} %bitcast.22, ...), custom_call_target="tpu_custom_call" | custom-call | flops 2000000000 | bytes 7209776 | tf_op jit(solution)/shard_map/local/pallas_call | solution.py:61
  28.9 1.5 %collective-permute-done.act_far = bf16[192,640]{1,0:T(8,128)(2,1)S(1)} collective-permute-done((bf16[192,640]{1,0:T(8,128)(2,1)S(1)}, bf16[192,640]{1,0:T(8,128)(2,1)S(1)}, u32[]{:S(2)}, u32[]{:S(2)}) %collective-permute-start) | collective-permute-done | bytes 245792 | tf_op jit(solution)/shard_map/ppermute | solution.py:423
  32.7 2.5 %collective-permute-start.3 = (bf16[160,1280]{1,0:T(8,128)(2,1)S(1)}, bf16[160,1280]{1,0:T(8,128)(2,1)S(1)}, u32[]{:S(2)}, u32[]{:S(2)}) collective-permute-start(bf16[160,1280]{1,0:T(8,128)(2,1)S(1)} %get-tuple-element.43), channel_id=1, source_target_pairs={{0,64},{32,96},{64,0},{96,32},{128,192},{160,224},{192,128},{224,1... | collective-permute-start | bytes 1228808 | tf_op jit(solution)/shard_map/ppermute | solution.py:428
  36.3 7.3 %collective-permute-done.2.a = bf16[160,1280]{1,0:T(8,128)(2,1)S(1)} collective-permute-done((bf16[160,1280]{1,0:T(8,128)(2,1)S(1)}, bf16[160,1280]{1,0:T(8,128)(2,1)S(1)}, u32[]{:S(2)}, u32[]{:S(2)}) %collective-permute-start.2) | collective-permute-done | bytes 409632 | tf_op jit(solution)/shard_map/ppermute | solution.py:428
  43.6 9.8 %collective-permute-done.3.b = bf16[160,1280]{1,0:T(8,128)(2,1)S(1)} collective-permute-done((bf16[160,1280]{1,0:T(8,128)(2,1)S(1)}, bf16[160,1280]{1,0:T(8,128)(2,1)S(1)}, u32[]{:S(2)}, u32[]{:S(2)}) %collective-permute-start.3) | collective-permute-done | bytes 409632 | tf_op jit(solution)/shard_map/ppermute | solution.py:428
  53.6 1.6 %collective-permute-start.5 = (bf16[40,1280]{1,0:T(8,128)(2,1)S(1)}, bf16[40,1280]{1,0:T(8,128)(2,1)S(1)}, u32[]{:S(2)}, u32[]{:S(2)}) collective-permute-start(bf16[40,1280]{1,0:T(8,128)(2,1)S(1)} %get-tuple-element.45), channel_id=1, source_target_pairs={{0,2},{1,3},{2,4},{3,5},{4,6},{5,7},{6,0},{7,1},{8,10},{9,11},{10,... | collective-permute-start | bytes 307208 | tf_op jit(solution)/shard_map/ppermute | solution.py:438
  55.2 2.4 %collective-permute-start.6 = (bf16[40,1280]{1,0:T(8,128)(2,1)S(1)}, bf16[40,1280]{1,0:T(8,128)(2,1)S(1)}, u32[]{:S(2)}, u32[]{:S(2)}) collective-permute-start(bf16[40,1280]{1,0:T(8,128)(2,1)S(1)} %get-tuple-element.46), channel_id=1, source_target_pairs={{0,4},{1,5},{2,6},{3,7},{4,0},{5,1},{6,2},{7,3},{8,12},{9,13},{10,... | collective-permute-start | bytes 307208 | tf_op jit(solution)/shard_map/ppermute | solution.py:438
  58.8 5.8 %all-to-all-done = bf16[16,96,640]{2,1,0:T(8,128)(2,1)S(1)} async-done(((bf16[16,96,640]{2,1,0:T(8,128)(2,1)}), bf16[16,96,640]{2,1,0:T(8,128)(2,1)S(1)}, u32[]{:S(2)}, u32[]{:S(2)}) %all-to-all-start) | async-done | bytes 1966112 | tf_op jit(solution)/shard_map/all_to_all | solution.py:455
  64.6 5.5 %collective-permute-start.9 = (bf16[16,24,640]{2,1,0:T(8,128)(2,1)S(1)}, bf16[16,24,640]{2,1,0:T(8,128)(2,1)S(1)}, u32[]{:S(2)}, u32[]{:S(2)}) collective-permute-start(bf16[16,24,640]{2,1,0:T(8,128)(2,1)S(1)} %slice.4), channel_id=1, source_target_pairs={{0,1},{1,0},{2,3},{3,2},{4,5},{5,4},{6,7},{7,6},{8,9},{9,8},{10,11... | collective-permute-start | bytes 1474568 | tf_op jit(solution)/shard_map/ppermute | solution.py:423
  70.1 3.1 %group.1 = (bf16[3,2,192,640]{3,2,1,0:T(8,128)(2,1)S(1)}, bf16[192,1280]{1,0:T(8,128)(2,1)S(1)}, f32[1536,64]{1,0:T(8,128)S(1)}, bf16[384,640]{1,0:T(8,128)(2,1)S(1)}) custom-call(s32[4]{0:T(128)S(1)} %pad_add_fusion.place, bf16[40,1280]{1,0:T(8,128)(2,1)S(1)} %collective-permute-done.5.after.refs_1_, ...), custom_call_target="tpu_custom_call" | custom-call | flops 99999997952 | bytes 5124112 | tf_op jit(solution)/shard_map/group/pallas_call | solution.py:61
  73.3 2.2 %group_weight.1 = (f32[160,1280]{1,0:T(8,128)S(1)}, bf16[160,1280]{1,0:T(8,128)(2,1)}, bf16[160,1280]{1,0:T(8,128)(2,1)}, bf16[160,1280]{1,0:T(8,128)(2,1)S(1)}, bf16[192,1280]{1,0:T(8,128)(2,1)S(1)}) custom-call(bf16[384,640]{1,0:T(8,128)(2,1)S(1)} %get-tuple-element.51.act, bf16[192,1280]{1,0:T(8,128)(2,1)S(1)} %get-tuple-element.50.cot, ...), custom_call_target="tpu_custom_call" | custom-call | flops 629145600 | bytes 4014080 | tf_op jit(solution)/shard_map/group_weight/pallas_call | solution.py:61
  75.4 2.8 %collective-permute-start.12 = (bf16[160,1280]{1,0:T(8,128)(2,1)}, bf16[160,1280]{1,0:T(8,128)(2,1)S(1)}, u32[]{:S(2)}, u32[]{:S(2)}) collective-permute-start(bf16[160,1280]{1,0:T(8,128)(2,1)} %get-tuple-element.60), channel_id=1, source_target_pairs={{0,4},{1,5},{2,6},{3,7},{4,0},{5,1},{6,2},{7,3},{8,12},{9,13},{10,... | collective-permute-start | bytes 1228808 | tf_op jit(solution)/shard_map/ppermute | solution.py:438
  78.3 5.2 %group_back.1 = bf16[1152,640]{1,0:T(8,128)(2,1)} custom-call(s32[4]{0:T(128)S(1)} %pad_add_fusion.place, f32[1536,64]{1,0:T(8,128)S(1)} %get-tuple-element.48.probs_in, bf16[3,2,192,640]{3,2,1,0:T(8,128)(2,1)S(1)} %get-tuple-element.49.data, bf16[192,1280]{1,0:T(8,128)(2,1)S(1)} %get-tuple-element.50.cot, bf16[192,1280]{1,0:T(8,128)(2,1)S(1)} %get-tuple-element.52.cot_far, ...), custom_call_target="tpu_custom_call" | custom-call | flops 2000000000 | bytes 7602192 | tf_op jit(solution)/shard_map/group_back/pallas_call | solution.py:61
  83.5 5.2 %all-to-all-start.1 = ((bf16[16,72,640]{2,1,0:T(8,128)(2,1)}), bf16[16,72,640]{2,1,0:T(8,128)(2,1)S(1)}, u32[]{:S(2)}, u32[]{:S(2)}) async-start(bf16[16,72,640]{2,1,0:T(8,128)(2,1)} %bitcast.13), calls=%async_computation.1 | async-start | bytes 2949120 | tf_op jit(solution)/shard_map/all_to_all | solution.py:455
  88.7 8.2 %collective-permute-done.12.b = bf16[160,1280]{1,0:T(8,128)(2,1)S(1)} collective-permute-done((bf16[160,1280]{1,0:T(8,128)(2,1)}, bf16[160,1280]{1,0:T(8,128)(2,1)S(1)}, u32[]{:S(2)}, u32[]{:S(2)}) %collective-permute-start.12) | collective-permute-done | bytes 409632 | tf_op jit(solution)/shard_map/ppermute | solution.py:438
  100.5 2.6 %collective-permute-start.15 = (bf16[40,1280]{1,0:T(8,128)(2,1)S(1)}, bf16[40,1280]{1,0:T(8,128)(2,1)S(1)}, u32[]{:S(2)}, u32[]{:S(2)}) collective-permute-start(bf16[40,1280]{1,0:T(8,128)(2,1)S(1)} %get-tuple-element.64), channel_id=1, source_target_pairs={{0,64},{32,96},{64,0},{96,32},{128,192},{160,224},{192,128},{224,1... | collective-permute-start | bytes 307208 | tf_op jit(solution)/shard_map/ppermute | solution.py:428
  104.5 2.1 %collective-permute-done.15.refs_6_ = bf16[40,1280]{1,0:T(8,128)(2,1)S(1)} collective-permute-done((bf16[40,1280]{1,0:T(8,128)(2,1)S(1)}, bf16[40,1280]{1,0:T(8,128)(2,1)S(1)}, u32[]{:S(2)}, u32[]{:S(2)}) %collective-permute-start.15) | collective-permute-done | bytes 102432 | tf_op jit(solution)/shard_map/ppermute | solution.py:428
  107.5 7.9 %collective-permute-start.17 = (bf16[24,1280]{1,0:T(8,128)(2,1)S(1)}, bf16[24,1280]{1,0:T(8,128)(2,1)S(1)}, u32[]{:S(2)}, u32[]{:S(2)}) collective-permute-start(bf16[24,1280]{1,0:T(8,128)(2,1)S(1)} %get-tuple-element.66), channel_id=1, source_target_pairs={{0,0},{1,16},{2,2},{3,18},{4,4},{5,20},{6,6},{7,22},{8,1},{9,17},{... | collective-permute-start | bytes 184328 | tf_op jit(solution)/shard_map/ppermute | solution.py:448
  115.4 6.5 %collective-permute-start.18 = (bf16[24,1280]{1,0:T(8,128)(2,1)S(1)}, bf16[24,1280]{1,0:T(8,128)(2,1)S(1)}, u32[]{:S(2)}, u32[]{:S(2)}) collective-permute-start(bf16[24,1280]{1,0:T(8,128)(2,1)S(1)} %get-tuple-element.67), channel_id=1, source_target_pairs={{0,1},{1,17},{2,3},{3,19},{4,5},{5,21},{6,7},{7,23},{8,8},{9,24},{... | collective-permute-start | bytes 184328 | tf_op jit(solution)/shard_map/ppermute | solution.py:448
  122.0 2.2 %collective-permute-start.20 = (bf16[24,1280]{1,0:T(8,128)(2,1)S(1)}, bf16[24,1280]{1,0:T(8,128)(2,1)S(1)}, u32[]{:S(2)}, u32[]{:S(2)}) collective-permute-start(bf16[24,1280]{1,0:T(8,128)(2,1)S(1)} %get-tuple-element.69), channel_id=1, source_target_pairs={{0,9},{1,25},{2,11},{3,27},{4,13},{5,29},{6,15},{7,31},{8,0},{9,16... | collective-permute-start | bytes 184328 | tf_op jit(solution)/shard_map/ppermute | solution.py:448
  125.7 1.9 %collective-permute-done.18.b = bf16[24,1280]{1,0:T(8,128)(2,1)S(1)} collective-permute-done((bf16[24,1280]{1,0:T(8,128)(2,1)S(1)}, bf16[24,1280]{1,0:T(8,128)(2,1)S(1)}, u32[]{:S(2)}, u32[]{:S(2)}) %collective-permute-start.18) | collective-permute-done | bytes 61472 | tf_op jit(solution)/shard_map/ppermute | solution.py:448
  127.6 2.7 %collective-permute-done.19.c = bf16[24,1280]{1,0:T(8,128)(2,1)S(1)} collective-permute-done((bf16[24,1280]{1,0:T(8,128)(2,1)S(1)}, bf16[24,1280]{1,0:T(8,128)(2,1)S(1)}, u32[]{:S(2)}, u32[]{:S(2)}) %collective-permute-start.19) | collective-permute-done | bytes 61472 | tf_op jit(solution)/shard_map/ppermute | solution.py:448
  130.3 1.6 %collective-permute-done.20.d = bf16[24,1280]{1,0:T(8,128)(2,1)S(1)} collective-permute-done((bf16[24,1280]{1,0:T(8,128)(2,1)S(1)}, bf16[24,1280]{1,0:T(8,128)(2,1)S(1)}, u32[]{:S(2)}, u32[]{:S(2)}) %collective-permute-start.20) | collective-permute-done | bytes 61472 | tf_op jit(solution)/shard_map/ppermute | solution.py:448
  132.7 4.1 %all-to-all-start.2 = ((bf16[8,24,1280]{2,1,0:T(8,128)(2,1)}), bf16[8,24,1280]{2,1,0:T(8,128)(2,1)S(1)}, u32[]{:S(2)}, u32[]{:S(2)}) async-start(bf16[8,24,1280]{2,1,0:T(8,128)(2,1)} %sum_z.1), calls=%async_computation.2 | async-start | bytes 983040 | tf_op jit(solution)/shard_map/all_to_all | solution.py:617
  136.8 2.2 %collective-permute-done.10.far = bf16[2,96,1920]{2,1,0:T(8,128)(2,1)S(1)} collective-permute-done((bf16[2,96,1920]{2,1,0:T(8,128)(2,1)S(1)}, bf16[2,96,1920]{2,1,0:T(8,128)(2,1)S(1)}, u32[]{:S(2)}, u32[]{:S(2)}) %collective-permute-start.10) | collective-permute-done | bytes 737312 | tf_op jit(solution)/shard_map/ppermute | solution.py:423
  139.0 1.7 %merge.1 = (bf16[2,96,3840]{2,1,0:T(8,128)(2,1)}, f32[8,128]{1,0:T(8,128)S(1)}) custom-call(s32[4]{0:T(128)S(1)} %pad_add_fusion.place, bf16[2,96,1920]{2,1,0:T(8,128)(2,1)S(1)} %get-tuple-element.53.mine.after, bf16[2,96,1920]{2,1,0:T(8,128)(2,1)S(1)} %collective-permute-done.10.far), custom_call_target="tpu_custom_call" | custom-call | bytes 2953232 | tf_op jit(solution)/shard_map/merge/pallas_call | solution.py:61
  140.7 4.7 %all-to-all-done.2.pieces = bf16[8,24,1280]{2,1,0:T(8,128)(2,1)S(1)} async-done(((bf16[8,24,1280]{2,1,0:T(8,128)(2,1)}), bf16[8,24,1280]{2,1,0:T(8,128)(2,1)S(1)}, u32[]{:S(2)}, u32[]{:S(2)}) %all-to-all-start.2) | async-done | bytes 491552 | tf_op jit(solution)/shard_map/all_to_all | solution.py:617
  (52 shorter events, 18.4 us)
Async XLA Ops:
  0.8 1.4 copy-start
  2.1 5.8 %copy-start.1 = (bf16[1,2,96,3840]{3,2,1,0:T(8,128)(2,1)S(1)}, bf16[1,2,96,3840]{3,2,1,0:T(8,128)(2,1)}, u32[]{:S(2)}) copy-start(bf16[1,2,96,3840]{3,2,1,0:T(8,128)(2,1)} %param.8) | copy-start | bytes 4423684
  2.1 5.8 %copy-start.3 = (bf16[1,2,96,1280]{3,2,1,0:T(8,128)(2,1)S(1)}, bf16[1,2,96,1280]{3,2,1,0:T(8,128)(2,1)}, u32[]{:S(2)}) copy-start(bf16[1,2,96,1280]{3,2,1,0:T(8,128)(2,1)} %param.11) | copy-start | bytes 1474564
  2.8 5.2 %collective-permute-start.8 = (bf16[2,96,1920]{2,1,0:T(8,128)(2,1)S(1)}, bf16[2,96,1920]{2,1,0:T(8,128)(2,1)S(1)}, u32[]{:S(2)}, u32[]{:S(2)}) collective-permute-start(bf16[2,96,1920]{2,1,0:T(8,128)(2,1)S(1)} %far.1), channel_id=1, source_target_pairs={{0,1},{1,0},{2,3},{3,2},{4,5},{5,4},{6,7},{7,6},{8,9},{9,8},{10,11... | collective-permute-start | bytes 2211848 | tf_op jit(solution)/shard_map/ppermute | solution.py:423
  10.8 10.0 %copy-start.6 = (s32[1,2,96]{2,1,0:T(2,128)S(1)}, s32[1,2,96]{2,1,0:T(2,128)}, u32[]{:S(2)}) copy-start(s32[1,2,96]{2,1,0:T(2,128)} %param.9) | copy-start | bytes 2308
  10.8 10.0 %copy-start.7 = (f32[8]{0:T(128)S(1)}, f32[8]{0:T(128)}, u32[]{:S(2)}) copy-start(f32[8]{0:T(128)} %slopes.1) | copy-start | bytes 100
  10.8 53.7 %all-to-all-start = ((bf16[16,96,640]{2,1,0:T(8,128)(2,1)}), bf16[16,96,640]{2,1,0:T(8,128)(2,1)S(1)}, u32[]{:S(2)}, u32[]{:S(2)}) async-start(bf16[16,96,640]{2,1,0:T(8,128)(2,1)} %bitcast.10), calls=%async_computation | async-start | bytes 3932160 | tf_op jit(solution)/shard_map/all_to_all | solution.py:455
  20.0 10.3 %collective-permute-start.1 = (bf16[192,1280]{1,0:T(8,128)(2,1)S(1)}, bf16[192,1280]{1,0:T(8,128)(2,1)S(1)}, u32[]{:S(2)}, u32[]{:S(2)}) collective-permute-start(bf16[192,1280]{1,0:T(8,128)(2,1)S(1)} %bitcast.21), channel_id=1, source_target_pairs={{0,1},{1,0},{2,3},{3,2},{4,5},{5,4},{6,7},{7,6},{8,9},{9,8},{10,11... | collective-permute-start | bytes 1474568 | tf_op jit(solution)/shard_map/ppermute | solution.py:423
  20.8 1.9 %copy-start.4 = (bf16[1280,1280]{1,0:T(8,128)(2,1)S(1)}, bf16[1280,1280]{1,0:T(8,128)(2,1)}, u32[]{:S(2)}) copy-start(bf16[1280,1280]{1,0:T(8,128)(2,1)} %weight.2) | copy-start | bytes 9830404
  28.8 1.5 %collective-permute-start = (bf16[192,640]{1,0:T(8,128)(2,1)S(1)}, bf16[192,640]{1,0:T(8,128)(2,1)S(1)}, u32[]{:S(2)}, u32[]{:S(2)}) collective-permute-start(bf16[192,640]{1,0:T(8,128)(2,1)S(1)} %get-tuple-element.40), channel_id=1, source_target_pairs={{0,1},{1,0},{2,3},{3,2},{4,5},{5,4},{6,7},{7,6},{8,9},{9,8},{10,11... | collective-permute-start | bytes 737288 | tf_op jit(solution)/shard_map/ppermute | solution.py:423
  31.4 12.2 %collective-permute-start.2 = (bf16[160,1280]{1,0:T(8,128)(2,1)S(1)}, bf16[160,1280]{1,0:T(8,128)(2,1)S(1)}, u32[]{:S(2)}, u32[]{:S(2)}) collective-permute-start(bf16[160,1280]{1,0:T(8,128)(2,1)S(1)} %get-tuple-element.42), channel_id=1, source_target_pairs={{0,32},{32,64},{64,96},{96,0},{128,160},{160,192},{192,224},{224,1... | collective-permute-start | bytes 1228808 | tf_op jit(solution)/shard_map/ppermute | solution.py:428
  32.7 20.7 %collective-permute-start.3 = (bf16[160,1280]{1,0:T(8,128)(2,1)S(1)}, bf16[160,1280]{1,0:T(8,128)(2,1)S(1)}, u32[]{:S(2)}, u32[]{:S(2)}) collective-permute-start(bf16[160,1280]{1,0:T(8,128)(2,1)S(1)} %get-tuple-element.43), channel_id=1, source_target_pairs={{0,64},{32,96},{64,0},{96,32},{128,192},{160,224},{192,128},{224,1... | collective-permute-start | bytes 1228808 | tf_op jit(solution)/shard_map/ppermute | solution.py:428
  35.2 18.2 %collective-permute-start.4 = (bf16[160,1280]{1,0:T(8,128)(2,1)S(1)}, bf16[160,1280]{1,0:T(8,128)(2,1)S(1)}, u32[]{:S(2)}, u32[]{:S(2)}) collective-permute-start(bf16[160,1280]{1,0:T(8,128)(2,1)S(1)} %get-tuple-element.44), channel_id=1, source_target_pairs={{0,96},{32,0},{64,32},{96,64},{128,224},{160,128},{192,160},{224,1... | collective-permute-start | bytes 1228808 | tf_op jit(solution)/shard_map/ppermute | solution.py:428
  53.6 16.5 %collective-permute-start.5 = (bf16[40,1280]{1,0:T(8,128)(2,1)S(1)}, bf16[40,1280]{1,0:T(8,128)(2,1)S(1)}, u32[]{:S(2)}, u32[]{:S(2)}) collective-permute-start(bf16[40,1280]{1,0:T(8,128)(2,1)S(1)} %get-tuple-element.45), channel_id=1, source_target_pairs={{0,2},{1,3},{2,4},{3,5},{4,6},{5,7},{6,0},{7,1},{8,10},{9,11},{10,... | collective-permute-start | bytes 307208 | tf_op jit(solution)/shard_map/ppermute | solution.py:438
  55.2 14.9 %collective-permute-start.6 = (bf16[40,1280]{1,0:T(8,128)(2,1)S(1)}, bf16[40,1280]{1,0:T(8,128)(2,1)S(1)}, u32[]{:S(2)}, u32[]{:S(2)}) collective-permute-start(bf16[40,1280]{1,0:T(8,128)(2,1)S(1)} %get-tuple-element.46), channel_id=1, source_target_pairs={{0,4},{1,5},{2,6},{3,7},{4,0},{5,1},{6,2},{7,3},{8,12},{9,13},{10,... | collective-permute-start | bytes 307208 | tf_op jit(solution)/shard_map/ppermute | solution.py:438
  57.6 12.5 %collective-permute-start.7 = (bf16[40,1280]{1,0:T(8,128)(2,1)S(1)}, bf16[40,1280]{1,0:T(8,128)(2,1)S(1)}, u32[]{:S(2)}, u32[]{:S(2)}) collective-permute-start(bf16[40,1280]{1,0:T(8,128)(2,1)S(1)} %get-tuple-element.47), channel_id=1, source_target_pairs={{0,6},{1,7},{2,0},{3,1},{4,2},{5,3},{6,4},{7,5},{8,14},{9,15},{10,... | collective-permute-start | bytes 307208 | tf_op jit(solution)/shard_map/ppermute | solution.py:438
  64.6 8.6 %collective-permute-start.9 = (bf16[16,24,640]{2,1,0:T(8,128)(2,1)S(1)}, bf16[16,24,640]{2,1,0:T(8,128)(2,1)S(1)}, u32[]{:S(2)}, u32[]{:S(2)}) collective-permute-start(bf16[16,24,640]{2,1,0:T(8,128)(2,1)S(1)} %slice.4), channel_id=1, source_target_pairs={{0,1},{1,0},{2,3},{3,2},{4,5},{5,4},{6,7},{7,6},{8,9},{9,8},{10,11... | collective-permute-start | bytes 1474568 | tf_op jit(solution)/shard_map/ppermute | solution.py:423
  70.1 8.2 %copy-start.2 = (bf16[1280,1280]{1,0:T(8,128)(2,1)S(1)}, bf16[1280,1280]{1,0:T(8,128)(2,1)}, u32[]{:S(2)}) copy-start(bf16[1280,1280]{1,0:T(8,128)(2,1)} %weight.3) | copy-start | bytes 9830404
  75.4 8.1 %copy-start.8 = (f32[160,1280]{1,0:T(8,128)}, f32[160,1280]{1,0:T(8,128)S(1)}, u32[]{:S(2)}) copy-start(f32[160,1280]{1,0:T(8,128)S(1)} %get-tuple-element.58.own) | copy-start | bytes 2457604
  75.4 13.2 %collective-permute-start.11 = (bf16[160,1280]{1,0:T(8,128)(2,1)}, bf16[160,1280]{1,0:T(8,128)(2,1)S(1)}, u32[]{:S(2)}, u32[]{:S(2)}) collective-permute-start(bf16[160,1280]{1,0:T(8,128)(2,1)} %get-tuple-element.59), channel_id=1, source_target_pairs={{0,2},{1,3},{2,4},{3,5},{4,6},{5,7},{6,0},{7,1},{8,10},{9,11},{10,... | collective-permute-start | bytes 1228808 | tf_op jit(solution)/shard_map/ppermute | solution.py:438
  75.4 21.5 %collective-permute-start.12 = (bf16[160,1280]{1,0:T(8,128)(2,1)}, bf16[160,1280]{1,0:T(8,128)(2,1)S(1)}, u32[]{:S(2)}, u32[]{:S(2)}) collective-permute-start(bf16[160,1280]{1,0:T(8,128)(2,1)} %get-tuple-element.60), channel_id=1, source_target_pairs={{0,4},{1,5},{2,6},{3,7},{4,0},{5,1},{6,2},{7,3},{8,12},{9,13},{10,... | collective-permute-start | bytes 1228808 | tf_op jit(solution)/shard_map/ppermute | solution.py:438
  78.3 18.8 %collective-permute-start.13 = (bf16[160,1280]{1,0:T(8,128)(2,1)S(1)}, bf16[160,1280]{1,0:T(8,128)(2,1)}, u32[]{:S(2)}, u32[]{:S(2)}) collective-permute-start(bf16[160,1280]{1,0:T(8,128)(2,1)S(1)} %get-tuple-element.61), channel_id=1, source_target_pairs={{0,6},{1,7},{2,0},{3,1},{4,2},{5,3},{6,4},{7,5},{8,14},{9,15},{10,... | collective-permute-start | bytes 1228808 | tf_op jit(solution)/shard_map/ppermute | solution.py:438
  83.5 40.7 %all-to-all-start.1 = ((bf16[16,72,640]{2,1,0:T(8,128)(2,1)}), bf16[16,72,640]{2,1,0:T(8,128)(2,1)S(1)}, u32[]{:S(2)}, u32[]{:S(2)}) async-start(bf16[16,72,640]{2,1,0:T(8,128)(2,1)} %bitcast.13), calls=%async_computation.1 | async-start | bytes 2949120 | tf_op jit(solution)/shard_map/all_to_all | solution.py:455
  99.4 5.1 %collective-permute-start.14 = (bf16[40,1280]{1,0:T(8,128)(2,1)S(1)}, bf16[40,1280]{1,0:T(8,128)(2,1)S(1)}, u32[]{:S(2)}, u32[]{:S(2)}) collective-permute-start(bf16[40,1280]{1,0:T(8,128)(2,1)S(1)} %get-tuple-element.63), channel_id=1, source_target_pairs={{0,32},{32,64},{64,96},{96,0},{128,160},{160,192},{192,224},{224,1... | collective-permute-start | bytes 307208 | tf_op jit(solution)/shard_map/ppermute | solution.py:428
  100.5 6.0 %collective-permute-start.15 = (bf16[40,1280]{1,0:T(8,128)(2,1)S(1)}, bf16[40,1280]{1,0:T(8,128)(2,1)S(1)}, u32[]{:S(2)}, u32[]{:S(2)}) collective-permute-start(bf16[40,1280]{1,0:T(8,128)(2,1)S(1)} %get-tuple-element.64), channel_id=1, source_target_pairs={{0,64},{32,96},{64,0},{96,32},{128,192},{160,224},{192,128},{224,1... | collective-permute-start | bytes 307208 | tf_op jit(solution)/shard_map/ppermute | solution.py:428
  103.2 4.2 %collective-permute-start.16 = (bf16[40,1280]{1,0:T(8,128)(2,1)S(1)}, bf16[40,1280]{1,0:T(8,128)(2,1)S(1)}, u32[]{:S(2)}, u32[]{:S(2)}) collective-permute-start(bf16[40,1280]{1,0:T(8,128)(2,1)S(1)} %get-tuple-element.65), channel_id=1, source_target_pairs={{0,96},{32,0},{64,32},{96,64},{128,224},{160,128},{192,160},{224,1... | collective-permute-start | bytes 307208 | tf_op jit(solution)/shard_map/ppermute | solution.py:428
  107.5 18.2 %collective-permute-start.17 = (bf16[24,1280]{1,0:T(8,128)(2,1)S(1)}, bf16[24,1280]{1,0:T(8,128)(2,1)S(1)}, u32[]{:S(2)}, u32[]{:S(2)}) collective-permute-start(bf16[24,1280]{1,0:T(8,128)(2,1)S(1)} %get-tuple-element.66), channel_id=1, source_target_pairs={{0,0},{1,16},{2,2},{3,18},{4,4},{5,20},{6,6},{7,22},{8,1},{9,17},{... | collective-permute-start | bytes 184328 | tf_op jit(solution)/shard_map/ppermute | solution.py:448
  115.4 12.2 %collective-permute-start.18 = (bf16[24,1280]{1,0:T(8,128)(2,1)S(1)}, bf16[24,1280]{1,0:T(8,128)(2,1)S(1)}, u32[]{:S(2)}, u32[]{:S(2)}) collective-permute-start(bf16[24,1280]{1,0:T(8,128)(2,1)S(1)} %get-tuple-element.67), channel_id=1, source_target_pairs={{0,1},{1,17},{2,3},{3,19},{4,5},{5,21},{6,7},{7,23},{8,8},{9,24},{... | collective-permute-start | bytes 184328 | tf_op jit(solution)/shard_map/ppermute | solution.py:448
  121.9 8.4 %collective-permute-start.19 = (bf16[24,1280]{1,0:T(8,128)(2,1)S(1)}, bf16[24,1280]{1,0:T(8,128)(2,1)S(1)}, u32[]{:S(2)}, u32[]{:S(2)}) collective-permute-start(bf16[24,1280]{1,0:T(8,128)(2,1)S(1)} %get-tuple-element.68), channel_id=1, source_target_pairs={{0,8},{1,24},{2,10},{3,26},{4,12},{5,28},{6,14},{7,30},{8,9},{9,25... | collective-permute-start | bytes 184328 | tf_op jit(solution)/shard_map/ppermute | solution.py:448
  122.0 9.9 %collective-permute-start.20 = (bf16[24,1280]{1,0:T(8,128)(2,1)S(1)}, bf16[24,1280]{1,0:T(8,128)(2,1)S(1)}, u32[]{:S(2)}, u32[]{:S(2)}) collective-permute-start(bf16[24,1280]{1,0:T(8,128)(2,1)S(1)} %get-tuple-element.69), channel_id=1, source_target_pairs={{0,9},{1,25},{2,11},{3,27},{4,13},{5,29},{6,15},{7,31},{8,0},{9,16... | collective-permute-start | bytes 184328 | tf_op jit(solution)/shard_map/ppermute | solution.py:448
  132.7 12.8 %all-to-all-start.2 = ((bf16[8,24,1280]{2,1,0:T(8,128)(2,1)}), bf16[8,24,1280]{2,1,0:T(8,128)(2,1)S(1)}, u32[]{:S(2)}, u32[]{:S(2)}) async-start(bf16[8,24,1280]{2,1,0:T(8,128)(2,1)} %sum_z.1), calls=%async_computation.2 | async-start | bytes 983040 | tf_op jit(solution)/shard_map/all_to_all | solution.py:617
  136.8 2.2 %collective-permute-start.10 = (bf16[2,96,1920]{2,1,0:T(8,128)(2,1)S(1)}, bf16[2,96,1920]{2,1,0:T(8,128)(2,1)S(1)}, u32[]{:S(2)}, u32[]{:S(2)}) collective-permute-start(bf16[2,96,1920]{2,1,0:T(8,128)(2,1)S(1)} %get-tuple-element.54), channel_id=1, source_target_pairs={{0,1},{1,0},{2,3},{3,2},{4,5},{5,4},{6,7},{7,6},{8,9},{9,8},{10,11... | collective-permute-start | bytes 2211848 | tf_op jit(solution)/shard_map/ppermute | solution.py:423
  (2 other events, 2.5 us)

commit v8 on v7

--- a/solution.py
+++ b/solution.py
@@ -388,18 +388,25 @@
     return total
 
 
+def folded(x):
+    return jnp.concatenate([x[:, :640], x[:, 640:]], axis=0)
+
+
 def first_sum_kernel(own, a, b, c, *chunks):
     total = sum_of(own, a, b, c)
     for d, ref in enumerate(chunks):
-        ref[...] = total[40 * d : 40 * d + 40].astype(ref.dtype)
+        ref[...] = folded(total[40 * d : 40 * d + 40]).astype(ref.dtype)
 
 
 def second_sum_kernel(*refs):
     local, total, chunks = sum_of(*refs[:4]), sum_of(*refs[4:8]), refs[8:]
+    blank = jnp.zeros((4, 640), F32)
     for d, ref in enumerate(chunks):
-        rows = slice(10 * d, 10 * d + 10)
-        both = jnp.concatenate([local[rows], total[rows], jnp.zeros((4, 1280), F32)], axis=0)
-        ref[...] = both.astype(BF16)
+        pieces = []
+        for half in range(2):
+            rows = slice(40 * half + 10 * d, 40 * half + 10 * d + 10)
+            pieces += [local[rows], total[rows], blank]
+        ref[...] = jnp.concatenate(pieces, axis=0).astype(BF16)
 
 
 def sum_z_kernel(after, a, b, c, d, out):
@@ -411,8 +418,10 @@
 def final_kernel(scale, after, pieces, local, glob):
     for x in range(4):
         both = (pieces[x].astype(F32) + pieces[4 + x].astype(F32)) * scale
-        local[10 * x : 10 * x + 10, :] = both[:10]
-        glob[10 * x : 10 * x + 10, :] = both[10:20]
+        for half in range(2):
+            cols, top = slice(640 * half, 640 * half + 640), 24 * half
+            local[10 * x : 10 * x + 10, cols] = both[top : top + 10]
+            glob[10 * x : 10 * x + 10, cols] = both[top + 10 : top + 20]
 
 
 def chip(z, y, c):
@@ -467,7 +476,7 @@
     cotangent = cotangent.reshape(2, 96, 1280)
     flat_cot = cotangent.reshape(192, 1280)
     positions = positions.reshape(2, 96)
-    first_sums = [sds((40, 1280), F32)] + [sds((40, 1280), BF16)] * 3
+    first_sums = [sds((80, 640), F32)] + [sds((80, 640), BF16)] * 3
     partials = [sds((160, 1280), F32)] + [sds((160, 1280), BF16)] * 3
 
     (other,) = call(
@@ -592,7 +601,7 @@
     )
     chunks = call(
         second_sum_kernel,
-        [sds((24, 1280), BF16)] * 4,
+        [sds((48, 640), BF16)] * 4,
         *local_parts,
         own,
         along_x(one, 1),
@@ -608,7 +617,7 @@
     )
     (sums,) = call(
         sum_z_kernel,
-        [sds((8, 24, 1280), BF16)],
+        [sds((8, 48, 640), BF16)],
         mine,
         *[to_owner(chunk, d) for d, chunk in enumerate(chunks)],
         unread=(0,),

time: 147 us -> 147 us (level)
  no operation moved by 1% of the time
where the time goes in v8:
time: 147 us; the launch traced here: 146 us
  starting transfers between devices  62.6 us (43%)
  waiting for transfers between devices  50.7 us (34%)
  Pallas kernels  26.1 us (18%)
  local copies, waits for them, and re-layouts  5.89 us (4%)
    pallas_call x14, Pallas kernels, call(): pl.pallas_call(kernel, out_shape=outs, in_specs=specs, out_specs=[pl.Bloc...  26.1 us
    ppermute x6, waiting for transfers between devices, along_x(): return lax.ppermute(a, 'dp', pairs)  20.1 us
    ppermute x4, starting transfers between devices, to_owner(): return lax.ppermute(a, 'tok', pairs)  16.7 us
    all_to_all x2, starting transfers between devices, exchange(): lax.all_to_all(a, 'tok', split_axis=0, concat_axis=0, axis_index_groups=C...  14.3 us
    ppermute x6, starting transfers between devices, along_x(): return lax.ppermute(a, 'dp', pairs)  9.78 us
    ppermute x5, starting transfers between devices, swap_cores(): return lax.ppermute(a, 'tok', [(i, i ^ 1) for i in range(32)])  9.65 us
    ppermute x6, waiting for transfers between devices, along_y(): return lax.ppermute(a, 'tok', pairs)  8.44 us
    ppermute x6, starting transfers between devices, along_y(): return lax.ppermute(a, 'tok', pairs)  8.07 us
  transfers between devices with their start and end apart: 24, of which 15 were waited for; matrix products, arithmetic and copies ran while one was open for 0% of the time, Pallas kernels for 13%

profile of v8, /device:TPU:1, one launch (start us, length us, event | category | flops | bytes accessed | tf_op | source)
XLA Modules:
  0.0 146.3 jit_solution(535222008496474542)
XLA Ops:
  2.8 3.3 %collective-permute-start.8 = (bf16[2,96,1920]{2,1,0:T(8,128)(2,1)S(1)}, bf16[2,96,1920]{2,1,0:T(8,128)(2,1)S(1)}, u32[]{:S(2)}, u32[]{:S(2)}) collective-permute-start(bf16[2,96,1920]{2,1,0:T(8,128)(2,1)S(1)} %far.1), channel_id=1, source_target_pairs={{0,1},{1,0},{2,3},{3,2},{4,5},{5,4},{6,7},{7,6},{8,9},{9,8},{10,11... | collective-permute-start | bytes 2211848 | tf_op jit(solution)/shard_map/ppermute | solution.py:432
  6.1 1.8 %collective-permute-done.8.far = bf16[2,96,1920]{2,1,0:T(8,128)(2,1)S(1)} collective-permute-done((bf16[2,96,1920]{2,1,0:T(8,128)(2,1)S(1)}, bf16[2,96,1920]{2,1,0:T(8,128)(2,1)S(1)}, u32[]{:S(2)}, u32[]{:S(2)}) %collective-permute-start.8) | collective-permute-done | bytes 737312 | tf_op jit(solution)/shard_map/ppermute | solution.py:432
  8.0 2.8 %pack.1 = bf16[1536,640]{1,0:T(8,128)(2,1)} custom-call(s32[4]{0:T(128)S(1)} %pad_add_fusion.place, bf16[2,96,3840]{2,1,0:T(8,128)(2,1)S(1)} %bitcast.17, bf16[2,96,1920]{2,1,0:T(8,128)(2,1)S(1)} %collective-permute-done.8.far, bf16[2,96,1280]{2,1,0:T(8,128)(2,1)S(1)} %bitcast.20), custom_call_target="tpu_custom_call" | custom-call | bytes 4669456 | tf_op jit(solution)/shard_map/pack/pallas_call | solution.py:61
  10.8 9.2 %all-to-all-start = ((bf16[16,96,640]{2,1,0:T(8,128)(2,1)}), bf16[16,96,640]{2,1,0:T(8,128)(2,1)S(1)}, u32[]{:S(2)}, u32[]{:S(2)}) async-start(bf16[16,96,640]{2,1,0:T(8,128)(2,1)} %bitcast.10), calls=%async_computation | async-start | bytes 3932160 | tf_op jit(solution)/shard_map/all_to_all | solution.py:464
  20.8 1.9 %copy-done.4 = bf16[1280,1280]{1,0:T(8,128)(2,1)S(1)} copy-done((bf16[1280,1280]{1,0:T(8,128)(2,1)S(1)}, bf16[1280,1280]{1,0:T(8,128)(2,1)}, u32[]{:S(2)}) %copy-start.4) | copy-done | bytes 3276824
  24.1 4.8 %local.1 = (bf16[2,96,3840]{2,1,0:T(8,128)(2,1)}, bf16[192,640]{1,0:T(8,128)(2,1)S(1)}, bf16[192,640]{1,0:T(8,128)(2,1)S(1)}) custom-call(s32[4]{0:T(128)S(1)} %pad_add_fusion.place, f32[8]{0:T(128)S(1)} %copy-done.7, bf16[2,96,3840]{2,1,0:T(8,128)(2,1)S(1)} %bitcast.24, bf16[2,96,1280]{2,1,0:T(8,128)(2,1)S(1)} %bitcast.22, ...), custom_call_target="tpu_custom_call" | custom-call | flops 2000000000 | bytes 7209776 | tf_op jit(solution)/shard_map/local/pallas_call | solution.py:61
  28.9 1.5 %collective-permute-done.act_far = bf16[192,640]{1,0:T(8,128)(2,1)S(1)} collective-permute-done((bf16[192,640]{1,0:T(8,128)(2,1)S(1)}, bf16[192,640]{1,0:T(8,128)(2,1)S(1)}, u32[]{:S(2)}, u32[]{:S(2)}) %collective-permute-start) | collective-permute-done | bytes 245792 | tf_op jit(solution)/shard_map/ppermute | solution.py:432
  32.7 2.5 %collective-permute-start.3 = (bf16[160,1280]{1,0:T(8,128)(2,1)S(1)}, bf16[160,1280]{1,0:T(8,128)(2,1)S(1)}, u32[]{:S(2)}, u32[]{:S(2)}) collective-permute-start(bf16[160,1280]{1,0:T(8,128)(2,1)S(1)} %get-tuple-element.43), channel_id=1, source_target_pairs={{0,64},{32,96},{64,0},{96,32},{128,192},{160,224},{192,128},{224,1... | collective-permute-start | bytes 1228808 | tf_op jit(solution)/shard_map/ppermute | solution.py:437
  36.3 7.3 %collective-permute-done.2.a = bf16[160,1280]{1,0:T(8,128)(2,1)S(1)} collective-permute-done((bf16[160,1280]{1,0:T(8,128)(2,1)S(1)}, bf16[160,1280]{1,0:T(8,128)(2,1)S(1)}, u32[]{:S(2)}, u32[]{:S(2)}) %collective-permute-start.2) | collective-permute-done | bytes 409632 | tf_op jit(solution)/shard_map/ppermute | solution.py:437
  43.6 9.8 %collective-permute-done.3.b = bf16[160,1280]{1,0:T(8,128)(2,1)S(1)} collective-permute-done((bf16[160,1280]{1,0:T(8,128)(2,1)S(1)}, bf16[160,1280]{1,0:T(8,128)(2,1)S(1)}, u32[]{:S(2)}, u32[]{:S(2)}) %collective-permute-start.3) | collective-permute-done | bytes 409632 | tf_op jit(solution)/shard_map/ppermute | solution.py:437
  53.6 1.6 %collective-permute-start.5 = (bf16[80,640]{1,0:T(8,128)(2,1)S(1)}, bf16[80,640]{1,0:T(8,128)(2,1)S(1)}, u32[]{:S(2)}, u32[]{:S(2)}) collective-permute-start(bf16[80,640]{1,0:T(8,128)(2,1)S(1)} %get-tuple-element.45), channel_id=1, source_target_pairs={{0,2},{1,3},{2,4},{3,5},{4,6},{5,7},{6,0},{7,1},{8,10},{9,11},{10,... | collective-permute-start | bytes 307208 | tf_op jit(solution)/shard_map/ppermute | solution.py:447
  55.2 2.4 %collective-permute-start.6 = (bf16[80,640]{1,0:T(8,128)(2,1)S(1)}, bf16[80,640]{1,0:T(8,128)(2,1)S(1)}, u32[]{:S(2)}, u32[]{:S(2)}) collective-permute-start(bf16[80,640]{1,0:T(8,128)(2,1)S(1)} %get-tuple-element.46), channel_id=1, source_target_pairs={{0,4},{1,5},{2,6},{3,7},{4,0},{5,1},{6,2},{7,3},{8,12},{9,13},{10,... | collective-permute-start | bytes 307208 | tf_op jit(solution)/shard_map/ppermute | solution.py:447
  58.8 5.8 %all-to-all-done = bf16[16,96,640]{2,1,0:T(8,128)(2,1)S(1)} async-done(((bf16[16,96,640]{2,1,0:T(8,128)(2,1)}), bf16[16,96,640]{2,1,0:T(8,128)(2,1)S(1)}, u32[]{:S(2)}, u32[]{:S(2)}) %all-to-all-start) | async-done | bytes 1966112 | tf_op jit(solution)/shard_map/all_to_all | solution.py:464
  64.6 5.5 %collective-permute-start.9 = (bf16[16,24,640]{2,1,0:T(8,128)(2,1)S(1)}, bf16[16,24,640]{2,1,0:T(8,128)(2,1)S(1)}, u32[]{:S(2)}, u32[]{:S(2)}) collective-permute-start(bf16[16,24,640]{2,1,0:T(8,128)(2,1)S(1)} %slice.4), channel_id=1, source_target_pairs={{0,1},{1,0},{2,3},{3,2},{4,5},{5,4},{6,7},{7,6},{8,9},{9,8},{10,11... | collective-permute-start | bytes 1474568 | tf_op jit(solution)/shard_map/ppermute | solution.py:432
  70.1 3.1 %group.1 = (bf16[3,2,192,640]{3,2,1,0:T(8,128)(2,1)S(1)}, bf16[192,1280]{1,0:T(8,128)(2,1)S(1)}, f32[1536,64]{1,0:T(8,128)S(1)}, bf16[384,640]{1,0:T(8,128)(2,1)S(1)}) custom-call(s32[4]{0:T(128)S(1)} %pad_add_fusion.place, bf16[80,640]{1,0:T(8,128)(2,1)S(1)} %collective-permute-done.5.after.refs_1_, ...), custom_call_target="tpu_custom_call" | custom-call | flops 99999997952 | bytes 5124112 | tf_op jit(solution)/shard_map/group/pallas_call | solution.py:61
  73.3 2.2 %group_weight.1 = (f32[160,1280]{1,0:T(8,128)S(1)}, bf16[160,1280]{1,0:T(8,128)(2,1)}, bf16[160,1280]{1,0:T(8,128)(2,1)}, bf16[160,1280]{1,0:T(8,128)(2,1)S(1)}, bf16[192,1280]{1,0:T(8,128)(2,1)S(1)}) custom-call(bf16[384,640]{1,0:T(8,128)(2,1)S(1)} %get-tuple-element.51.act, bf16[192,1280]{1,0:T(8,128)(2,1)S(1)} %get-tuple-element.50.cot, ...), custom_call_target="tpu_custom_call" | custom-call | flops 629145600 | bytes 4014080 | tf_op jit(solution)/shard_map/group_weight/pallas_call | solution.py:61
  75.4 2.8 %collective-permute-start.12 = (bf16[160,1280]{1,0:T(8,128)(2,1)}, bf16[160,1280]{1,0:T(8,128)(2,1)S(1)}, u32[]{:S(2)}, u32[]{:S(2)}) collective-permute-start(bf16[160,1280]{1,0:T(8,128)(2,1)} %get-tuple-element.60), channel_id=1, source_target_pairs={{0,4},{1,5},{2,6},{3,7},{4,0},{5,1},{6,2},{7,3},{8,12},{9,13},{10,... | collective-permute-start | bytes 1228808 | tf_op jit(solution)/shard_map/ppermute | solution.py:447
  78.3 5.2 %group_back.1 = bf16[1152,640]{1,0:T(8,128)(2,1)} custom-call(s32[4]{0:T(128)S(1)} %pad_add_fusion.place, f32[1536,64]{1,0:T(8,128)S(1)} %get-tuple-element.48.probs_in, bf16[3,2,192,640]{3,2,1,0:T(8,128)(2,1)S(1)} %get-tuple-element.49.data, bf16[192,1280]{1,0:T(8,128)(2,1)S(1)} %get-tuple-element.50.cot, bf16[192,1280]{1,0:T(8,128)(2,1)S(1)} %get-tuple-element.52.cot_far, ...), custom_call_target="tpu_custom_call" | custom-call | flops 2000000000 | bytes 7602192 | tf_op jit(solution)/shard_map/group_back/pallas_call | solution.py:61
  83.5 5.2 %all-to-all-start.1 = ((bf16[16,72,640]{2,1,0:T(8,128)(2,1)}), bf16[16,72,640]{2,1,0:T(8,128)(2,1)S(1)}, u32[]{:S(2)}, u32[]{:S(2)}) async-start(bf16[16,72,640]{2,1,0:T(8,128)(2,1)} %bitcast.13), calls=%async_computation.1 | async-start | bytes 2949120 | tf_op jit(solution)/shard_map/all_to_all | solution.py:464
  88.7 8.2 %collective-permute-done.12.b = bf16[160,1280]{1,0:T(8,128)(2,1)S(1)} collective-permute-done((bf16[160,1280]{1,0:T(8,128)(2,1)}, bf16[160,1280]{1,0:T(8,128)(2,1)S(1)}, u32[]{:S(2)}, u32[]{:S(2)}) %collective-permute-start.12) | collective-permute-done | bytes 409632 | tf_op jit(solution)/shard_map/ppermute | solution.py:447
  100.5 2.6 %collective-permute-start.15 = (bf16[80,640]{1,0:T(8,128)(2,1)S(1)}, bf16[80,640]{1,0:T(8,128)(2,1)S(1)}, u32[]{:S(2)}, u32[]{:S(2)}) collective-permute-start(bf16[80,640]{1,0:T(8,128)(2,1)S(1)} %get-tuple-element.64), channel_id=1, source_target_pairs={{0,64},{32,96},{64,0},{96,32},{128,192},{160,224},{192,128},{224,1... | collective-permute-start | bytes 307208 | tf_op jit(solution)/shard_map/ppermute | solution.py:437
  104.5 2.1 %collective-permute-done.15.refs_6_ = bf16[80,640]{1,0:T(8,128)(2,1)S(1)} collective-permute-done((bf16[80,640]{1,0:T(8,128)(2,1)S(1)}, bf16[80,640]{1,0:T(8,128)(2,1)S(1)}, u32[]{:S(2)}, u32[]{:S(2)}) %collective-permute-start.15) | collective-permute-done | bytes 102432 | tf_op jit(solution)/shard_map/ppermute | solution.py:437
  107.5 7.9 %collective-permute-start.17 = (bf16[48,640]{1,0:T(8,128)(2,1)S(1)}, bf16[48,640]{1,0:T(8,128)(2,1)S(1)}, u32[]{:S(2)}, u32[]{:S(2)}) collective-permute-start(bf16[48,640]{1,0:T(8,128)(2,1)S(1)} %get-tuple-element.66), channel_id=1, source_target_pairs={{0,0},{1,16},{2,2},{3,18},{4,4},{5,20},{6,6},{7,22},{8,1},{9,17},{... | collective-permute-start | bytes 184328 | tf_op jit(solution)/shard_map/ppermute | solution.py:457
  115.4 6.5 %collective-permute-start.18 = (bf16[48,640]{1,0:T(8,128)(2,1)S(1)}, bf16[48,640]{1,0:T(8,128)(2,1)S(1)}, u32[]{:S(2)}, u32[]{:S(2)}) collective-permute-start(bf16[48,640]{1,0:T(8,128)(2,1)S(1)} %get-tuple-element.67), channel_id=1, source_target_pairs={{0,1},{1,17},{2,3},{3,19},{4,5},{5,21},{6,7},{7,23},{8,8},{9,24},{... | collective-permute-start | bytes 184328 | tf_op jit(solution)/shard_map/ppermute | solution.py:457
  122.0 2.2 %collective-permute-start.20 = (bf16[48,640]{1,0:T(8,128)(2,1)S(1)}, bf16[48,640]{1,0:T(8,128)(2,1)S(1)}, u32[]{:S(2)}, u32[]{:S(2)}) collective-permute-start(bf16[48,640]{1,0:T(8,128)(2,1)S(1)} %get-tuple-element.69), channel_id=1, source_target_pairs={{0,9},{1,25},{2,11},{3,27},{4,13},{5,29},{6,15},{7,31},{8,0},{9,16... | collective-permute-start | bytes 184328 | tf_op jit(solution)/shard_map/ppermute | solution.py:457
  125.7 1.9 %collective-permute-done.18.b = bf16[48,640]{1,0:T(8,128)(2,1)S(1)} collective-permute-done((bf16[48,640]{1,0:T(8,128)(2,1)S(1)}, bf16[48,640]{1,0:T(8,128)(2,1)S(1)}, u32[]{:S(2)}, u32[]{:S(2)}) %collective-permute-start.18) | collective-permute-done | bytes 61472 | tf_op jit(solution)/shard_map/ppermute | solution.py:457
  127.6 2.7 %collective-permute-done.19.c = bf16[48,640]{1,0:T(8,128)(2,1)S(1)} collective-permute-done((bf16[48,640]{1,0:T(8,128)(2,1)S(1)}, bf16[48,640]{1,0:T(8,128)(2,1)S(1)}, u32[]{:S(2)}, u32[]{:S(2)}) %collective-permute-start.19) | collective-permute-done | bytes 61472 | tf_op jit(solution)/shard_map/ppermute | solution.py:457
  130.3 1.5 %collective-permute-done.20.d = bf16[48,640]{1,0:T(8,128)(2,1)S(1)} collective-permute-done((bf16[48,640]{1,0:T(8,128)(2,1)S(1)}, bf16[48,640]{1,0:T(8,128)(2,1)S(1)}, u32[]{:S(2)}, u32[]{:S(2)}) %collective-permute-start.20) | collective-permute-done | bytes 61472 | tf_op jit(solution)/shard_map/ppermute | solution.py:457
  132.7 4.1 %all-to-all-start.2 = ((bf16[8,48,640]{2,1,0:T(8,128)(2,1)}), bf16[8,48,640]{2,1,0:T(8,128)(2,1)S(1)}, u32[]{:S(2)}, u32[]{:S(2)}) async-start(bf16[8,48,640]{2,1,0:T(8,128)(2,1)} %sum_z.1), calls=%async_computation.2 | async-start | bytes 983040 | tf_op jit(solution)/shard_map/all_to_all | solution.py:626
  136.9 2.2 %collective-permute-done.10.far = bf16[2,96,1920]{2,1,0:T(8,128)(2,1)S(1)} collective-permute-done((bf16[2,96,1920]{2,1,0:T(8,128)(2,1)S(1)}, bf16[2,96,1920]{2,1,0:T(8,128)(2,1)S(1)}, u32[]{:S(2)}, u32[]{:S(2)}) %collective-permute-start.10) | collective-permute-done | bytes 737312 | tf_op jit(solution)/shard_map/ppermute | solution.py:432
  139.0 1.7 %merge.1 = (bf16[2,96,3840]{2,1,0:T(8,128)(2,1)}, f32[8,128]{1,0:T(8,128)S(1)}) custom-call(s32[4]{0:T(128)S(1)} %pad_add_fusion.place, bf16[2,96,1920]{2,1,0:T(8,128)(2,1)S(1)} %get-tuple-element.53.mine.after, bf16[2,96,1920]{2,1,0:T(8,128)(2,1)S(1)} %collective-permute-done.10.far), custom_call_target="tpu_custom_call" | custom-call | bytes 2953232 | tf_op jit(solution)/shard_map/merge/pallas_call | solution.py:61
  140.7 4.7 %all-to-all-done.2.pieces = bf16[8,48,640]{2,1,0:T(8,128)(2,1)S(1)} async-done(((bf16[8,48,640]{2,1,0:T(8,128)(2,1)}), bf16[8,48,640]{2,1,0:T(8,128)(2,1)S(1)}, u32[]{:S(2)}, u32[]{:S(2)}) %all-to-all-start.2) | async-done | bytes 491552 | tf_op jit(solution)/shard_map/all_to_all | solution.py:626
  (52 shorter events, 18.4 us)
Async XLA Ops:
  0.8 1.4 copy-start
  2.1 5.8 %copy-start.1 = (bf16[1,2,96,3840]{3,2,1,0:T(8,128)(2,1)S(1)}, bf16[1,2,96,3840]{3,2,1,0:T(8,128)(2,1)}, u32[]{:S(2)}) copy-start(bf16[1,2,96,3840]{3,2,1,0:T(8,128)(2,1)} %param.8) | copy-start | bytes 4423684
  2.1 5.8 %copy-start.3 = (bf16[1,2,96,1280]{3,2,1,0:T(8,128)(2,1)S(1)}, bf16[1,2,96,1280]{3,2,1,0:T(8,128)(2,1)}, u32[]{:S(2)}) copy-start(bf16[1,2,96,1280]{3,2,1,0:T(8,128)(2,1)} %param.11) | copy-start | bytes 1474564
  2.8 5.2 %collective-permute-start.8 = (bf16[2,96,1920]{2,1,0:T(8,128)(2,1)S(1)}, bf16[2,96,1920]{2,1,0:T(8,128)(2,1)S(1)}, u32[]{:S(2)}, u32[]{:S(2)}) collective-permute-start(bf16[2,96,1920]{2,1,0:T(8,128)(2,1)S(1)} %far.1), channel_id=1, source_target_pairs={{0,1},{1,0},{2,3},{3,2},{4,5},{5,4},{6,7},{7,6},{8,9},{9,8},{10,11... | collective-permute-start | bytes 2211848 | tf_op jit(solution)/shard_map/ppermute | solution.py:432
  10.8 10.0 %copy-start.6 = (s32[1,2,96]{2,1,0:T(2,128)S(1)}, s32[1,2,96]{2,1,0:T(2,128)}, u32[]{:S(2)}) copy-start(s32[1,2,96]{2,1,0:T(2,128)} %param.9) | copy-start | bytes 2308
  10.8 10.0 %copy-start.7 = (f32[8]{0:T(128)S(1)}, f32[8]{0:T(128)}, u32[]{:S(2)}) copy-start(f32[8]{0:T(128)} %slopes.1) | copy-start | bytes 100
  10.8 53.7 %all-to-all-start = ((bf16[16,96,640]{2,1,0:T(8,128)(2,1)}), bf16[16,96,640]{2,1,0:T(8,128)(2,1)S(1)}, u32[]{:S(2)}, u32[]{:S(2)}) async-start(bf16[16,96,640]{2,1,0:T(8,128)(2,1)} %bitcast.10), calls=%async_computation | async-start | bytes 3932160 | tf_op jit(solution)/shard_map/all_to_all | solution.py:464
  20.0 10.3 %collective-permute-start.1 = (bf16[192,1280]{1,0:T(8,128)(2,1)S(1)}, bf16[192,1280]{1,0:T(8,128)(2,1)S(1)}, u32[]{:S(2)}, u32[]{:S(2)}) collective-permute-start(bf16[192,1280]{1,0:T(8,128)(2,1)S(1)} %bitcast.21), channel_id=1, source_target_pairs={{0,1},{1,0},{2,3},{3,2},{4,5},{5,4},{6,7},{7,6},{8,9},{9,8},{10,11... | collective-permute-start | bytes 1474568 | tf_op jit(solution)/shard_map/ppermute | solution.py:432
  20.8 1.9 %copy-start.4 = (bf16[1280,1280]{1,0:T(8,128)(2,1)S(1)}, bf16[1280,1280]{1,0:T(8,128)(2,1)}, u32[]{:S(2)}) copy-start(bf16[1280,1280]{1,0:T(8,128)(2,1)} %weight.2) | copy-start | bytes 9830404
  28.8 1.5 %collective-permute-start = (bf16[192,640]{1,0:T(8,128)(2,1)S(1)}, bf16[192,640]{1,0:T(8,128)(2,1)S(1)}, u32[]{:S(2)}, u32[]{:S(2)}) collective-permute-start(bf16[192,640]{1,0:T(8,128)(2,1)S(1)} %get-tuple-element.40), channel_id=1, source_target_pairs={{0,1},{1,0},{2,3},{3,2},{4,5},{5,4},{6,7},{7,6},{8,9},{9,8},{10,11... | collective-permute-start | bytes 737288 | tf_op jit(solution)/shard_map/ppermute | solution.py:432
  31.4 12.2 %collective-permute-start.2 = (bf16[160,1280]{1,0:T(8,128)(2,1)S(1)}, bf16[160,1280]{1,0:T(8,128)(2,1)S(1)}, u32[]{:S(2)}, u32[]{:S(2)}) collective-permute-start(bf16[160,1280]{1,0:T(8,128)(2,1)S(1)} %get-tuple-element.42), channel_id=1, source_target_pairs={{0,32},{32,64},{64,96},{96,0},{128,160},{160,192},{192,224},{224,1... | collective-permute-start | bytes 1228808 | tf_op jit(solution)/shard_map/ppermute | solution.py:437
  32.7 20.7 %collective-permute-start.3 = (bf16[160,1280]{1,0:T(8,128)(2,1)S(1)}, bf16[160,1280]{1,0:T(8,128)(2,1)S(1)}, u32[]{:S(2)}, u32[]{:S(2)}) collective-permute-start(bf16[160,1280]{1,0:T(8,128)(2,1)S(1)} %get-tuple-element.43), channel_id=1, source_target_pairs={{0,64},{32,96},{64,0},{96,32},{128,192},{160,224},{192,128},{224,1... | collective-permute-start | bytes 1228808 | tf_op jit(solution)/shard_map/ppermute | solution.py:437
  35.2 18.2 %collective-permute-start.4 = (bf16[160,1280]{1,0:T(8,128)(2,1)S(1)}, bf16[160,1280]{1,0:T(8,128)(2,1)S(1)}, u32[]{:S(2)}, u32[]{:S(2)}) collective-permute-start(bf16[160,1280]{1,0:T(8,128)(2,1)S(1)} %get-tuple-element.44), channel_id=1, source_target_pairs={{0,96},{32,0},{64,32},{96,64},{128,224},{160,128},{192,160},{224,1... | collective-permute-start | bytes 1228808 | tf_op jit(solution)/shard_map/ppermute | solution.py:437
  53.6 16.5 %collective-permute-start.5 = (bf16[80,640]{1,0:T(8,128)(2,1)S(1)}, bf16[80,640]{1,0:T(8,128)(2,1)S(1)}, u32[]{:S(2)}, u32[]{:S(2)}) collective-permute-start(bf16[80,640]{1,0:T(8,128)(2,1)S(1)} %get-tuple-element.45), channel_id=1, source_target_pairs={{0,2},{1,3},{2,4},{3,5},{4,6},{5,7},{6,0},{7,1},{8,10},{9,11},{10,... | collective-permute-start | bytes 307208 | tf_op jit(solution)/shard_map/ppermute | solution.py:447
  55.2 14.9 %collective-permute-start.6 = (bf16[80,640]{1,0:T(8,128)(2,1)S(1)}, bf16[80,640]{1,0:T(8,128)(2,1)S(1)}, u32[]{:S(2)}, u32[]{:S(2)}) collective-permute-start(bf16[80,640]{1,0:T(8,128)(2,1)S(1)} %get-tuple-element.46), channel_id=1, source_target_pairs={{0,4},{1,5},{2,6},{3,7},{4,0},{5,1},{6,2},{7,3},{8,12},{9,13},{10,... | collective-permute-start | bytes 307208 | tf_op jit(solution)/shard_map/ppermute | solution.py:447
  57.6 12.5 %collective-permute-start.7 = (bf16[80,640]{1,0:T(8,128)(2,1)S(1)}, bf16[80,640]{1,0:T(8,128)(2,1)S(1)}, u32[]{:S(2)}, u32[]{:S(2)}) collective-permute-start(bf16[80,640]{1,0:T(8,128)(2,1)S(1)} %get-tuple-element.47), channel_id=1, source_target_pairs={{0,6},{1,7},{2,0},{3,1},{4,2},{5,3},{6,4},{7,5},{8,14},{9,15},{10,... | collective-permute-start | bytes 307208 | tf_op jit(solution)/shard_map/ppermute | solution.py:447
  64.6 8.6 %collective-permute-start.9 = (bf16[16,24,640]{2,1,0:T(8,128)(2,1)S(1)}, bf16[16,24,640]{2,1,0:T(8,128)(2,1)S(1)}, u32[]{:S(2)}, u32[]{:S(2)}) collective-permute-start(bf16[16,24,640]{2,1,0:T(8,128)(2,1)S(1)} %slice.4), channel_id=1, source_target_pairs={{0,1},{1,0},{2,3},{3,2},{4,5},{5,4},{6,7},{7,6},{8,9},{9,8},{10,11... | collective-permute-start | bytes 1474568 | tf_op jit(solution)/shard_map/ppermute | solution.py:432
  70.1 8.2 %copy-start.2 = (bf16[1280,1280]{1,0:T(8,128)(2,1)S(1)}, bf16[1280,1280]{1,0:T(8,128)(2,1)}, u32[]{:S(2)}) copy-start(bf16[1280,1280]{1,0:T(8,128)(2,1)} %weight.3) | copy-start | bytes 9830404
  75.4 8.1 %copy-start.8 = (f32[160,1280]{1,0:T(8,128)}, f32[160,1280]{1,0:T(8,128)S(1)}, u32[]{:S(2)}) copy-start(f32[160,1280]{1,0:T(8,128)S(1)} %get-tuple-element.58.own) | copy-start | bytes 2457604
  75.4 13.2 %collective-permute-start.11 = (bf16[160,1280]{1,0:T(8,128)(2,1)}, bf16[160,1280]{1,0:T(8,128)(2,1)S(1)}, u32[]{:S(2)}, u32[]{:S(2)}) collective-permute-start(bf16[160,1280]{1,0:T(8,128)(2,1)} %get-tuple-element.59), channel_id=1, source_target_pairs={{0,2},{1,3},{2,4},{3,5},{4,6},{5,7},{6,0},{7,1},{8,10},{9,11},{10,... | collective-permute-start | bytes 1228808 | tf_op jit(solution)/shard_map/ppermute | solution.py:447
  75.4 21.5 %collective-permute-start.12 = (bf16[160,1280]{1,0:T(8,128)(2,1)}, bf16[160,1280]{1,0:T(8,128)(2,1)S(1)}, u32[]{:S(2)}, u32[]{:S(2)}) collective-permute-start(bf16[160,1280]{1,0:T(8,128)(2,1)} %get-tuple-element.60), channel_id=1, source_target_pairs={{0,4},{1,5},{2,6},{3,7},{4,0},{5,1},{6,2},{7,3},{8,12},{9,13},{10,... | collective-permute-start | bytes 1228808 | tf_op jit(solution)/shard_map/ppermute | solution.py:447
  78.3 18.8 %collective-permute-start.13 = (bf16[160,1280]{1,0:T(8,128)(2,1)S(1)}, bf16[160,1280]{1,0:T(8,128)(2,1)}, u32[]{:S(2)}, u32[]{:S(2)}) collective-permute-start(bf16[160,1280]{1,0:T(8,128)(2,1)S(1)} %get-tuple-element.61), channel_id=1, source_target_pairs={{0,6},{1,7},{2,0},{3,1},{4,2},{5,3},{6,4},{7,5},{8,14},{9,15},{10,... | collective-permute-start | bytes 1228808 | tf_op jit(solution)/shard_map/ppermute | solution.py:447
  83.5 40.7 %all-to-all-start.1 = ((bf16[16,72,640]{2,1,0:T(8,128)(2,1)}), bf16[16,72,640]{2,1,0:T(8,128)(2,1)S(1)}, u32[]{:S(2)}, u32[]{:S(2)}) async-start(bf16[16,72,640]{2,1,0:T(8,128)(2,1)} %bitcast.13), calls=%async_computation.1 | async-start | bytes 2949120 | tf_op jit(solution)/shard_map/all_to_all | solution.py:464
  99.4 5.1 %collective-permute-start.14 = (bf16[80,640]{1,0:T(8,128)(2,1)S(1)}, bf16[80,640]{1,0:T(8,128)(2,1)S(1)}, u32[]{:S(2)}, u32[]{:S(2)}) collective-permute-start(bf16[80,640]{1,0:T(8,128)(2,1)S(1)} %get-tuple-element.63), channel_id=1, source_target_pairs={{0,32},{32,64},{64,96},{96,0},{128,160},{160,192},{192,224},{224,1... | collective-permute-start | bytes 307208 | tf_op jit(solution)/shard_map/ppermute | solution.py:437
  100.5 6.0 %collective-permute-start.15 = (bf16[80,640]{1,0:T(8,128)(2,1)S(1)}, bf16[80,640]{1,0:T(8,128)(2,1)S(1)}, u32[]{:S(2)}, u32[]{:S(2)}) collective-permute-start(bf16[80,640]{1,0:T(8,128)(2,1)S(1)} %get-tuple-element.64), channel_id=1, source_target_pairs={{0,64},{32,96},{64,0},{96,32},{128,192},{160,224},{192,128},{224,1... | collective-permute-start | bytes 307208 | tf_op jit(solution)/shard_map/ppermute | solution.py:437
  103.1 4.2 %collective-permute-start.16 = (bf16[80,640]{1,0:T(8,128)(2,1)S(1)}, bf16[80,640]{1,0:T(8,128)(2,1)S(1)}, u32[]{:S(2)}, u32[]{:S(2)}) collective-permute-start(bf16[80,640]{1,0:T(8,128)(2,1)S(1)} %get-tuple-element.65), channel_id=1, source_target_pairs={{0,96},{32,0},{64,32},{96,64},{128,224},{160,128},{192,160},{224,1... | collective-permute-start | bytes 307208 | tf_op jit(solution)/shard_map/ppermute | solution.py:437
  107.5 18.2 %collective-permute-start.17 = (bf16[48,640]{1,0:T(8,128)(2,1)S(1)}, bf16[48,640]{1,0:T(8,128)(2,1)S(1)}, u32[]{:S(2)}, u32[]{:S(2)}) collective-permute-start(bf16[48,640]{1,0:T(8,128)(2,1)S(1)} %get-tuple-element.66), channel_id=1, source_target_pairs={{0,0},{1,16},{2,2},{3,18},{4,4},{5,20},{6,6},{7,22},{8,1},{9,17},{... | collective-permute-start | bytes 184328 | tf_op jit(solution)/shard_map/ppermute | solution.py:457
  115.4 12.2 %collective-permute-start.18 = (bf16[48,640]{1,0:T(8,128)(2,1)S(1)}, bf16[48,640]{1,0:T(8,128)(2,1)S(1)}, u32[]{:S(2)}, u32[]{:S(2)}) collective-permute-start(bf16[48,640]{1,0:T(8,128)(2,1)S(1)} %get-tuple-element.67), channel_id=1, source_target_pairs={{0,1},{1,17},{2,3},{3,19},{4,5},{5,21},{6,7},{7,23},{8,8},{9,24},{... | collective-permute-start | bytes 184328 | tf_op jit(solution)/shard_map/ppermute | solution.py:457
  121.9 8.4 %collective-permute-start.19 = (bf16[48,640]{1,0:T(8,128)(2,1)S(1)}, bf16[48,640]{1,0:T(8,128)(2,1)S(1)}, u32[]{:S(2)}, u32[]{:S(2)}) collective-permute-start(bf16[48,640]{1,0:T(8,128)(2,1)S(1)} %get-tuple-element.68), channel_id=1, source_target_pairs={{0,8},{1,24},{2,10},{3,26},{4,12},{5,28},{6,14},{7,30},{8,9},{9,25... | collective-permute-start | bytes 184328 | tf_op jit(solution)/shard_map/ppermute | solution.py:457
  122.0 9.9 %collective-permute-start.20 = (bf16[48,640]{1,0:T(8,128)(2,1)S(1)}, bf16[48,640]{1,0:T(8,128)(2,1)S(1)}, u32[]{:S(2)}, u32[]{:S(2)}) collective-permute-start(bf16[48,640]{1,0:T(8,128)(2,1)S(1)} %get-tuple-element.69), channel_id=1, source_target_pairs={{0,9},{1,25},{2,11},{3,27},{4,13},{5,29},{6,15},{7,31},{8,0},{9,16... | collective-permute-start | bytes 184328 | tf_op jit(solution)/shard_map/ppermute | solution.py:457
  132.7 12.7 %all-to-all-start.2 = ((bf16[8,48,640]{2,1,0:T(8,128)(2,1)}), bf16[8,48,640]{2,1,0:T(8,128)(2,1)S(1)}, u32[]{:S(2)}, u32[]{:S(2)}) async-start(bf16[8,48,640]{2,1,0:T(8,128)(2,1)} %sum_z.1), calls=%async_computation.2 | async-start | bytes 983040 | tf_op jit(solution)/shard_map/all_to_all | solution.py:626
  136.8 2.2 %collective-permute-start.10 = (bf16[2,96,1920]{2,1,0:T(8,128)(2,1)S(1)}, bf16[2,96,1920]{2,1,0:T(8,128)(2,1)S(1)}, u32[]{:S(2)}, u32[]{:S(2)}) collective-permute-start(bf16[2,96,1920]{2,1,0:T(8,128)(2,1)S(1)} %get-tuple-element.54), channel_id=1, source_target_pairs={{0,1},{1,0},{2,3},{3,2},{4,5},{5,4},{6,7},{7,6},{8,9},{9,8},{10,11... | collective-permute-start | bytes 2211848 | tf_op jit(solution)/shard_map/ppermute | solution.py:432
  (2 other events, 2.5 us)
